TPU v7x, 32 devices: a whole 2x2x4 slice. The times are simulated.
32 devices in a mesh: ctx: 4 (over y, x), exp: 8 (over z, core).
Axes of the slice: x: 2, y: 2, z: 4, core: 2. Of those that a mesh axis runs over, the one named last changes fastest.
Arguments:
- tokens: bfloat16 [8, 2048, 1024], P('exp', 'ctx'), may hold values from -6 to 6
- attn_gain: float32 [1024], replicated, may hold values from 0.25 to 1.75
- query_weight: bfloat16 [1024, 1024], replicated, may hold values from -0.75 to 0.75
- key_weight: bfloat16 [1024, 512], replicated, may hold values from -0.75 to 0.75
- value_weight: bfloat16 [1024, 512], replicated, may hold values from -0.1875 to 0.1875
- output_weight: bfloat16 [1024, 1024], replicated, may hold values from -1.5 to 1.5
- moe_gain: float32 [1024], replicated, may hold values from 0.25 to 1.75
- w_router: bfloat16 [1024, 32], replicated, may hold values from -0.09375 to 0.09375
- routes: int32 [8, 2048, 8], P('exp', 'ctx'), may hold values from 0 to 31, all different within a row; in each aligned block of 512 rows (0 to 511, 512 to 1023, ..., all dimensions but the last counted through in order) at most 192 rows name the same one
- w_gate: bfloat16 [32, 1024, 512], P('exp'), may hold values from -0.1875 to 0.1875
- w_up: bfloat16 [32, 1024, 512], P('exp'), may hold values from -0.1875 to 0.1875
- w_down: bfloat16 [32, 512, 1024], P('exp'), may hold values from -1.5 to 1.5
- cotangent: bfloat16 [8, 2048, 1024], P('exp', 'ctx'), may hold values from -6 to 6
Outputs:
- layer_out: bfloat16 [8, 2048, 1024], P('exp', 'ctx')
- grad_tokens: float32 [8, 2048, 1024], P('exp', 'ctx')
- grad_attn_gain: float32 [1024], replicated
- grad_query: float32 [1024, 1024], replicated
- grad_key: float32 [1024, 512], replicated
- grad_value: float32 [1024, 512], replicated
- grad_out: float32 [1024, 1024], replicated
- grad_moe_gain: float32 [1024], replicated
- grad_router: float32 [1024, 32], replicated
- grad_gate: float32 [32, 1024, 512], P('exp')
- grad_up: float32 [32, 1024, 512], P('exp')
- grad_down: float32 [32, 512, 1024], P('exp')
Inputs may be any that keep to these rules, and one draw needn't show every extreme that they name: `routes`: each token names 8 different experts; among the 512 rows of one device (consecutive positions of one sequence) no expert is named by more than 192 rows, a bound that some block reaches.
All inputs are finite; a program needn't handle non-finite values.
Results may differ from a plain program's by a relative error of at most 0.03.
Values may be sent and summed in bfloat16 or wider, within the bound.
No kernel may reach another device: no remote copies, remote signals or barrier semaphores. Data moves between devices by JAX's collectives and lax.ppermute only.
A program may use at most 256 MiB of HBM per device.

v0:
```python
import jax
import jax.numpy as jnp
from jax import lax
from jax.sharding import PartitionSpec as P

HEAD_DIM = 64
CAP = 192


SCALE = 0.015625
THETA = 10000.0
EPSILON = 1e-06
NEG = -1e30


def normalize(values):
    factor = lax.rsqrt(jnp.mean(values * values, axis=-1, keepdims=True) + EPSILON)
    return (values * factor, factor)


def norm_back(grad_scaled, scaled, factor):
    return factor * (grad_scaled - scaled * jnp.mean(grad_scaled * scaled, axis=-1, keepdims=True))


def rotate(values, positions, direction):
    half_size = values.shape[-1] // 2
    inverse = THETA ** (-jnp.arange(half_size, dtype=jnp.float32) * 2.0 / values.shape[-1])
    angles = positions.astype(jnp.float32)[:, None] * inverse[None, :]
    cosine_table = jnp.concatenate([jnp.cos(angles), jnp.cos(angles)], -1)[:, None, :]
    sine_table = jnp.concatenate([jnp.sin(angles), jnp.sin(angles)], -1)[:, None, :]
    turned = jnp.concatenate([-values[..., half_size:], values[..., :half_size]], -1)
    return values * cosine_table + direction * turned * sine_table


def key_scores(queries, key_block, start, positions):
    scores = (
        jnp.einsum("qkgd,nkd->qkgn", queries, key_block, preferred_element_type=jnp.float32) * SCALE
    )
    places = start + jnp.arange(key_block.shape[0], dtype=jnp.int32)
    allowed = (places[None, :] <= positions[:, None])[:, None, None, :]
    return (scores, allowed)


def by_blocks(visit, carried, piece, block_size):
    key_rows, value_rows = piece
    key_count = key_rows.shape[0]
    block_count = key_count // block_size

    def one_block(inner, block_item):
        key_part, value_part, block_index = block_item
        return (visit(inner, key_part, value_part, block_index * block_size), None)

    carried, _ = lax.scan(
        one_block,
        carried,
        (
            key_rows.reshape(block_count, block_size, -1),
            value_rows.reshape(block_count, block_size, -1),
            jnp.arange(block_count, dtype=jnp.int32),
        ),
    )
    return carried


def per_device(
    tokens,
    attn_gain,
    query_weight,
    key_weight,
    value_weight,
    output_weight,
    moe_gain,
    w_router,
    routes,
    w_gate,
    w_up,
    w_down,
    cotangent,
):
    tok_rows = tokens.shape[1]
    model_width = tokens.shape[2]
    kv_heads = key_weight.shape[1] // HEAD_DIM
    groups = query_weight.shape[1] // key_weight.shape[1]
    experts = w_router.shape[1]
    top_k = routes.shape[2]
    owned_experts = w_gate.shape[0]
    exp_peers = lax.axis_size("exp")
    seq_length = lax.axis_size("ctx") * tok_rows
    positions = lax.axis_index("ctx") * tok_rows + jnp.arange(tok_rows, dtype=jnp.int32)
    layer_inputs = tokens[0].astype(jnp.float32)
    scaled_one, factor_one = normalize(layer_inputs)
    first_normalized = (scaled_one * attn_gain).astype(jnp.bfloat16)
    query_linear = jnp.dot(
        first_normalized, query_weight, preferred_element_type=jnp.float32
    ).reshape(tok_rows, -1, HEAD_DIM)
    key_linear = jnp.dot(first_normalized, key_weight, preferred_element_type=jnp.float32).reshape(
        tok_rows, kv_heads, HEAD_DIM
    )
    queries = (
        rotate(query_linear, positions, 1.0)
        .astype(jnp.bfloat16)
        .reshape(tok_rows, kv_heads, groups, HEAD_DIM)
    )
    key_rows = rotate(key_linear, positions, 1.0).astype(jnp.bfloat16).reshape(tok_rows, -1)
    value_rows = jnp.dot(first_normalized, value_weight, preferred_element_type=jnp.float32).astype(
        jnp.bfloat16
    )

    def forward_visit(carried, key_block, value_block, start):
        summed, running, total_mass = carried
        key_block = key_block.reshape(key_block.shape[0], kv_heads, HEAD_DIM)
        value_block = value_block.reshape(value_block.shape[0], kv_heads, HEAD_DIM)
        scores, allowed = key_scores(queries, key_block, start, positions)
        newest = jnp.maximum(running, jnp.max(jnp.where(allowed, scores, NEG), axis=-1))
        weights = jnp.where(allowed, jnp.exp(scores - newest[..., None]), 0.0)
        rescale = jnp.exp(running - newest)
        total_mass = total_mass * rescale + jnp.sum(weights, axis=-1)
        summed = summed * rescale[..., None] + jnp.einsum(
            "qkgn,nkd->qkgd",
            weights.astype(jnp.bfloat16),
            value_block,
            preferred_element_type=jnp.float32,
        )
        return (summed, newest, total_mass)

    stat_shape = (tok_rows, kv_heads, groups)
    initial = (
        jnp.zeros(stat_shape + (HEAD_DIM,), jnp.float32),
        jnp.full(stat_shape, NEG, jnp.float32),
        jnp.zeros(stat_shape, jnp.float32),
    )
    summed, running, total_mass = by_blocks(
        forward_visit,
        initial,
        (
            lax.all_gather(key_rows, "ctx", axis=0, tiled=True),
            lax.all_gather(value_rows, "ctx", axis=0, tiled=True),
        ),
        tok_rows,
    )
    attention_result = summed / total_mass[..., None]
    log_total = running + jnp.log(total_mass)
    attended_low = attention_result.reshape(tok_rows, -1).astype(jnp.bfloat16)
    residual_stream = layer_inputs + jnp.dot(
        attended_low, output_weight, preferred_element_type=jnp.float32
    )
    scaled_two, factor_two = normalize(residual_stream)
    normed_two = (scaled_two * moe_gain).astype(jnp.bfloat16)
    logits = jnp.dot(normed_two, w_router, preferred_element_type=jnp.float32)
    expert_ids = routes[0]
    one_hot = (expert_ids[..., None] == jnp.arange(experts, dtype=jnp.int32)).astype(jnp.int32)
    flat_hot = one_hot.reshape(tok_rows * top_k, experts)
    slot_index = jnp.sum(
        (jnp.cumsum(flat_hot, axis=0, dtype=jnp.int32) - 1) * flat_hot, axis=-1, dtype=jnp.int32
    )
    targets = expert_ids.reshape(-1) * CAP + slot_index
    gate_weights = jax.nn.softmax(jnp.take_along_axis(logits, expert_ids, axis=1), axis=-1)

    def pack_rows(row_values):
        filled = jnp.zeros((experts * CAP, model_width), jnp.bfloat16).at[targets].set(row_values)
        return filled.reshape(experts, CAP, model_width)

    def expert_front(arrived):
        gate_lin = jnp.einsum("sicd,idf->sicf", arrived, w_gate, preferred_element_type=jnp.float32)
        up_lin = jnp.einsum("sicd,idf->sicf", arrived, w_up, preferred_element_type=jnp.float32)
        return (gate_lin, up_lin)

    repeated = jnp.repeat(normed_two, top_k, axis=0)
    received = lax.all_to_all(pack_rows(repeated), "exp", split_axis=0, concat_axis=0, tiled=True)
    received = received.reshape(exp_peers, owned_experts, CAP, model_width)
    gate_lin, up_lin = expert_front(received)
    hidden = (gate_lin * jax.nn.sigmoid(gate_lin) * up_lin).astype(jnp.bfloat16)
    produced = jnp.einsum(
        "sicf,ifd->sicd", hidden, w_down, preferred_element_type=jnp.float32
    ).astype(jnp.bfloat16)
    returned = lax.all_to_all(
        produced.reshape(experts, CAP, model_width), "exp", split_axis=0, concat_axis=0, tiled=True
    )
    picked = returned.reshape(experts * CAP, model_width)[targets].reshape(
        tok_rows, top_k, model_width
    )
    output = residual_stream + jnp.sum(gate_weights[..., None] * picked.astype(jnp.float32), axis=1)
    upstream = cotangent[0].astype(jnp.float32)
    gate_grad = jnp.sum(upstream[:, None, :] * picked.astype(jnp.float32), axis=-1)
    chosen_grad = gate_weights * (
        gate_grad - jnp.sum(gate_weights * gate_grad, axis=-1, keepdims=True)
    )
    logit_grad = jnp.sum(chosen_grad[..., None] * one_hot.astype(jnp.float32), axis=1).astype(
        jnp.bfloat16
    )
    router_grad = jnp.einsum(
        "td,te->de", normed_two, logit_grad, preferred_element_type=jnp.float32
    )
    normed_two_grad = jnp.einsum(
        "te,de->td", logit_grad, w_router, preferred_element_type=jnp.float32
    )
    out_grad = (
        (gate_weights[..., None] * upstream[:, None, :])
        .astype(jnp.bfloat16)
        .reshape(-1, model_width)
    )
    arrived_grad = lax.all_to_all(
        pack_rows(out_grad), "exp", split_axis=0, concat_axis=0, tiled=True
    )
    arrived_grad = arrived_grad.reshape(exp_peers, owned_experts, CAP, model_width)
    arrived = lax.all_to_all(pack_rows(repeated), "exp", split_axis=0, concat_axis=0, tiled=True)
    arrived = arrived.reshape(exp_peers, owned_experts, CAP, model_width)
    gate_again, up_again = expert_front(arrived)
    sigmoid_gate = jax.nn.sigmoid(gate_again)
    activated = gate_again * sigmoid_gate
    hidden_again = (activated * up_again).astype(jnp.bfloat16)
    down_grad = jnp.einsum(
        "sicf,sicd->ifd", hidden_again, arrived_grad, preferred_element_type=jnp.float32
    )
    hidden_grad = jnp.einsum(
        "sicd,ifd->sicf", arrived_grad, w_down, preferred_element_type=jnp.float32
    )
    gate_back = (
        hidden_grad * up_again * sigmoid_gate * (1.0 + gate_again * (1.0 - sigmoid_gate))
    ).astype(jnp.bfloat16)
    up_back = (hidden_grad * activated).astype(jnp.bfloat16)
    wgate_grad = jnp.einsum(
        "sicd,sicf->idf", arrived, gate_back, preferred_element_type=jnp.float32
    )
    wup_grad = jnp.einsum("sicd,sicf->idf", arrived, up_back, preferred_element_type=jnp.float32)
    row_grad = (
        jnp.einsum("sicf,idf->sicd", gate_back, w_gate, preferred_element_type=jnp.float32)
        + jnp.einsum("sicf,idf->sicd", up_back, w_up, preferred_element_type=jnp.float32)
    ).astype(jnp.bfloat16)
    row_back = lax.all_to_all(
        row_grad.reshape(experts, CAP, model_width), "exp", split_axis=0, concat_axis=0, tiled=True
    )
    row_back = row_back.reshape(experts * CAP, model_width)[targets].reshape(
        tok_rows, top_k, model_width
    )
    normed_two_grad = normed_two_grad + jnp.sum(row_back.astype(jnp.float32), axis=1)
    wgate_grad, wup_grad, down_grad = (
        lax.psum(wgate_grad.astype(jnp.bfloat16), "ctx").astype(jnp.float32),
        lax.psum(wup_grad.astype(jnp.bfloat16), "ctx").astype(jnp.float32),
        lax.psum(down_grad.astype(jnp.bfloat16), "ctx").astype(jnp.float32),
    )
    gain_two_grad = jnp.sum(normed_two_grad * scaled_two, axis=0)
    residual_grad = upstream + norm_back(normed_two_grad * moe_gain, scaled_two, factor_two)
    residual_low = residual_grad.astype(jnp.bfloat16)
    wout_grad = jnp.einsum(
        "tq,td->qd", attended_low, residual_low, preferred_element_type=jnp.float32
    )
    attended_grad = jnp.einsum(
        "td,qd->tq", residual_low, output_weight, preferred_element_type=jnp.float32
    )
    attended_grad = attended_grad.astype(jnp.bfloat16).reshape(tok_rows, kv_heads, groups, HEAD_DIM)
    offset = jnp.sum(attended_grad.astype(jnp.float32) * attention_result, axis=-1)

    def backward_visit(carried, key_block, value_block, start):
        query_grad, key_sum, value_sum = carried
        key_count = key_block.shape[0]
        key_block = key_block.reshape(key_count, kv_heads, HEAD_DIM)
        value_block = value_block.reshape(key_count, kv_heads, HEAD_DIM)
        scores, allowed = key_scores(queries, key_block, start, positions)
        soft = jnp.where(allowed, jnp.exp(scores - log_total[..., None]), 0.0)
        value_part = jnp.einsum(
            "qkgn,qkgd->nkd",
            soft.astype(jnp.bfloat16),
            attended_grad,
            preferred_element_type=jnp.float32,
        )
        prob_grad = jnp.einsum(
            "qkgd,nkd->qkgn", attended_grad, value_block, preferred_element_type=jnp.float32
        )
        score_grad = (soft * (prob_grad - offset[..., None])).astype(jnp.bfloat16)
        query_grad = query_grad + SCALE * jnp.einsum(
            "qkgn,nkd->qkgd", score_grad, key_block, preferred_element_type=jnp.float32
        )
        key_part = SCALE * jnp.einsum(
            "qkgn,qkgd->nkd", score_grad, queries, preferred_element_type=jnp.float32
        )
        key_sum = lax.dynamic_update_slice_in_dim(
            key_sum,
            lax.dynamic_slice_in_dim(key_sum, start, key_count, 0)
            + key_part.reshape(key_count, -1),
            start,
            0,
        )
        value_sum = lax.dynamic_update_slice_in_dim(
            value_sum,
            lax.dynamic_slice_in_dim(value_sum, start, key_count, 0)
            + value_part.reshape(key_count, -1),
            start,
            0,
        )
        return (query_grad, key_sum, value_sum)

    kv_width = kv_heads * HEAD_DIM
    initial_back = (
        jnp.zeros(stat_shape + (HEAD_DIM,), jnp.float32),
        jnp.zeros((seq_length, kv_width), jnp.float32),
        jnp.zeros((seq_length, kv_width), jnp.float32),
    )
    query_grad, key_sum, value_sum = by_blocks(
        backward_visit,
        initial_back,
        (
            lax.all_gather(key_rows, "ctx", axis=0, tiled=True),
            lax.all_gather(value_rows, "ctx", axis=0, tiled=True),
        ),
        tok_rows,
    )
    key_grad, value_grad = (
        lax.psum_scatter(
            key_sum.astype(jnp.bfloat16), "ctx", scatter_dimension=0, tiled=True
        ).astype(jnp.float32),
        lax.psum_scatter(
            value_sum.astype(jnp.bfloat16), "ctx", scatter_dimension=0, tiled=True
        ).astype(jnp.float32),
    )
    query_back = (
        rotate(query_grad.reshape(tok_rows, -1, HEAD_DIM), positions, -1.0)
        .astype(jnp.bfloat16)
        .reshape(tok_rows, -1)
    )
    key_back = (
        rotate(key_grad.reshape(tok_rows, kv_heads, HEAD_DIM), positions, -1.0)
        .astype(jnp.bfloat16)
        .reshape(tok_rows, -1)
    )
    value_back = value_grad.astype(jnp.bfloat16)
    wq_grad = jnp.einsum(
        "td,te->de", first_normalized, query_back, preferred_element_type=jnp.float32
    )
    wk_grad = jnp.einsum(
        "td,te->de", first_normalized, key_back, preferred_element_type=jnp.float32
    )
    wv_grad = jnp.einsum(
        "td,te->de", first_normalized, value_back, preferred_element_type=jnp.float32
    )
    normed_one_grad = (
        jnp.einsum("te,de->td", query_back, query_weight, preferred_element_type=jnp.float32)
        + jnp.einsum("te,de->td", key_back, key_weight, preferred_element_type=jnp.float32)
        + jnp.einsum("te,de->td", value_back, value_weight, preferred_element_type=jnp.float32)
    )
    gain_one_grad = jnp.sum(normed_one_grad * scaled_one, axis=0)
    input_grad = residual_grad + norm_back(normed_one_grad * attn_gain, scaled_one, factor_one)
    wq_grad, wk_grad, wv_grad, wout_grad, router_grad, gain_one_grad, gain_two_grad = lax.psum(
        (wq_grad, wk_grad, wv_grad, wout_grad, router_grad, gain_one_grad, gain_two_grad),
        ("ctx", "exp"),
    )
    return (
        output.astype(jnp.bfloat16)[None],
        input_grad[None],
        gain_one_grad,
        wq_grad,
        wk_grad,
        wv_grad,
        wout_grad,
        gain_two_grad,
        router_grad,
        wgate_grad,
        wup_grad,
        down_grad,
    )


def solution(mesh):
    return jax.shard_map(
        per_device,
        mesh=mesh,
        in_specs=(
            P("exp", "ctx", None),
            P(),
            P(),
            P(),
            P(),
            P(),
            P(),
            P(),
            P("exp", "ctx", None),
            P("exp", None, None),
            P("exp", None, None),
            P("exp", None, None),
            P("exp", "ctx", None),
        ),
        out_specs=(
            P("exp", "ctx", None),
            P("exp", "ctx", None),
            P(),
            P(),
            P(),
            P(),
            P(),
            P(),
            P(),
            P("exp", None, None),
            P("exp", None, None),
            P("exp", None, None),
        ),
        check_vma=False,
    )
```

profile of v0, /device:TPU:0, one launch (start us, length us, event | category | flops | bytes accessed | tf_op | source)
XLA Modules:
  0.0 2228.8 jit_solution(17070611208499194939)
XLA Ops:
  26.9 18.1 reduce-window.6
  63.3 29.5 %all-gather.5.cloned.1.call-done = bf16[2048,512]{1,0:T(8,128)(2,1)} async-done(((bf16[512,512]{1,0:T(8,128)(2,1)}), bf16[2048,512]{1,0:T(8,128)(2,1)}) %all-gather.5.cloned.1.call-update) | async-done | bytes 2097168 | tf_op jit(solution)/shard_map/all_gather | solution.py:137
  96.9 125.2 %while.30 = (s32[]{:T(128)}, f32[512,8,2,64]{0,3,2,1:T(8,128)}, f32[512,8,2]{0,2,1:T(2,128)S(1)}, f32[512,8,2]{0,2,1:T(2,128)S(1)}, s32[4]{0:T(128)S(1)}, /*inde...) while((s32[]{:T(128)}, f32[512,8,2,64]{0,3,2,1:T(8,128)}, ...), condition=%wide.region_4.5_spmd.clone, body=%wide.region_1.4_spmd.clone.sunk | while | flops 1121756160 | bytes 60301472 | solution.py:53
  117.1 10.7 bitcast_add_fusion.8
  147.9 11.3 bitcast_add_fusion.8
  179.3 11.3 bitcast_add_fusion.8
  210.7 11.3 bitcast_add_fusion.8
  229.0 26.1 %scatter_custom_fusion = bf16[6144,1024]{1,0:T(8,128)(2,1)} fusion(s32[4096]{0:T(1024)} %bitcast.415, bf16[]{:T(256)} %constant.100.clone.1, bf16[512,1024]{1,0:T(8,128)(2,1)S(1)} %multiply_convert_fusion), kind=kCustom, calls=%fused_computation.90 | custom fusion | bytes 13632000 | tf_op jit(solution)/shard_map/scatter | solution.py:160
  264.5 33.0 %gather_fusion.2 = f32[4096]{0:T(1024)S(1)} fusion(f32[512,32]{0,1:T(8,128)S(1)} %fusion.131, s32[4096]{0:T(1024)S(1)} %reshape.524), kind=kCustom, calls=%fused_computation.2 | custom fusion | bytes 65536 | tf_op jit(solution)/shard_map/jit(take_along_axis)/gather | solution.py:157
  298.8 27.3 %scatter_custom_fusion.1 = bf16[6144,1024]{1,0:T(8,128)(2,1)} fusion(s32[4096]{0:T(1024)S(1)} %bitcast.416, f32[4096]{0:T(1024)S(1)} %exponential_divide_fusion, f32[512,1024]{1,0:T(8,128)} %bitcast_convert_fusion.3, bf16[]{:T(256)} %constant.100.clone.1), kind=kCustom, calls=%fused_computation.86 | custom fusion | flops 8388608 | bytes 14696450 | tf_op jit(solution)/shard_map/scatter | solution.py:160
  326.1 208.7 %all-to-all-done = bf16[32,192,1024]{2,1,0:T(8,128)(2,1)} async-done(((bf16[32,192,1024]{2,1,0:T(8,128)(2,1)}), bf16[32,192,1024]{2,1,0:T(8,128)(2,1)}, u32[]{:S(2)}, u32[]{:S(2)}) %all-to-all-start) | async-done | bytes 12582944 | tf_op jit(solution)/shard_map/all_to_all | solution.py:169
  540.3 13.6 fusion.46
  553.9 12.3 fusion.48
  566.3 247.8 %all-to-all-done.2 = bf16[32,192,1024]{2,1,0:T(8,128)(2,1)} async-done(((bf16[32,192,1024]{2,1,0:T(8,128)(2,1)}), bf16[32,192,1024]{2,1,0:T(8,128)(2,1)}, u32[]{:S(2)}, u32[]{:S(2)}) %all-to-all-start.2) | async-done | bytes 12582944 | tf_op jit(solution)/shard_map/all_to_all | solution.py:202
  814.0 25.6 %fusion.36 = (bf16[8,4,192,512]{3,2,0,1:T(8,128)(2,1)}, bf16[8,4,192,512]{3,2,0,1:T(8,128)(2,1)}, bf16[8,4,192,512]{3,2,0,1:T(8,128)(2,1)}) fusion(f32[4,8,192,512]{3,2,1,0:T(8,128)} %fusion.48, f32[4,8,192,512]{3,2,1,0:T(8,128)} %fusion.46, bf16[4,512,1024]{2,1,0:T(8,128)(2,1)} %param.28, bf16[8,4,192,1024]{3,2,1,0:T(8,128)(2,1)} %bitcast.39), kind=kOutput, calls=%fused_computation.67 | convolution fusion | flops 6489636864 | bytes 60817408 | tf_op jit(solution)/shard_map/sicd,ifd->sicf/dot_general | solution.py:215
  860.4 14.9 fusion.64
  875.4 19.2 fusion.32
  894.5 10.7 copy.83
  905.2 229.0 %all-to-all-done.1 = bf16[32,192,1024]{2,1,0:T(8,128)(2,1)} async-done(((bf16[32,192,1024]{2,1,0:T(8,128)(2,1)}), bf16[32,192,1024]{2,1,0:T(8,128)(2,1)}, u32[]{:S(2)}, u32[]{:S(2)}) %all-to-all-start.1) | async-done | bytes 12582944 | tf_op jit(solution)/shard_map/all_to_all | solution.py:176
  1140.0 27.0 %gather_fusion = bf16[4096,1024]{1,0:T(8,128)(2,1)} fusion(bf16[6144,1024]{1,0:T(8,128)(2,1)} %bitcast.30, s32[4096]{0:T(1024)S(1)} %broadcast_clamp_fusion), kind=kCustom, calls=%fused_computation | custom fusion | bytes 16793600 | tf_op jit(solution)/shard_map/gather | solution.py:179
  1177.4 236.0 %all-to-all-done.3 = bf16[32,192,1024]{2,1,0:T(8,128)(2,1)} async-done(((bf16[32,192,1024]{2,1,0:T(8,128)(2,1)}), bf16[32,192,1024]{2,1,0:T(8,128)(2,1)}, u32[]{:S(2)}, u32[]{:S(2)}) %all-to-all-start.3) | async-done | bytes 12582944 | tf_op jit(solution)/shard_map/all_to_all | solution.py:230
  1413.5 27.4 %gather_fusion.1 = bf16[4096,1024]{1,0:T(8,128)(2,1)} fusion(bf16[6144,1024]{1,0:T(8,128)(2,1)} %bitcast.46, s32[4096]{0:T(1024)S(1)} %broadcast_clamp_fusion), kind=kCustom, calls=%fused_computation.1 | custom fusion | bytes 16793600 | tf_op jit(solution)/shard_map/gather | solution.py:233
  1440.9 11.9 convert_reduce_fusion
  1469.0 175.1 %while.31 = (s32[]{:T(128)}, f32[512,8,2,64]{0,3,2,1:T(8,128)}, f32[2048,512]{0,1:T(8,128)}, f32[2048,512]{0,1:T(8,128)}, bf16[4,512,512]{1,2,0:T(8,128)(2,1)}, ...) while((s32[]{:T(128)}, f32[512,8,2,64]{0,3,2,1:T(8,128)}, ...), condition=%wide.region_21.22_spmd.clone, body=%wide.region_20.21_spmd.clone.sunk | while | flops 2728920064 | bytes 168141104 | solution.py:53
  1535.6 10.3 fusion.217
  1648.0 13.6 bitcast_convert_fusion.1
  1663.3 14.0 bitcast_convert_fusion
  1677.3 13.0 bitcast_convert_fusion.2
  1708.3 11.9 reduce-scatter.5.cloned.1.call-done
  1723.5 242.0 %all-reduce.8.cloned.1.call-done = (bf16[4,1024,512]{2,1,0:T(8,128)(2,1)}, bf16[4,1024,512]{2,1,0:T(8,128)(2,1)}, bf16[4,512,1024]{2,1,0:T(8,128)(2,1)}) async-done(((bf16[4,1024,512]{2,1,0:T(8,128)(2,1)}, bf16[4,1024,512]{2,1,0:T(8,128)(2,1)}, bf16[4,512,1024]{2,1,0:T(8,128)(2,1)}), (bf16[4,1024,512]{2,1,0:T(8,128)(2,1)}, bf16[4,1024,512]{2,1,0:T(8,128)(2,1)}, ...) | async-done | bytes 12582928 | tf_op jit(solution)/shard_map/psum | solution.py:238
  1988.2 41.2 %all-reduce = (f32[1024]{0:T(1024)}, f32[1024]{0:T(1024)}) all-reduce(f32[1024]{0:T(1024)S(1)} %get-tuple-element.273, f32[1024]{0:T(1024)S(1)} %copy-done.66), channel_id=1, replica_groups=mesh['ctx'=4,'exp'=8] {'ctx','exp'}, use_global_device_ids=true, to_apply=%region_26.27 | all-reduce | flops 2048 | bytes 16384 | tf_op jit(solution)/shard_map/psum | solution.py:343
  2032.9 177.3 %all-reduce.6.cloned.1.call-done = (f32[1024,1024]{1,0:T(8,128)}, f32[1024,512]{1,0:T(8,128)}, f32[1024,512]{1,0:T(8,128)}, f32[1024,1024]{1,0:T(8,128)}, f32[1024,32]{0,1:T(8,128)}) async-done(((f32[1024,1024]{1,0:T(8,128)}, f32[1024,512]{1,0:T(8,128)}, f32[1024,512]{1,0:T(8,128)}, f32[1024,1024]{1,0:T(8,128)}, f32[1024,32]{0,1:T(8,128)}), (f32[1024,1024]{1,0:T(8,128)}, f32[1024,512]{1,0:T(8,128)}, ...) | async-done | bytes 12714000 | tf_op jit(solution)/shard_map/psum | solution.py:343
  (349 shorter events, 421.5 us)
Async XLA Ops:
  7.2 217.2 %copy-start = (bf16[1024,1024]{1,0:T(8,128)(2,1)S(1)}, bf16[1024,1024]{1,0:T(8,128)(2,1)}, u32[]{:S(2)}) copy-start(bf16[1024,1024]{1,0:T(8,128)(2,1)} %param.22) | copy-start | bytes 6291460
  7.2 52.0 %all-gather.3.cloned.1.call-start = ((), (), s32[]{:S(2)}) async-start(), calls=%async_computation.6 | async-start | bytes 2621440 | tf_op jit(solution)/shard_map/all_gather | solution.py:136
  13.6 44.2 %copy-start.26 = (f32[512,64]{0,1:T(8,128)}, f32[512,64]{0,1:T(8,128)S(1)}, u32[]{:S(2)}) copy-start(f32[512,64]{0,1:T(8,128)S(1)} %get-tuple-element.358) | copy-start | bytes 393220
  16.8 75.9 %all-gather.5.cloned.1.call-start = ((), (), s32[]{:S(2)}) async-start(), calls=%async_computation.7 | async-start | bytes 2621440 | tf_op jit(solution)/shard_map/all_gather | solution.py:137
  19.9 33.6 %copy-start.19 = (s32[1,512,8]{2,1,0:T(8,128)}, s32[1,512,8]{2,1,0:T(8,128)S(1)}, u32[]{:S(2)}) copy-start(s32[1,512,8]{2,1,0:T(8,128)S(1)} %copy.72) | copy-start | bytes 49156
  59.1 37.7 %copy-start.34 = (f32[512,8,2]{0,2,1:T(2,128)S(1)}, f32[512,8,2]{0,2,1:T(2,128)}, u32[]{:S(2)}) copy-start(f32[512,8,2]{0,2,1:T(2,128)} %custom-call.3) | copy-start | bytes 98308
  59.1 37.7 %copy-start.37 = (f32[512,8,2]{0,2,1:T(2,128)S(1)}, f32[512,8,2]{0,2,1:T(2,128)}, u32[]{:S(2)}) copy-start(f32[512,8,2]{0,2,1:T(2,128)} %custom-call.4) | copy-start | bytes 98308
  227.4 27.7 %copy-start.64 = (f32[512]{0:T(512)}, f32[512]{0:T(512)S(1)}, u32[]{:S(2)}) copy-start(f32[512]{0:T(512)S(1)} %add_rsqrt_fusion) | copy-start | bytes 6148
  229.0 35.1 %copy-start.15 = (bf16[512,1024]{1,0:T(8,128)(2,1)}, bf16[512,1024]{1,0:T(8,128)(2,1)S(1)}, u32[]{:S(2)}) copy-start(bf16[512,1024]{1,0:T(8,128)(2,1)S(1)} %multiply_convert_fusion) | copy-start | bytes 3145732
  255.1 279.7 %all-to-all-start = ((bf16[32,192,1024]{2,1,0:T(8,128)(2,1)}), bf16[32,192,1024]{2,1,0:T(8,128)(2,1)}, u32[]{:S(2)}, u32[]{:S(2)}) async-start(bf16[32,192,1024]{2,1,0:T(8,128)(2,1)} %bitcast.392), calls=%async_computation | async-start | bytes 25165824 | tf_op jit(solution)/shard_map/all_to_all | solution.py:169
  264.5 33.2 %copy-start.20 = (s32[1,512,8]{2,1,0:T(8,128)S(1)}, s32[1,512,8]{2,1,0:T(8,128)}, u32[]{:S(2)}) copy-start(s32[1,512,8]{2,1,0:T(8,128)} %copy-done.19) | copy-start | bytes 49156
  264.5 34.2 %copy-start.55 = (s32[4096]{0:T(1024)S(1)}, s32[4096]{0:T(1024)}, u32[]{:S(2)}) copy-start(s32[4096]{0:T(1024)} %eq.32) | copy-start | bytes 49156
  264.5 34.2 %copy-start.57 = (s32[4096,1]{0,1:T(1,128)S(1)}, s32[4096,1]{0,1:T(1,128)}, u32[]{:S(2)}) copy-start(s32[4096,1]{0,1:T(1,128)} %compare_select_fusion.1) | copy-start | bytes 49156
  534.8 279.3 %all-to-all-start.2 = ((bf16[32,192,1024]{2,1,0:T(8,128)(2,1)}), bf16[32,192,1024]{2,1,0:T(8,128)(2,1)}, u32[]{:S(2)}, u32[]{:S(2)}) async-start(bf16[32,192,1024]{2,1,0:T(8,128)(2,1)} %bitcast.393), calls=%async_computation.2 | async-start | bytes 25165824 | tf_op jit(solution)/shard_map/all_to_all | solution.py:202
  540.3 13.7 copy-start.67
  854.8 279.4 %all-to-all-start.1 = ((bf16[32,192,1024]{2,1,0:T(8,128)(2,1)}), bf16[32,192,1024]{2,1,0:T(8,128)(2,1)}, u32[]{:S(2)}, u32[]{:S(2)}) async-start(bf16[32,192,1024]{2,1,0:T(8,128)(2,1)} %bitcast.394), calls=%async_computation.1 | async-start | bytes 25165824 | tf_op jit(solution)/shard_map/all_to_all | solution.py:176
  1134.2 279.2 %all-to-all-start.3 = ((bf16[32,192,1024]{2,1,0:T(8,128)(2,1)}), bf16[32,192,1024]{2,1,0:T(8,128)(2,1)}, u32[]{:S(2)}, u32[]{:S(2)}) async-start(bf16[32,192,1024]{2,1,0:T(8,128)(2,1)} %bitcast.391), calls=%async_computation.3 | async-start | bytes 25165824 | tf_op jit(solution)/shard_map/all_to_all | solution.py:230
  1139.7 562.9 %reduce-scatter.3.cloned.1.call-start = ((), (), s32[]{:S(2)}) async-start(), calls=%async_computation.8 | async-start | bytes 2621440 | tf_op jit(solution)/shard_map/reduce_scatter | solution.py:309
  1440.8 11.9 copy-start.54
  1440.8 12.0 copy-start.51
  1440.8 12.0 copy-start.63
  1440.9 12.0 copy-start.65
  1474.1 11.2 copy-start.2
  1492.3 10.3 copy-start.6
  1517.4 11.2 copy-start.2
  1561.2 11.2 copy-start.2
  1605.1 11.2 copy-start.2
  1647.9 72.2 %reduce-scatter.5.cloned.1.call-start = ((), (), s32[]{:S(2)}) async-start(), calls=%async_computation.9 | async-start | bytes 2621440 | tf_op jit(solution)/shard_map/reduce_scatter | solution.py:312
  1648.0 13.6 copy-start.7
  1663.3 302.1 %all-reduce.8.cloned.1.call-start = ((), (), s32[]{:S(2)}) async-start(), calls=%async_computation.11 | async-start | bytes 25165824 | tf_op jit(solution)/shard_map/psum | solution.py:238
  1690.3 519.9 %all-reduce.6.cloned.1.call-start = ((), (), s32[]{:S(2)}) async-start(), calls=%async_computation.10 | async-start | bytes 25427968 | tf_op jit(solution)/shard_map/psum | solution.py:343
  1985.6 43.8 %copy-start.14 = (f32[512,1024]{1,0:T(8,128)S(1)}, f32[512,1024]{1,0:T(8,128)}, u32[]{:S(2)}) copy-start(f32[512,1024]{1,0:T(8,128)} %copy-done.12) | copy-start | bytes 6291460
  (52 other events, 207.9 us)
Sparse Core Ops, SparseCore 0:
  16.9 38.0 all-gather.2
  57.4 35.2 all-gather.4
  1648.1 33.0 reduce-scatter.2
  1684.9 35.2 reduce-scatter.4
  1724.4 240.9 all-reduce.7
  1972.3 237.9 all-reduce.5
where the time goes:
time: 2240 us; the launch traced here: 2230 us
  waiting for transfers between devices  1380 us (62%)
  matrix products  389 us (17%)
  local copies, waits for them, and re-layouts  201 us (9%)
  other arithmetic  172 us (8%)
  blocking collectives  41.2 us (2%)
  starting transfers between devices  22.9 us (1%)
    all_to_all x1, waiting for transfers between devices, per_device(): lax.all_to_all(pack_rows(out_grad), 'exp', split_axis=0, concat_axis=0, t...  248 us
    psum x1, waiting for transfers between devices, per_device(): lax.psum(wgate_grad.astype(jnp.bfloat16), 'ctx').astype(jnp.float32)  242 us
    all_to_all x1, waiting for transfers between devices, per_device(): lax.all_to_all(row_grad.reshape(experts, CAP, model_width), 'exp', split_...  236 us
    all_to_all x1, waiting for transfers between devices, per_device(): lax.all_to_all(produced.reshape(experts, CAP, model_width), 'exp', split_...  229 us
    all_to_all x1, waiting for transfers between devices, per_device(): lax.all_to_all(pack_rows(repeated), 'exp', split_axis=0, concat_axis=0, t...  209 us
    psum x1, waiting for transfers between devices, per_device(): lax.psum((wq_grad, wk_grad, wv_grad, wout_grad, router_grad, gain_one_gra...  177 us
  transfers between devices with their start and end apart: 10, of which 8 were waited for; matrix products, arithmetic and copies ran while one was open for 14% of the time, Pallas kernels for 0%

commit v1 on v0

v1 whole, which is shorter than its diff:
```python
import functools

import jax
import jax.numpy as jnp
from jax import lax
from jax.experimental import pallas as pl
from jax.experimental.pallas import tpu as pltpu
from jax.sharding import PartitionSpec as P

HEAD_DIM = 64
CAP = 192


SCALE = 0.015625
THETA = 10000.0
EPSILON = 1e-06
NEG = -1e30

F32 = jnp.float32
BF16 = jnp.bfloat16
NN = (((1,), (0,)), ((), ()))
NT = (((1,), (1,)), ((), ()))
TN = (((0,), (0,)), ((), ()))


def mm(left, right, dims=NN):
    return lax.dot_general(left, right, dims, preferred_element_type=F32)


def normalize(values):
    factor = lax.rsqrt(jnp.mean(values * values, axis=-1, keepdims=True) + EPSILON)
    return (values * factor, factor)


def norm_back(grad_scaled, scaled, factor):
    return factor * (grad_scaled - scaled * jnp.mean(grad_scaled * scaled, axis=-1, keepdims=True))


def rotate_columns(values, cosine, sine, direction):
    half = HEAD_DIM // 2
    split = values.reshape(-1, 2, half, values.shape[-1])
    first, second = split[:, 0], split[:, 1]
    turned = direction * sine
    return jnp.stack(
        [first * cosine - second * turned, second * cosine + first * turned], axis=1
    ).reshape(values.shape)


def head_columns(block, which):
    low = 2 * HEAD_DIM * which
    pair = jnp.concatenate(
        [block[low : low + HEAD_DIM], block[low + HEAD_DIM : low + 2 * HEAD_DIM]], axis=1
    )
    empty = jnp.zeros_like(pair)
    return jnp.concatenate([pair, empty] if which == 0 else [empty, pair], axis=0)


def causal(rows):
    keys = lax.broadcasted_iota(jnp.int32, (rows, rows), 0)
    places = lax.broadcasted_iota(jnp.int32, (rows, rows), 1)
    one = keys <= places
    return jnp.concatenate([one, one], axis=1)


def attend_kernel(own_ref, q_ref, k_ref, v_ref, wide_ref, low_ref, log_ref):
    rows = q_ref.shape[1]
    own = own_ref[0]
    columns = [head_columns(q_ref[...], which) for which in range(2)]

    def visit(block, carried, masked):
        at = pl.ds(pl.multiple_of(block * rows, rows), rows)
        keys = k_ref[at, :]
        values = v_ref[at, :].T
        result = []
        for which in range(2):
            running, mass, total = carried[which]
            scores = mm(keys, columns[which])
            if masked:
                scores = jnp.where(causal(rows), scores, NEG)
            newest = jnp.maximum(running, jnp.max(scores, axis=0, keepdims=True))
            weights = jnp.exp(scores - newest)
            rescale = jnp.exp(running - newest)
            mass = mass * rescale + jnp.sum(weights, axis=0, keepdims=True)
            mine = values[which * HEAD_DIM : (which + 1) * HEAD_DIM]
            total = total * rescale + mm(mine, weights.astype(BF16))
            result.append((newest, mass, total))
        return tuple(result)

    initial = tuple(
        (
            jnp.full((1, 2 * rows), NEG, F32),
            jnp.zeros((1, 2 * rows), F32),
            jnp.zeros((HEAD_DIM, 2 * rows), F32),
        )
        for _ in range(2)
    )
    carried = visit(own, initial, True)
    carried = lax.fori_loop(0, own, lambda block, inner: visit(block, inner, False), carried)
    for which in range(2):
        running, mass, total = carried[which]
        result = total / mass
        logs = running + jnp.log(mass)
        for group in range(2):
            head = 2 * which + group
            part = slice(group * rows, (group + 1) * rows)
            wide_ref[head * HEAD_DIM : (head + 1) * HEAD_DIM, :] = result[:, part]
            log_ref[0, head : head + 1, :] = logs[:, part]
    low_ref[...] = wide_ref[...].T.astype(BF16)


def attend_back_kernel(
    own_ref, q_ref, k_ref, v_ref, grad_ref, wide_ref, log_ref, dq_ref, dk_ref, dv_ref, sum_ref
):
    rows = q_ref.shape[1]
    own = own_ref[0]
    columns = [head_columns(q_ref[...], which) for which in range(2)]
    grads = [head_columns(grad_ref[...], which) for which in range(2)]
    offsets, logs = [], []
    for which in range(2):
        pieces = []
        for group in range(2):
            part = slice((2 * which + group) * HEAD_DIM, (2 * which + group + 1) * HEAD_DIM)
            pieces.append(
                jnp.sum(grad_ref[part, :].astype(F32) * wide_ref[part, :], axis=0, keepdims=True)
            )
        offsets.append(jnp.concatenate(pieces, axis=1))
        logs.append(
            jnp.concatenate(
                [log_ref[0, 2 * which : 2 * which + 1, :], log_ref[0, 2 * which + 1 : 2 * which + 2, :]],
                axis=1,
            )
        )
    sum_ref[...] = jnp.zeros_like(sum_ref)
    dk_ref[...] = jnp.zeros_like(dk_ref)
    dv_ref[...] = jnp.zeros_like(dv_ref)

    def visit(block, masked):
        at = pl.ds(pl.multiple_of(block * rows, rows), rows)
        keys = k_ref[at, :]
        values = v_ref[at, :]
        turned = keys.T
        key_sum, value_sum = None, None
        for which in range(2):
            soft = jnp.exp(mm(keys, columns[which]) - logs[which])
            if masked:
                soft = jnp.where(causal(rows), soft, 0.0)
            prob_grad = mm(values, grads[which])
            score_grad = (soft * (prob_grad - offsets[which])).astype(BF16)
            value_part = mm(soft.astype(BF16), grads[which], NT)
            key_part = mm(score_grad, columns[which], NT)
            key_sum = key_part if key_sum is None else key_sum + key_part
            value_sum = value_part if value_sum is None else value_sum + value_part
            mine = slice(which * HEAD_DIM, (which + 1) * HEAD_DIM)
            sum_ref[mine, :] += mm(turned[mine], score_grad)
        dk_ref[at, :] = key_sum.astype(BF16)
        dv_ref[at, :] = value_sum.astype(BF16)

    visit(own, True)
    lax.fori_loop(0, own, lambda block, inner: (visit(block, False), inner)[1], 0)
    for which in range(2):
        for group in range(2):
            head = 2 * which + group
            dq_ref[head * HEAD_DIM : (head + 1) * HEAD_DIM, :] = (
                sum_ref[
                    which * HEAD_DIM : (which + 1) * HEAD_DIM, group * rows : (group + 1) * rows
                ]
                * SCALE
            )


def attend(own, queries, keys, values):
    width, rows = queries.shape
    length, kv_width = keys.shape
    pairs = kv_width // (2 * HEAD_DIM)
    step = width // pairs
    heads = step // HEAD_DIM
    return pl.pallas_call(
        attend_kernel,
        grid=(pairs,),
        in_specs=[
            pl.BlockSpec(memory_space=pltpu.SMEM),
            pl.BlockSpec((step, rows), lambda p: (p, 0)),
            pl.BlockSpec((length, 2 * HEAD_DIM), lambda p: (0, p)),
            pl.BlockSpec((length, 2 * HEAD_DIM), lambda p: (0, p)),
        ],
        out_specs=[
            pl.BlockSpec((step, rows), lambda p: (p, 0)),
            pl.BlockSpec((rows, step), lambda p: (0, p)),
            pl.BlockSpec((1, heads, rows), lambda p: (p, 0, 0)),
        ],
        out_shape=[
            jax.ShapeDtypeStruct((width, rows), F32),
            jax.ShapeDtypeStruct((rows, width), BF16),
            jax.ShapeDtypeStruct((pairs, heads, rows), F32),
        ],
        compiler_params=pltpu.CompilerParams(vmem_limit_bytes=48 * 1024 * 1024),
        name="attend",
    )(own, queries, keys, values)


def attend_back(own, queries, keys, values, grads, wide, logs):
    width, rows = queries.shape
    length, kv_width = keys.shape
    pairs = kv_width // (2 * HEAD_DIM)
    step = width // pairs
    heads = step // HEAD_DIM
    columns = pl.BlockSpec((step, rows), lambda p: (p, 0))
    whole = pl.BlockSpec((length, 2 * HEAD_DIM), lambda p: (0, p))
    return pl.pallas_call(
        attend_back_kernel,
        grid=(pairs,),
        in_specs=[
            pl.BlockSpec(memory_space=pltpu.SMEM),
            columns,
            whole,
            whole,
            columns,
            columns,
            pl.BlockSpec((1, heads, rows), lambda p: (p, 0, 0)),
        ],
        out_specs=[columns, whole, whole],
        out_shape=[
            jax.ShapeDtypeStruct((width, rows), F32),
            jax.ShapeDtypeStruct((length, kv_width), BF16),
            jax.ShapeDtypeStruct((length, kv_width), BF16),
        ],
        scratch_shapes=[pltpu.VMEM((2 * HEAD_DIM, 2 * rows), F32)],
        compiler_params=pltpu.CompilerParams(vmem_limit_bytes=48 * 1024 * 1024),
        name="attend_back",
    )(own, queries, keys, values, grads, wide, logs)


def experts_kernel(blocks, owned, first, *refs):
    if first:
        x_ref, c_ref, rank_ref, mask_ref, router_ref, gate_ref, up_ref, down_ref = refs[:8]
        olds = (None, None, None)
        rest = refs[8:]
    else:
        x_ref, c_ref, rank_ref, mask_ref, router_ref, gate_ref, up_ref, down_ref = refs[:8]
        olds = refs[8:11]
        rest = refs[11:]
    (
        y_ref,
        dx_ref,
        dgate_ref,
        dup_ref,
        ddown_ref,
        chosen_ref,
        rows_x,
        rows_c,
        rows_w,
    ) = rest
    step = pl.program_id(0)
    tokens = x_ref.shape[1]

    def hot(block, expert):
        slots = lax.broadcasted_iota(jnp.int32, (CAP, tokens), 0)
        return slots == rank_ref[block, pl.ds(expert, 1), :]

    def places(block):
        return jnp.concatenate(
            [hot(block, e).astype(F32).astype(BF16) for e in range(owned)], axis=0
        )

    @pl.when(step < blocks)
    def gather():
        block = step
        at = pl.ds(pl.multiple_of(block * CAP, CAP), CAP)
        select = places(block)
        picked = mm(select, x_ref[0]).astype(BF16)
        upstream = mm(select, c_ref[0]).astype(BF16)
        logits = mm(picked, router_ref[...])
        named = mm(select, mask_ref[block]) > 0.5
        masked = jnp.where(named, logits, NEG)
        grown = jnp.where(
            named, jnp.exp(masked - jnp.max(masked, axis=1, keepdims=True)), 0.0
        )
        mass = jnp.sum(grown, axis=1, keepdims=True)
        weights = grown / jnp.where(mass > 0.0, mass, 1.0)
        for e in range(owned):
            part = slice(e * CAP, (e + 1) * CAP)
            rows_x[e, at, :] = picked[part]
            rows_c[e, at, :] = upstream[part]
            rows_w[e, at, :] = weights[part, e : e + 1]

    @pl.when((step >= blocks) & (step < blocks + owned))
    def multiply():
        e = step - blocks
        x = rows_x[e]
        c = rows_c[e]
        weight = rows_w[e]
        gate = mm(x, gate_ref[0])
        up = mm(x, up_ref[0])
        back = mm(c, down_ref[0], NT)
        sigmoid = 1.0 / (1.0 + jnp.exp(-gate))
        activated = gate * sigmoid
        hidden = activated * up
        scored = jnp.sum(hidden * back, axis=1, keepdims=True)
        for block in range(blocks):
            part = scored[block * CAP : (block + 1) * CAP]
            chosen_ref[0, block : block + 1, :] = jnp.sum(
                jnp.where(hot(block, e), part, 0.0), axis=0, keepdims=True
            )
        weighted = (hidden * weight).astype(BF16)
        back = back * weight
        gate_back = (back * up * sigmoid * (1.0 + gate * (1.0 - sigmoid))).astype(BF16)
        up_back = (back * activated).astype(BF16)
        turned = x.T
        grads = (mm(turned, gate_back), mm(turned, up_back), mm(weighted.T, c))
        for out_ref, old_ref, grad in zip((dgate_ref, dup_ref, ddown_ref), olds, grads):
            if old_ref is not None:
                grad = grad + old_ref[0].astype(F32)
            out_ref[0] = grad.astype(BF16)
        rows_c[e] = mm(weighted, down_ref[0]).astype(BF16)
        rows_x[e] = (mm(gate_back, gate_ref[0], NT) + mm(up_back, up_ref[0], NT)).astype(BF16)

    @pl.when(step >= blocks + owned)
    def scatter():
        block = step - blocks - owned
        at = pl.ds(pl.multiple_of(block * CAP, CAP), CAP)
        select = places(block).T
        y_ref[0] = mm(
            select, jnp.concatenate([rows_c[e, at, :] for e in range(owned)], axis=0)
        ).astype(BF16)
        dx_ref[0] = mm(
            select, jnp.concatenate([rows_x[e, at, :] for e in range(owned)], axis=0)
        ).astype(BF16)


def run_experts(x, c, rank, mask, router, w_gate, w_up, w_down, olds):
    blocks, tokens, width = x.shape
    owned, _, hidden = w_gate.shape
    first = olds is None

    def entering(s):
        return (jnp.minimum(s, blocks - 1), 0, 0)

    def expert(s):
        return (jnp.clip(s - blocks, 0, owned - 1), 0, 0)

    def leaving(s):
        return (jnp.clip(s - blocks - owned, 0, blocks - 1), 0, 0)

    def fixed(*shape):
        return pl.BlockSpec(shape, lambda s: (0,) * len(shape))

    grads = [
        pl.BlockSpec((1, width, hidden), expert),
        pl.BlockSpec((1, width, hidden), expert),
        pl.BlockSpec((1, hidden, width), expert),
    ]
    return pl.pallas_call(
        functools.partial(experts_kernel, blocks, owned, first),
        grid=(2 * blocks + owned,),
        in_specs=[
            pl.BlockSpec((1, tokens, width), entering),
            pl.BlockSpec((1, tokens, width), entering),
            fixed(*rank.shape),
            fixed(*mask.shape),
            fixed(*router.shape),
            *grads,
            *([] if first else grads),
        ],
        out_specs=[
            pl.BlockSpec((1, tokens, width), leaving),
            pl.BlockSpec((1, tokens, width), leaving),
            *grads,
            pl.BlockSpec((1, blocks, tokens), expert),
        ],
        out_shape=[
            jax.ShapeDtypeStruct(x.shape, BF16),
            jax.ShapeDtypeStruct(x.shape, BF16),
            jax.ShapeDtypeStruct(w_gate.shape, BF16),
            jax.ShapeDtypeStruct(w_up.shape, BF16),
            jax.ShapeDtypeStruct(w_down.shape, BF16),
            jax.ShapeDtypeStruct((owned, blocks, tokens), F32),
        ],
        scratch_shapes=[
            pltpu.VMEM((owned, blocks * CAP, width), BF16),
            pltpu.VMEM((owned, blocks * CAP, width), BF16),
            pltpu.VMEM((owned, blocks * CAP, 1), F32),
        ],
        compiler_params=pltpu.CompilerParams(vmem_limit_bytes=60 * 1024 * 1024),
        name="experts",
    )(x, c, rank, mask, router, w_gate, w_up, w_down, *([] if first else olds))


def swap(value, bit, peers):
    return lax.ppermute(value, "exp", [(i, i ^ bit) for i in range(peers)])


def gather_blocks(value, peers):
    held = {0: value}
    bit = peers // 2
    while bit >= 1:
        for m in list(held):
            held[m | bit] = swap(held[m], bit, peers)
        bit //= 2
    return [held[m] for m in range(peers)]


def reduce_blocks(parts, peers):
    held = dict(enumerate(parts))
    bit = 1
    while bit < peers:
        for m in sorted(held, reverse=True):
            if m & bit:
                arrived = swap(held.pop(m), bit, peers)
                held[m ^ bit] = (
                    held[m ^ bit].astype(F32) + arrived.astype(F32)
                ).astype(BF16)
        bit *= 2
    return held[0]


def per_device(
    tokens,
    attn_gain,
    query_weight,
    key_weight,
    value_weight,
    output_weight,
    moe_gain,
    w_router,
    routes,
    w_gate,
    w_up,
    w_down,
    cotangent,
):
    tok_rows = tokens.shape[1]
    model_width = tokens.shape[2]
    experts = w_router.shape[1]
    owned = w_gate.shape[0]
    peers = lax.axis_size("exp")
    here = lax.axis_index("exp")
    own = lax.axis_index("ctx")
    positions = own * tok_rows + jnp.arange(tok_rows, dtype=jnp.int32)
    half = HEAD_DIM // 2
    inverse = THETA ** (-jnp.arange(half, dtype=F32) * 2.0 / HEAD_DIM)
    angles = inverse[:, None] * positions.astype(F32)[None, :]
    cosine, sine = jnp.cos(angles), jnp.sin(angles)

    cot_blocks = gather_blocks(cotangent[0], peers)
    route_blocks = jnp.stack(gather_blocks(routes[0], peers))
    order = jnp.arange(experts, dtype=jnp.int32)
    order = ((order // owned) ^ here) * owned + order % owned
    permutation = (jnp.arange(experts, dtype=jnp.int32)[:, None] == order[None, :]).astype(BF16)
    named = jnp.any(route_blocks[..., None] == order, axis=2)
    mask = named.astype(BF16)
    earlier = jnp.tril(jnp.ones((tok_rows, tok_rows), BF16))
    rank = jnp.einsum(
        "ts,bse->bet", earlier, mask[..., :owned], preferred_element_type=F32
    ).astype(jnp.int32)
    rank = jnp.where(jnp.swapaxes(named[..., :owned], 1, 2), rank - 1, -1)
    router = mm(w_router, permutation).astype(BF16)

    layer_inputs = tokens[0].astype(F32)
    scaled_one, factor_one = normalize(layer_inputs)
    first_normalized = (scaled_one * attn_gain).astype(BF16)
    value_rows = mm(first_normalized, value_weight).astype(BF16)
    key_turned = rotate_columns(
        jnp.einsum("de,td->et", key_weight, first_normalized, preferred_element_type=F32),
        cosine,
        sine,
        1.0,
    ).astype(BF16)
    key_rows = key_turned.T
    queries = (
        rotate_columns(
            jnp.einsum("de,td->et", query_weight, first_normalized, preferred_element_type=F32),
            cosine,
            sine,
            1.0,
        ).astype(BF16)
        * SCALE
    ).astype(BF16)
    keys = lax.all_gather(key_rows, "ctx", axis=0, tiled=True)
    values = lax.all_gather(value_rows, "ctx", axis=0, tiled=True)
    own_index = jnp.full((1,), own, jnp.int32)
    attended_wide, attended_low, logs = attend(own_index, queries, keys, values)
    residual_stream = layer_inputs + mm(attended_low, output_weight)
    scaled_two, factor_two = normalize(residual_stream)
    normed_two = (scaled_two * moe_gain).astype(BF16)

    x_blocks = gather_blocks(normed_two, peers)
    olds = None
    mixed, dx, chosen = [], [], []
    group = min(4, peers)
    for start in range(0, peers, group):
        part = slice(start, start + group)
        y_part, dx_part, *olds, chosen_part = run_experts(
            jnp.stack(x_blocks[part]),
            jnp.stack(cot_blocks[part]),
            rank[part],
            mask[part],
            router,
            w_gate,
            w_up,
            w_down,
            olds,
        )
        mixed += [y_part[i] for i in range(group)]
        dx += [dx_part[i] for i in range(group)]
        chosen += [chosen_part[:, i] for i in range(group)]

    logits = mm(normed_two, router)
    named_here = named[0]
    masked = jnp.where(named_here, logits, NEG)
    grown = jnp.where(named_here, jnp.exp(masked - jnp.max(masked, axis=1, keepdims=True)), 0.0)
    gate_weights = grown / jnp.sum(grown, axis=1, keepdims=True)
    gate_grad = jnp.concatenate(
        [chosen[0]] + [swap(chosen[m], m, peers) for m in range(1, peers)], axis=0
    ).T
    chosen_grad = gate_weights * (
        gate_grad - jnp.sum(gate_weights * gate_grad, axis=-1, keepdims=True)
    )
    logit_grad = mm(chosen_grad.astype(BF16), permutation, NT).astype(BF16)
    router_grad = mm(normed_two, logit_grad, TN)

    upstream = cotangent[0].astype(F32)
    normed_two_grad = mm(logit_grad, w_router, NT) + reduce_blocks(dx, peers).astype(F32)
    output = residual_stream + reduce_blocks(mixed, peers).astype(F32)
    wgate_grad, wup_grad, down_grad = (
        lax.psum(grad, "ctx").astype(F32) for grad in olds
    )
    gain_two_grad = jnp.sum(normed_two_grad * scaled_two, axis=0)
    residual_grad = upstream + norm_back(normed_two_grad * moe_gain, scaled_two, factor_two)
    residual_low = residual_grad.astype(BF16)
    wout_grad = mm(attended_low, residual_low, TN)
    attended_grad = mm(output_weight, residual_low, NT).astype(BF16)

    query_grad, key_sum, value_sum = attend_back(
        own_index, queries, keys, values, attended_grad, attended_wide, logs
    )
    key_grad, value_grad = (
        lax.psum_scatter(part, "ctx", scatter_dimension=0, tiled=True).astype(F32)
        for part in (key_sum, value_sum)
    )
    query_back = rotate_columns(query_grad, cosine, sine, -1.0).astype(BF16)
    key_back = rotate_columns(key_grad.T, cosine, sine, -1.0).astype(BF16)
    value_back = value_grad.astype(BF16)
    wq_grad = jnp.einsum("td,et->de", first_normalized, query_back, preferred_element_type=F32)
    wk_grad = jnp.einsum("td,et->de", first_normalized, key_back, preferred_element_type=F32)
    wv_grad = mm(first_normalized, value_back, TN)
    normed_one_grad = (
        jnp.einsum("et,de->td", query_back, query_weight, preferred_element_type=F32)
        + jnp.einsum("et,de->td", key_back, key_weight, preferred_element_type=F32)
        + mm(value_back, value_weight, NT)
    )
    gain_one_grad = jnp.sum(normed_one_grad * scaled_one, axis=0)
    input_grad = residual_grad + norm_back(normed_one_grad * attn_gain, scaled_one, factor_one)
    early = lax.psum(
        (wout_grad.astype(BF16), router_grad.astype(BF16), gain_two_grad.astype(BF16)),
        ("ctx", "exp"),
    )
    late = lax.psum(
        tuple(g.astype(BF16) for g in (wq_grad, wk_grad, wv_grad, gain_one_grad)),
        ("ctx", "exp"),
    )
    wout_grad, router_grad, gain_two_grad = (g.astype(F32) for g in early)
    wq_grad, wk_grad, wv_grad, gain_one_grad = (g.astype(F32) for g in late)
    return (
        output.astype(BF16)[None],
        input_grad[None],
        gain_one_grad,
        wq_grad,
        wk_grad,
        wv_grad,
        wout_grad,
        gain_two_grad,
        router_grad,
        wgate_grad,
        wup_grad,
        down_grad,
    )


def solution(mesh):
    return jax.shard_map(
        per_device,
        mesh=mesh,
        in_specs=(
            P("exp", "ctx", None),
            P(),
            P(),
            P(),
            P(),
            P(),
            P(),
            P(),
            P("exp", "ctx", None),
            P("exp", None, None),
            P("exp", None, None),
            P("exp", None, None),
            P("exp", "ctx", None),
        ),
        out_specs=(
            P("exp", "ctx", None),
            P("exp", "ctx", None),
            P(),
            P(),
            P(),
            P(),
            P(),
            P(),
            P(),
            P("exp", None, None),
            P("exp", None, None),
            P("exp", None, None),
        ),
        check_vma=False,
    )
```

time: 2240 us -> 1050 us (0.47)
  waiting for transfers between devices: 1380 us -> 673 us
  matrix products: 389 us -> 34.5 us
  local copies, waits for them, and re-layouts: 201 us -> 31.3 us
  Pallas kernels: 0 us -> 141 us
  other arithmetic: 172 us -> 76.4 us
    all_to_all x4 -> x0, waiting for transfers between devices: 921 us -> none  [the longest x1 248 us: per_device(): lax.all_to_all(pack_rows(out_grad), 'exp', split_axis=0, concat_axis=0, t...]
    dot_general x52 -> x18, matrix products: 389 us -> 34.5 us  [the longest x11 18.7 us: mm(): return lax.dot_general(left, right, dims, preferred_element_type=F32)]
    ppermute x0 -> x42, waiting for transfers between devices: none -> 198 us  [swap(): return lax.ppermute(value, 'exp', [(i, i ^ bit) for i in range(peers)])]
    pallas_call x0 -> x4, Pallas kernels: none -> 141 us  [the longest x2 120 us: run_experts(): pl.pallas_call(functools.partial(experts_kernel, blocks, owned, first), g...]
    reduce_scatter x2, waiting for transfers between devices: 11.9 us -> 110 us  [per_device(): lax.psum_scatter(part, 'ctx', scatter_dimension=0, tiled=True).astype(F32)]
    gather x6 -> x0, local copies, waits for them, and re-layouts: 87.8 us -> none  [the longest x4 33.5 us: per_device(): jnp.take_along_axis(logits, expert_ids, axis=1)]
    psum x2, waiting for transfers between devices: 419 us -> 345 us  [the longest x1 234 us: per_device(): lax.psum(grad, 'ctx').astype(F32)]
    reduce_sum x10 -> x2, other arithmetic: 62.3 us -> 3.97 us  [the longest x1 3.36 us: per_device(): gain_two_grad = jnp.sum(normed_two_grad * scaled_two, axis=0)]
  transfers between devices with their start and end apart: 10 -> 48, of which waited for: 8 -> 17; matrix products, arithmetic and copies ran while one was open for 14% -> 9% of each run, Pallas kernels for 0% -> 6%
where the time goes in v1:
time: 1050 us
  waiting for transfers between devices  673 us (64%)
  Pallas kernels  141 us (13%)
  other arithmetic  76.4 us (7%)
  blocking collectives  41 us (4%)
  starting transfers between devices  36.4 us (3%)
  matrix products  34.5 us (3%)
  local copies, waits for them, and re-layouts  31.3 us (3%)
  between operations  15.1 us (1%)
    psum x1, waiting for transfers between devices, per_device(): lax.psum(grad, 'ctx').astype(F32)  234 us
    ppermute x42, waiting for transfers between devices, swap(): return lax.ppermute(value, 'exp', [(i, i ^ bit) for i in range(peers)])  198 us
    pallas_call x2, Pallas kernels, run_experts(): pl.pallas_call(functools.partial(experts_kernel, blocks, owned, first), g...  120 us
    psum x1, waiting for transfers between devices, per_device(): lax.psum(tuple((g.astype(BF16) for g in (wq_grad, wk_grad, wv_grad, gain_...  111 us
    reduce_scatter x2, waiting for transfers between devices, per_device(): lax.psum_scatter(part, 'ctx', scatter_dimension=0, tiled=True).astype(F32)  110 us
    psum x1, blocking collectives, per_device(): lax.psum(tuple((g.astype(BF16) for g in (wq_grad, wk_grad, wv_grad, gain_...  41 us
    ppermute x42, starting transfers between devices, swap(): return lax.ppermute(value, 'exp', [(i, i ^ bit) for i in range(peers)])  35.8 us
  transfers between devices with their start and end apart: 48, of which 17 were waited for; matrix products, arithmetic and copies ran while one was open for 9% of the time, Pallas kernels for 6%

profile of v1, /device:TPU:0, one launch (start us, length us, event | category | flops | bytes accessed | tf_op | source)
XLA Modules:
  0.0 1048.3 jit_solution(1260297387727116598)
XLA Ops:
  24.0 4.4 convolution_bitcast_fusion
  39.8 32.9 %collective-permute-done.20 = bf16[512,1024]{1,0:T(8,128)(2,1)} collective-permute-done((bf16[512,1024]{1,0:T(8,128)(2,1)}, bf16[512,1024]{1,0:T(8,128)(2,1)}, u32[]{:S(2)}, u32[]{:S(2)}) %collective-permute-start.20) | collective-permute-done | bytes 1048608 | tf_op jit(solution)/shard_map/ppermute | solution.py:389
  72.8 17.9 %all-gather.5.cloned.1.call-done.v_ref = bf16[2048,512]{1,0:T(8,128)(2,1)} async-done(((bf16[512,512]{1,0:T(8,128)(2,1)}), bf16[2048,512]{1,0:T(8,128)(2,1)}) %all-gather.5.cloned.1.call-update) | async-done | bytes 2097168 | tf_op jit(solution)/shard_map/all_gather | solution.py:479
  90.7 7.6 attend.1
  114.1 37.1 %collective-permute-done.16 = bf16[512,1024]{1,0:T(8,128)(2,1)} collective-permute-done((bf16[512,1024]{1,0:T(8,128)(2,1)}, bf16[512,1024]{1,0:T(8,128)(2,1)}, u32[]{:S(2)}, u32[]{:S(2)}) %collective-permute-start.16) | collective-permute-done | bytes 1048608 | tf_op jit(solution)/shard_map/ppermute | solution.py:389
  155.0 3.8 pad_maximum_fusion.1.refs_1_
  159.3 17.3 %collective-permute-done.18 = bf16[512,1024]{1,0:T(8,128)(2,1)} collective-permute-done((bf16[512,1024]{1,0:T(8,128)(2,1)}, bf16[512,1024]{1,0:T(8,128)(2,1)}, u32[]{:S(2)}, u32[]{:S(2)}) %collective-permute-start.18) | collective-permute-done | bytes 1048608 | tf_op jit(solution)/shard_map/ppermute | solution.py:389
  176.6 3.6 pad_maximum_fusion.3.refs_1_
  183.8 59.1 %experts.2 = (bf16[4,512,1024]{2,1,0:T(8,128)(2,1)}, bf16[4,512,1024]{2,1,0:T(8,128)(2,1)}, bf16[4,1024,512]{2,1,0:T(8,128)(2,1)}, bf16[4,1024,512]{2,1,0:T(8,12...) custom-call(bf16[4,512,1024]{2,1,0:T(8,128)(2,1)} %pad_maximum_fusion.refs_0_, ...), custom_call_target="tpu_custom_call" | custom-call | tf_op jit(solution)/shard_map/experts/pallas_call | solution.py:352
  242.9 3.8 pad_maximum_fusion.2.refs_0_
  246.7 60.4 %experts.3 = (bf16[4,512,1024]{2,1,0:T(8,128)(2,1)}, bf16[4,512,1024]{2,1,0:T(8,128)(2,1)}, bf16[4,1024,512]{2,1,0:T(8,128)(2,1)}, bf16[4,1024,512]{2,1,0:T(8,12...) custom-call(bf16[4,512,1024]{2,1,0:T(8,128)(2,1)} %pad_maximum_fusion.2.refs_0_, ...), custom_call_target="tpu_custom_call" | custom-call | tf_op jit(solution)/shard_map/experts/pallas_call | solution.py:352
  328.9 16.0 %collective-permute-done.31 = f32[4,512]{1,0:T(4,128)S(1)} collective-permute-done((f32[4,512]{1,0:T(4,128)S(1)}, f32[4,512]{1,0:T(4,128)S(1)}, u32[]{:S(2)}, u32[]{:S(2)}) %collective-permute-start.31) | collective-permute-done | bytes 8224 | tf_op jit(solution)/shard_map/ppermute | solution.py:389
  344.8 4.2 collective-permute-start.26
  355.9 16.1 %collective-permute-done.33 = f32[4,512]{1,0:T(4,128)S(1)} collective-permute-done((f32[4,512]{1,0:T(4,128)S(1)}, f32[4,512]{1,0:T(4,128)S(1)}, u32[]{:S(2)}, u32[]{:S(2)}) %collective-permute-start.33) | collective-permute-done | bytes 8224 | tf_op jit(solution)/shard_map/ppermute | solution.py:389
  372.0 4.5 collective-permute-start.41
  378.0 4.6 concatenate.3
  387.2 35.6 %collective-permute-done.37 = bf16[512,1024]{1,0:T(8,128)(2,1)} collective-permute-done((bf16[512,1024]{1,0:T(8,128)(2,1)}, bf16[512,1024]{1,0:T(8,128)(2,1)}, u32[]{:S(2)}, u32[]{:S(2)}) %collective-permute-start.37) | collective-permute-done | bytes 1048608 | tf_op jit(solution)/shard_map/ppermute | solution.py:389
  423.5 3.4 multiply_reduce_fusion
  426.9 33.3 %collective-permute-done.15 = bf16[512,1024]{1,0:T(8,128)(2,1)S(1)} collective-permute-done((bf16[512,1024]{1,0:T(8,128)(2,1)}, bf16[512,1024]{1,0:T(8,128)(2,1)S(1)}, u32[]{:S(2)}, u32[]{:S(2)}) %collective-permute-start.15) | collective-permute-done | bytes 1048608 | tf_op jit(solution)/shard_map/ppermute | solution.py:389
  460.2 5.6 collective-permute-done.27
  465.8 3.7 multiply_add_fusion
  470.8 13.7 %attend_back.1 = (f32[1024,512]{1,0:T(8,128)S(1)}, bf16[2048,512]{1,0:T(8,128)(2,1)}, bf16[2048,512]{1,0:T(8,128)(2,1)}) custom-call(s32[1]{0:T(128)} %bitcast.1.own_ref, bf16[1024,512]{1,0:T(8,128)(2,1)S(1)} %bitcast.217, bf16[2048,512]{1,0:T(8,128)(2,1)} %all-gather.3.cloned.1.call-done.k_ref, bf16[2048,512]{1,0:T(8,128)(2,1)} %all-gather.5.cloned.1.call-done.v_ref, ...), custom_call_target="tpu_custom_call" | custom-call | tf_op jit(solution)/shard_map/attend_back/pallas_call | solution.py:209
  493.9 79.9 %reduce-scatter.3.cloned.1.call-done = bf16[512,512]{1,0:T(8,128)(2,1)} async-done(((bf16[2048,512]{1,0:T(8,128)(2,1)}), bf16[512,512]{1,0:T(8,128)(2,1)}) %reduce-scatter.3.cloned.1.call-update) | async-done | bytes 524304 | tf_op jit(solution)/shard_map/reduce_scatter | solution.py:537
  582.7 30.1 %reduce-scatter.5.cloned.1.call-done = bf16[512,512]{1,0:T(8,128)(2,1)} async-done(((bf16[2048,512]{1,0:T(8,128)(2,1)}), bf16[512,512]{1,0:T(8,128)(2,1)}) %reduce-scatter.5.cloned.1.call-update) | async-done | bytes 524304 | tf_op jit(solution)/shard_map/reduce_scatter | solution.py:537
  623.3 41.0 %all-reduce = (bf16[1024]{0:T(1024)(128)(2,1)S(1)}, bf16[1024]{0:T(1024)(128)(2,1)S(1)}) all-reduce(bf16[1024]{0:T(1024)(128)(2,1)S(1)} %get-tuple-element.50, bf16[1024]{0:T(1024)(128)(2,1)S(1)} %get-tuple-element.48), channel_id=1, replica_groups=mesh['ctx'=4,'exp'=8] {'ctx','exp'}, use_global_device_ids=true, to_apply=%region_11.12 | all-reduce | flops 2048 | bytes 8192 | tf_op jit(solution)/shard_map/psum | solution.py:557
  665.5 3.7 fusion.12
  669.2 111.5 %all-reduce.6.cloned.1.call-done = (bf16[1024,1024]{1,0:T(8,128)(2,1)}, bf16[1024,512]{1,0:T(8,128)(2,1)}, bf16[1024,512]{1,0:T(8,128)(2,1)}, bf16[1024,1024]{1,0:T(8,128)(2,1)}, bf16[1024,32]{0,1:T(8,128)(2,1)}) async-done(((bf16[1024,1024]{1,0:T(8,128)(2,1)}, bf16[1024,512]{1,0:T(8,128)(2,1)}, bf16[1024,512]{1,0:T(8,128)(2,1)}, bf16[1024,1024]{1,0:T(8,128)(2,1)}, bf16[1024,32]{0,1:T(8,128)(2,1)}), ...) | async-done | bytes 6357008 | tf_op jit(solution)/shard_map/psum | solution.py:557
  780.7 4.2 convert_element_type.386
  791.3 234.0 %all-reduce.8.cloned.1.call-done = (bf16[4,1024,512]{2,1,0:T(8,128)(2,1)}, bf16[4,1024,512]{2,1,0:T(8,128)(2,1)}, bf16[4,512,1024]{2,1,0:T(8,128)(2,1)}) async-done(((bf16[4,1024,512]{2,1,0:T(8,128)(2,1)}, bf16[4,1024,512]{2,1,0:T(8,128)(2,1)}, bf16[4,512,1024]{2,1,0:T(8,128)(2,1)}), (bf16[4,1024,512]{2,1,0:T(8,128)(2,1)}, bf16[4,1024,512]{2,1,0:T(8,128)(2,1)}, ...) | async-done | bytes 12582928 | tf_op jit(solution)/shard_map/psum | solution.py:525
  1025.3 6.9 convert_element_type.397
  1032.2 4.6 convert_element_type.398
  1036.8 4.4 convert_element_type.399
  (273 shorter events, 124.3 us)
Async XLA Ops:
  7.2 65.6 %all-gather.3.cloned.1.call-start = ((), (), s32[]{:S(2)}) async-start(), calls=%async_computation.2 | async-start | bytes 2621440 | tf_op jit(solution)/shard_map/all_gather | solution.py:478
  14.8 75.9 %all-gather.5.cloned.1.call-start = ((), (), s32[]{:S(2)}) async-start(), calls=%async_computation.3 | async-start | bytes 2621440 | tf_op jit(solution)/shard_map/all_gather | solution.py:479
  17.6 556.2 %reduce-scatter.3.cloned.1.call-start = ((), (), s32[]{:S(2)}) async-start(), calls=%async_computation.4 | async-start | bytes 2621440 | tf_op jit(solution)/shard_map/reduce_scatter | solution.py:537
  23.6 83.2 %collective-permute-start.4 = (bf16[512,1024]{1,0:T(8,128)(2,1)}, bf16[512,1024]{1,0:T(8,128)(2,1)}, u32[]{:S(2)}, u32[]{:S(2)}) collective-permute-start(bf16[512,1024]{1,0:T(8,128)(2,1)} %bitcast.14), channel_id=1, source_target_pairs={{0,2},{1,3},{2,0},{3,1},{4,6},{5,7},{6,4},{7,5},{8,10},{9,11},{10,... | collective-permute-start | bytes 3145736 | tf_op jit(solution)/shard_map/ppermute | solution.py:389
  24.0 48.7 %collective-permute-start.20 = (bf16[512,1024]{1,0:T(8,128)(2,1)}, bf16[512,1024]{1,0:T(8,128)(2,1)}, u32[]{:S(2)}, u32[]{:S(2)}) collective-permute-start(bf16[512,1024]{1,0:T(8,128)(2,1)} %bitcast.14), channel_id=1, source_target_pairs={{0,4},{1,5},{2,6},{3,7},{4,0},{5,1},{6,2},{7,3},{8,12},{9,13},{10,... | collective-permute-start | bytes 3145736 | tf_op jit(solution)/shard_map/ppermute | solution.py:389
  35.0 78.5 %collective-permute-start.3 = (bf16[512,1024]{1,0:T(8,128)(2,1)}, bf16[512,1024]{1,0:T(8,128)(2,1)}, u32[]{:S(2)}, u32[]{:S(2)}) collective-permute-start(bf16[512,1024]{1,0:T(8,128)(2,1)} %bitcast.14), channel_id=1, source_target_pairs={{0,1},{1,0},{2,3},{3,2},{4,5},{5,4},{6,7},{7,6},{8,9},{9,8},{10,11... | collective-permute-start | bytes 3145736 | tf_op jit(solution)/shard_map/ppermute | solution.py:389
  36.7 65.8 %collective-permute-start.10 = (s32[512,8]{0,1:T(8,128)S(1)}, s32[512,8]{0,1:T(8,128)S(1)}, u32[]{:S(2)}, u32[]{:S(2)}) collective-permute-start(s32[512,8]{0,1:T(8,128)S(1)} %collective-permute-done.9), channel_id=1, source_target_pairs={{0,1},{1,0},{2,3},{3,2},{4,5},{5,4},{6,7},{7,6},{8,9},{9,8},{10,11... | collective-permute-start | bytes 49160 | tf_op jit(solution)/shard_map/ppermute | solution.py:389
  37.3 68.2 %collective-permute-start.11 = (s32[512,8]{0,1:T(8,128)S(1)}, s32[512,8]{0,1:T(8,128)S(1)}, u32[]{:S(2)}, u32[]{:S(2)}) collective-permute-start(s32[512,8]{0,1:T(8,128)S(1)} %collective-permute-done.9), channel_id=1, source_target_pairs={{0,2},{1,3},{2,0},{3,1},{4,6},{5,7},{6,4},{7,5},{8,10},{9,11},{10,... | collective-permute-start | bytes 49160 | tf_op jit(solution)/shard_map/ppermute | solution.py:389
  72.7 40.9 %collective-permute-start.22 = (bf16[512,1024]{1,0:T(8,128)(2,1)}, bf16[512,1024]{1,0:T(8,128)(2,1)}, u32[]{:S(2)}, u32[]{:S(2)}) collective-permute-start(bf16[512,1024]{1,0:T(8,128)(2,1)} %collective-permute-done.20), channel_id=1, source_target_pairs={{0,2},{1,3},{2,0},{3,1},{4,6},{5,7},{6,4},{7,5},{8,10},{9,11},{10,... | collective-permute-start | bytes 3145736 | tf_op jit(solution)/shard_map/ppermute | solution.py:389
  102.5 48.7 %collective-permute-start.16 = (bf16[512,1024]{1,0:T(8,128)(2,1)}, bf16[512,1024]{1,0:T(8,128)(2,1)}, u32[]{:S(2)}, u32[]{:S(2)}) collective-permute-start(bf16[512,1024]{1,0:T(8,128)(2,1)} %multiply_convert_fusion), channel_id=1, source_target_pairs={{0,4},{1,5},{2,6},{3,7},{4,0},{5,1},{6,2},{7,3},{8,12},{9,13},{10,... | collective-permute-start | bytes 3145736 | tf_op jit(solution)/shard_map/ppermute | solution.py:389
  106.7 46.8 %collective-permute-start.5 = (bf16[512,1024]{1,0:T(8,128)(2,1)}, bf16[512,1024]{1,0:T(8,128)(2,1)}, u32[]{:S(2)}, u32[]{:S(2)}) collective-permute-start(bf16[512,1024]{1,0:T(8,128)(2,1)} %collective-permute-done.4), channel_id=1, source_target_pairs={{0,1},{1,0},{2,3},{3,2},{4,5},{5,4},{6,7},{7,6},{8,9},{9,8},{10,11... | collective-permute-start | bytes 3145736 | tf_op jit(solution)/shard_map/ppermute | solution.py:389
  107.2 47.8 %collective-permute-start.1 = (bf16[512,1024]{1,0:T(8,128)(2,1)}, bf16[512,1024]{1,0:T(8,128)(2,1)}, u32[]{:S(2)}, u32[]{:S(2)}) collective-permute-start(bf16[512,1024]{1,0:T(8,128)(2,1)} %multiply_convert_fusion), channel_id=1, source_target_pairs={{0,2},{1,3},{2,0},{3,1},{4,6},{5,7},{6,4},{7,5},{8,10},{9,11},{10,... | collective-permute-start | bytes 3145736 | tf_op jit(solution)/shard_map/ppermute | solution.py:389
  113.5 45.3 %collective-permute-start.21 = (bf16[512,1024]{1,0:T(8,128)(2,1)}, bf16[512,1024]{1,0:T(8,128)(2,1)S(1)}, u32[]{:S(2)}, u32[]{:S(2)}) collective-permute-start(bf16[512,1024]{1,0:T(8,128)(2,1)} %collective-permute-done.20), channel_id=1, source_target_pairs={{0,1},{1,0},{2,3},{3,2},{4,5},{5,4},{6,7},{7,6},{8,9},{9,8},{10,11... | collective-permute-start | bytes 3145736 | tf_op jit(solution)/shard_map/ppermute | solution.py:389
  113.6 63.0 %collective-permute-start.23 = (bf16[512,1024]{1,0:T(8,128)(2,1)}, bf16[512,1024]{1,0:T(8,128)(2,1)S(1)}, u32[]{:S(2)}, u32[]{:S(2)}) collective-permute-start(bf16[512,1024]{1,0:T(8,128)(2,1)} %collective-permute-done.22), channel_id=1, source_target_pairs={{0,1},{1,0},{2,3},{3,2},{4,5},{5,4},{6,7},{7,6},{8,9},{9,8},{10,11... | collective-permute-start | bytes 3145736 | tf_op jit(solution)/shard_map/ppermute | solution.py:389
  151.2 25.4 %collective-permute-start.18 = (bf16[512,1024]{1,0:T(8,128)(2,1)}, bf16[512,1024]{1,0:T(8,128)(2,1)}, u32[]{:S(2)}, u32[]{:S(2)}) collective-permute-start(bf16[512,1024]{1,0:T(8,128)(2,1)} %collective-permute-done.16), channel_id=1, source_target_pairs={{0,2},{1,3},{2,0},{3,1},{4,6},{5,7},{6,4},{7,5},{8,10},{9,11},{10,... | collective-permute-start | bytes 3145736 | tf_op jit(solution)/shard_map/ppermute | solution.py:389
  153.6 26.9 %collective-permute-start = (bf16[512,1024]{1,0:T(8,128)(2,1)}, bf16[512,1024]{1,0:T(8,128)(2,1)S(1)}, u32[]{:S(2)}, u32[]{:S(2)}) collective-permute-start(bf16[512,1024]{1,0:T(8,128)(2,1)} %multiply_convert_fusion), channel_id=1, source_target_pairs={{0,1},{1,0},{2,3},{3,2},{4,5},{5,4},{6,7},{7,6},{8,9},{9,8},{10,11... | collective-permute-start | bytes 3145736 | tf_op jit(solution)/shard_map/ppermute | solution.py:389
  155.0 25.4 %collective-permute-start.2 = (bf16[512,1024]{1,0:T(8,128)(2,1)}, bf16[512,1024]{1,0:T(8,128)(2,1)S(1)}, u32[]{:S(2)}, u32[]{:S(2)}) collective-permute-start(bf16[512,1024]{1,0:T(8,128)(2,1)} %collective-permute-done.1), channel_id=1, source_target_pairs={{0,1},{1,0},{2,3},{3,2},{4,5},{5,4},{6,7},{7,6},{8,9},{9,8},{10,11... | collective-permute-start | bytes 3145736 | tf_op jit(solution)/shard_map/ppermute | solution.py:389
  158.8 84.1 %collective-permute-start.17 = (bf16[512,1024]{1,0:T(8,128)(2,1)}, bf16[512,1024]{1,0:T(8,128)(2,1)}, u32[]{:S(2)}, u32[]{:S(2)}) collective-permute-start(bf16[512,1024]{1,0:T(8,128)(2,1)} %collective-permute-done.16), channel_id=1, source_target_pairs={{0,1},{1,0},{2,3},{3,2},{4,5},{5,4},{6,7},{7,6},{8,9},{9,8},{10,11... | collective-permute-start | bytes 3145736 | tf_op jit(solution)/shard_map/ppermute | solution.py:389
  176.6 66.3 %collective-permute-start.19 = (bf16[512,1024]{1,0:T(8,128)(2,1)}, bf16[512,1024]{1,0:T(8,128)(2,1)}, u32[]{:S(2)}, u32[]{:S(2)}) collective-permute-start(bf16[512,1024]{1,0:T(8,128)(2,1)} %collective-permute-done.18), channel_id=1, source_target_pairs={{0,1},{1,0},{2,3},{3,2},{4,5},{5,4},{6,7},{7,6},{8,9},{9,8},{10,11... | collective-permute-start | bytes 3145736 | tf_op jit(solution)/shard_map/ppermute | solution.py:389
  320.5 30.1 %collective-permute-start.38 = (bf16[512,1024]{1,0:T(8,128)(2,1)S(1)}, bf16[512,1024]{1,0:T(8,128)(2,1)S(1)}, u32[]{:S(2)}, u32[]{:S(2)}) collective-permute-start(bf16[512,1024]{1,0:T(8,128)(2,1)S(1)} %get-tuple-element.65), channel_id=1, source_target_pairs={{0,1},{1,0},{2,3},{3,2},{4,5},{5,4},{6,7},{7,6},{8,9},{9,8},{10,11... | collective-permute-start | bytes 3145736 | tf_op jit(solution)/shard_map/ppermute | solution.py:389
  320.5 30.7 %collective-permute-start.40 = (bf16[512,1024]{1,0:T(8,128)(2,1)S(1)}, bf16[512,1024]{1,0:T(8,128)(2,1)S(1)}, u32[]{:S(2)}, u32[]{:S(2)}) collective-permute-start(bf16[512,1024]{1,0:T(8,128)(2,1)S(1)} %fusion.17), channel_id=1, source_target_pairs={{0,2},{1,3},{2,0},{3,1},{4,6},{5,7},{6,4},{7,5},{8,10},{9,11},{10,... | collective-permute-start | bytes 3145736 | tf_op jit(solution)/shard_map/ppermute | solution.py:389
  328.2 55.2 %collective-permute-start.24 = (bf16[512,1024]{1,0:T(8,128)(2,1)}, bf16[512,1024]{1,0:T(8,128)(2,1)}, u32[]{:S(2)}, u32[]{:S(2)}) collective-permute-start(bf16[512,1024]{1,0:T(8,128)(2,1)} %get-tuple-element.69), channel_id=1, source_target_pairs={{0,1},{1,0},{2,3},{3,2},{4,5},{5,4},{6,7},{7,6},{8,9},{9,8},{10,11... | collective-permute-start | bytes 3145736 | tf_op jit(solution)/shard_map/ppermute | solution.py:389
  344.8 38.7 %collective-permute-start.26 = (bf16[512,1024]{1,0:T(8,128)(2,1)}, bf16[512,1024]{1,0:T(8,128)(2,1)}, u32[]{:S(2)}, u32[]{:S(2)}) collective-permute-start(bf16[512,1024]{1,0:T(8,128)(2,1)} %fusion.21), channel_id=1, source_target_pairs={{0,2},{1,3},{2,0},{3,1},{4,6},{5,7},{6,4},{7,5},{8,10},{9,11},{10,... | collective-permute-start | bytes 3145736 | tf_op jit(solution)/shard_map/ppermute | solution.py:389
  350.5 35.7 %collective-permute-start.35 = (bf16[512,1024]{1,0:T(8,128)(2,1)}, bf16[512,1024]{1,0:T(8,128)(2,1)}, u32[]{:S(2)}, u32[]{:S(2)}) collective-permute-start(bf16[512,1024]{1,0:T(8,128)(2,1)} %get-tuple-element.63), channel_id=1, source_target_pairs={{0,1},{1,0},{2,3},{3,2},{4,5},{5,4},{6,7},{7,6},{8,9},{9,8},{10,11... | collective-permute-start | bytes 3145736 | tf_op jit(solution)/shard_map/ppermute | solution.py:389
  372.0 50.9 %collective-permute-start.37 = (bf16[512,1024]{1,0:T(8,128)(2,1)}, bf16[512,1024]{1,0:T(8,128)(2,1)}, u32[]{:S(2)}, u32[]{:S(2)}) collective-permute-start(bf16[512,1024]{1,0:T(8,128)(2,1)} %fusion.19), channel_id=1, source_target_pairs={{0,2},{1,3},{2,0},{3,1},{4,6},{5,7},{6,4},{7,5},{8,10},{9,11},{10,... | collective-permute-start | bytes 3145736 | tf_op jit(solution)/shard_map/ppermute | solution.py:389
  372.0 51.5 %collective-permute-start.41 = (bf16[512,1024]{1,0:T(8,128)(2,1)}, bf16[512,1024]{1,0:T(8,128)(2,1)}, u32[]{:S(2)}, u32[]{:S(2)}) collective-permute-start(bf16[512,1024]{1,0:T(8,128)(2,1)} %add_convert_fusion.1), channel_id=1, source_target_pairs={{0,4},{1,5},{2,6},{3,7},{4,0},{5,1},{6,2},{7,3},{8,12},{9,13},{10,... | collective-permute-start | bytes 3145736 | tf_op jit(solution)/shard_map/ppermute | solution.py:389
  383.5 43.4 %collective-permute-start.13 = (bf16[512,1024]{1,0:T(8,128)(2,1)}, bf16[512,1024]{1,0:T(8,128)(2,1)S(1)}, u32[]{:S(2)}, u32[]{:S(2)}) collective-permute-start(bf16[512,1024]{1,0:T(8,128)(2,1)} %get-tuple-element.67), channel_id=1, source_target_pairs={{0,1},{1,0},{2,3},{3,2},{4,5},{5,4},{6,7},{7,6},{8,9},{9,8},{10,11... | collective-permute-start | bytes 3145736 | tf_op jit(solution)/shard_map/ppermute | solution.py:389
  383.6 76.6 %collective-permute-start.15 = (bf16[512,1024]{1,0:T(8,128)(2,1)}, bf16[512,1024]{1,0:T(8,128)(2,1)S(1)}, u32[]{:S(2)}, u32[]{:S(2)}) collective-permute-start(bf16[512,1024]{1,0:T(8,128)(2,1)} %fusion.23), channel_id=1, source_target_pairs={{0,2},{1,3},{2,0},{3,1},{4,6},{5,7},{6,4},{7,5},{8,10},{9,11},{10,... | collective-permute-start | bytes 3145736 | tf_op jit(solution)/shard_map/ppermute | solution.py:389
  386.2 79.6 %collective-permute-start.27 = (bf16[512,1024]{1,0:T(8,128)(2,1)S(1)}, bf16[512,1024]{1,0:T(8,128)(2,1)S(1)}, u32[]{:S(2)}, u32[]{:S(2)}) collective-permute-start(bf16[512,1024]{1,0:T(8,128)(2,1)S(1)} %add_convert_fusion.5), channel_id=1, source_target_pairs={{0,4},{1,5},{2,6},{3,7},{4,0},{5,1},{6,2},{7,3},{8,12},{9,13},{10,... | collective-permute-start | bytes 3145736 | tf_op jit(solution)/shard_map/ppermute | solution.py:389
  484.5 128.2 %reduce-scatter.5.cloned.1.call-start = ((), (), s32[]{:S(2)}) async-start(), calls=%async_computation.5 | async-start | bytes 2621440 | tf_op jit(solution)/shard_map/reduce_scatter | solution.py:537
  485.1 295.6 %all-reduce.6.cloned.1.call-start = ((), (), s32[]{:S(2)}) async-start(), calls=%async_computation.6 | async-start | bytes 12713984 | tf_op jit(solution)/shard_map/psum | solution.py:557
  615.6 409.7 %all-reduce.8.cloned.1.call-start = ((), (), s32[]{:S(2)}) async-start(), calls=%async_computation.7 | async-start | bytes 25165824 | tf_op jit(solution)/shard_map/psum | solution.py:525
  (68 other events, 627.5 us)
Sparse Core Ops, SparseCore 0:
  14.9 38.0 all-gather.2
  55.3 35.2 all-gather.4
  484.6 89.1 reduce-scatter.2
  577.5 35.1 reduce-scatter.4
  620.1 160.4 all-reduce.5
  784.4 240.8 all-reduce.7

commit v2 on v1

v2 whole, which is shorter than its diff:
```python
import functools

import jax
import jax.numpy as jnp
from jax import lax
from jax.experimental import pallas as pl
from jax.experimental.pallas import tpu as pltpu
from jax.sharding import PartitionSpec as P

HEAD_DIM = 64
CAP = 192


SCALE = 0.015625
THETA = 10000.0
EPSILON = 1e-06
NEG = -1e30

F32 = jnp.float32
BF16 = jnp.bfloat16
NN = (((1,), (0,)), ((), ()))
NT = (((1,), (1,)), ((), ()))
TN = (((0,), (0,)), ((), ()))


def mm(left, right, dims=NN):
    return lax.dot_general(left, right, dims, preferred_element_type=F32)


def normalize(values):
    factor = lax.rsqrt(jnp.mean(values * values, axis=-1, keepdims=True) + EPSILON)
    return (values * factor, factor)


def norm_back(grad_scaled, scaled, factor):
    return factor * (grad_scaled - scaled * jnp.mean(grad_scaled * scaled, axis=-1, keepdims=True))


def rotate_columns(values, cosine, sine, direction):
    half = HEAD_DIM // 2
    split = values.reshape(-1, 2, half, values.shape[-1])
    first, second = split[:, 0], split[:, 1]
    turned = direction * sine
    return jnp.stack(
        [first * cosine - second * turned, second * cosine + first * turned], axis=1
    ).reshape(values.shape)


def head_columns(block, which):
    low = 2 * HEAD_DIM * which
    pair = jnp.concatenate(
        [block[low : low + HEAD_DIM], block[low + HEAD_DIM : low + 2 * HEAD_DIM]], axis=1
    )
    empty = jnp.zeros_like(pair)
    return jnp.concatenate([pair, empty] if which == 0 else [empty, pair], axis=0)


def causal(rows):
    keys = lax.broadcasted_iota(jnp.int32, (rows, rows), 0)
    places = lax.broadcasted_iota(jnp.int32, (rows, rows), 1)
    one = keys <= places
    return jnp.concatenate([one, one], axis=1)


def attend_kernel(peers, own_ref, q_ref, *refs):
    k_refs, v_refs = refs[:peers], refs[peers : 2 * peers]
    wide_ref, low_ref, log_ref, running_ref, mass_ref, total_ref = refs[2 * peers :]
    rows = q_ref.shape[1]
    own = own_ref[0]
    columns = [head_columns(q_ref[...], which) for which in range(2)]

    def visit(m):
        keys = k_refs[m][...]
        values = v_refs[m][...].T
        for which in range(2):
            scores = mm(keys, columns[which])
            if m == 0:
                scores = jnp.where(causal(rows), scores, NEG)
            newest = jnp.max(scores, axis=0, keepdims=True)
            if m > 0:
                newest = jnp.maximum(running_ref[which], newest)
            weights = jnp.exp(scores - newest)
            mass = jnp.sum(weights, axis=0, keepdims=True)
            mine = values[which * HEAD_DIM : (which + 1) * HEAD_DIM]
            total = mm(mine, weights.astype(BF16))
            if m > 0:
                rescale = jnp.exp(running_ref[which] - newest)
                mass = mass + mass_ref[which] * rescale
                total = total + total_ref[which] * rescale
            running_ref[which] = newest
            mass_ref[which] = mass
            total_ref[which] = total

    visit(0)
    for m in range(1, peers):
        pl.when((own ^ m) < own)(functools.partial(visit, m))
    for which in range(2):
        result = total_ref[which] / mass_ref[which]
        logs = running_ref[which] + jnp.log(mass_ref[which])
        for group in range(2):
            head = 2 * which + group
            part = slice(group * rows, (group + 1) * rows)
            wide_ref[head * HEAD_DIM : (head + 1) * HEAD_DIM, :] = result[:, part]
            log_ref[0, head : head + 1, :] = logs[:, part]
    low_ref[...] = wide_ref[...].T.astype(BF16)


def attend_back_kernel(peers, own_ref, q_ref, grad_ref, wide_ref, log_ref, cos_ref, sin_ref, *refs):
    k_refs, v_refs = refs[:peers], refs[peers : 2 * peers]
    dq_ref = refs[2 * peers]
    dk_refs = refs[2 * peers + 1 : 3 * peers + 1]
    dv_refs = refs[3 * peers + 1 : 4 * peers + 1]
    sum_ref = refs[4 * peers + 1]
    rows = q_ref.shape[1]
    own = own_ref[0]
    columns = [head_columns(q_ref[...], which) for which in range(2)]
    grads = [head_columns(grad_ref[...], which) for which in range(2)]
    offsets, logs = [], []
    for which in range(2):
        pieces = []
        for group in range(2):
            part = slice((2 * which + group) * HEAD_DIM, (2 * which + group + 1) * HEAD_DIM)
            pieces.append(
                jnp.sum(grad_ref[part, :].astype(F32) * wide_ref[part, :], axis=0, keepdims=True)
            )
        offsets.append(jnp.concatenate(pieces, axis=1))
        low = 2 * which
        logs.append(
            jnp.concatenate([log_ref[0, low : low + 1, :], log_ref[0, low + 1 : low + 2, :]], axis=1)
        )

    def visit(m):
        keys = k_refs[m][...]
        values = v_refs[m][...]
        turned = keys.T
        key_sum, value_sum = None, None
        for which in range(2):
            soft = jnp.exp(mm(keys, columns[which]) - logs[which])
            if m == 0:
                soft = jnp.where(causal(rows), soft, 0.0)
            prob_grad = mm(values, grads[which])
            score_grad = (soft * (prob_grad - offsets[which])).astype(BF16)
            value_part = mm(soft.astype(BF16), grads[which], NT)
            key_part = mm(score_grad, columns[which], NT)
            key_sum = key_part if key_sum is None else key_sum + key_part
            value_sum = value_part if value_sum is None else value_sum + value_part
            mine = slice(which * HEAD_DIM, (which + 1) * HEAD_DIM)
            part = mm(turned[mine], score_grad)
            sum_ref[mine, :] = part if m == 0 else sum_ref[mine, :] + part
        lanes = lax.broadcasted_iota(jnp.int32, key_sum.shape, 1) % HEAD_DIM
        ahead = pltpu.roll(key_sum, 3 * HEAD_DIM // 2, 1)
        behind = pltpu.roll(key_sum, HEAD_DIM // 2, 1)
        turned = jnp.where(lanes < HEAD_DIM // 2, -ahead, behind)
        dk_refs[m][...] = (key_sum * cos_ref[m] - turned * sin_ref[m]).astype(BF16)
        dv_refs[m][...] = value_sum.astype(BF16)

    def clear(m):
        dk_refs[m][...] = jnp.zeros_like(dk_refs[m])
        dv_refs[m][...] = jnp.zeros_like(dv_refs[m])

    visit(0)
    for m in range(1, peers):
        pl.when((own ^ m) < own)(functools.partial(visit, m))
        pl.when((own ^ m) > own)(functools.partial(clear, m))
    for which in range(2):
        mine = slice(which * HEAD_DIM, (which + 1) * HEAD_DIM)
        for group in range(2):
            head = 2 * which + group
            dq_ref[head * HEAD_DIM : (head + 1) * HEAD_DIM, :] = (
                sum_ref[mine, group * rows : (group + 1) * rows] * SCALE
            )


def attend(own, queries, keys, values):
    width, rows = queries.shape
    kv_width = keys[0].shape[1]
    pairs = kv_width // (2 * HEAD_DIM)
    step = width // pairs
    heads = step // HEAD_DIM
    block = pl.BlockSpec((rows, 2 * HEAD_DIM), lambda p: (0, p))
    return pl.pallas_call(
        functools.partial(attend_kernel, len(keys)),
        grid=(pairs,),
        in_specs=[
            pl.BlockSpec(memory_space=pltpu.SMEM),
            pl.BlockSpec((step, rows), lambda p: (p, 0)),
            *([block] * (2 * len(keys))),
        ],
        out_specs=[
            pl.BlockSpec((step, rows), lambda p: (p, 0)),
            pl.BlockSpec((rows, step), lambda p: (0, p)),
            pl.BlockSpec((1, heads, rows), lambda p: (p, 0, 0)),
        ],
        out_shape=[
            jax.ShapeDtypeStruct((width, rows), F32),
            jax.ShapeDtypeStruct((rows, width), BF16),
            jax.ShapeDtypeStruct((pairs, heads, rows), F32),
        ],
        scratch_shapes=[
            pltpu.VMEM((2, 1, 2 * rows), F32),
            pltpu.VMEM((2, 1, 2 * rows), F32),
            pltpu.VMEM((2, HEAD_DIM, 2 * rows), F32),
        ],
        compiler_params=pltpu.CompilerParams(vmem_limit_bytes=48 * 1024 * 1024),
        cost_estimate=pl.CostEstimate(
            flops=2 * 2 * len(keys) * rows * rows * 4 * width,
            bytes_accessed=12 * rows * width,
            transcendentals=len(keys) * rows * rows * width // HEAD_DIM,
        ),
        name="attend",
    )(own, queries, *keys, *values)


def attend_back(own, queries, keys, values, grads, wide, logs, cosine, sine):
    width, rows = queries.shape
    kv_width = keys[0].shape[1]
    pairs = kv_width // (2 * HEAD_DIM)
    step = width // pairs
    heads = step // HEAD_DIM
    columns = pl.BlockSpec((step, rows), lambda p: (p, 0))
    table = pl.BlockSpec(cosine.shape, lambda p: (0, 0, 0))
    block = pl.BlockSpec((rows, 2 * HEAD_DIM), lambda p: (0, p))
    peers = len(keys)
    result = pl.pallas_call(
        functools.partial(attend_back_kernel, peers),
        grid=(pairs,),
        in_specs=[
            pl.BlockSpec(memory_space=pltpu.SMEM),
            columns,
            columns,
            columns,
            pl.BlockSpec((1, heads, rows), lambda p: (p, 0, 0)),
            table,
            table,
            *([block] * (2 * peers)),
        ],
        out_specs=[columns, *([block] * (2 * peers))],
        out_shape=[
            jax.ShapeDtypeStruct((width, rows), F32),
            *([jax.ShapeDtypeStruct((rows, kv_width), BF16)] * (2 * peers)),
        ],
        scratch_shapes=[pltpu.VMEM((2 * HEAD_DIM, 2 * rows), F32)],
        compiler_params=pltpu.CompilerParams(vmem_limit_bytes=48 * 1024 * 1024),
        cost_estimate=pl.CostEstimate(
            flops=5 * 2 * len(keys) * rows * rows * 4 * width,
            bytes_accessed=12 * rows * width,
            transcendentals=len(keys) * rows * rows * width // HEAD_DIM,
        ),
        name="attend_back",
    )(own, queries, grads, wide, logs, cosine, sine, *keys, *values)
    return result[0], result[1 : 1 + peers], result[1 + peers :]


def one_hot_rows(rank_row, rows):
    slots = lax.broadcasted_iota(jnp.int32, (rows, rank_row.shape[1]), 0)
    return slots == rank_row


def places(rank_ref, block, owned):
    return jnp.concatenate(
        [
            one_hot_rows(rank_ref[block, e : e + 1, :], CAP).astype(F32).astype(BF16)
            for e in range(owned)
        ],
        axis=0,
    )


def gather_rows(block, place, x, c, rank_ref, mask_ref, router_ref, rows_x, rows_c, rows_w):
    owned = rows_x.shape[0]
    at = slice(block * CAP, (block + 1) * CAP)
    select = places(rank_ref, place, owned)
    picked = mm(select, x).astype(BF16)
    upstream = mm(select, c).astype(BF16)
    logits = mm(picked, router_ref[...])
    named = mm(select, mask_ref[place], NT) > 0.5
    masked = jnp.where(named, logits, NEG)
    grown = jnp.where(named, jnp.exp(masked - jnp.max(masked, axis=1, keepdims=True)), 0.0)
    mass = jnp.sum(grown, axis=1, keepdims=True)
    weights = grown / jnp.where(mass > 0.0, mass, 1.0)
    for e in range(owned):
        part = slice(e * CAP, (e + 1) * CAP)
        rows_x[e, at, :] = picked[part]
        rows_c[e, at, :] = upstream[part]
        rows_w[e, at, :] = weights[part, e : e + 1]


def scatter_rows(block, select, rows):
    at = slice(block * CAP, (block + 1) * CAP)
    return mm(
        select, jnp.concatenate([rows[e, at, :] for e in range(rows.shape[0])], axis=0), TN
    ).astype(BF16)


def front_kernel(blocks, start, owned, near, here_ref, *refs):
    x_refs, refs = refs[:blocks], refs[blocks:]
    c_refs, refs = refs[:blocks], refs[blocks:]
    rank_ref, mask_ref, router_ref, wide_ref, down_ref = refs[:5]
    dx_refs, refs = refs[5 : 5 + blocks], refs[5 + blocks :]
    out_x, out_c, out_back, out_hidden, rows_x, rows_c, rows_w, chosen_ref = refs
    step = pl.program_id(0)
    tokens = x_refs[0].shape[0]
    size = down_ref.shape[1]

    def place(block):
        return block if near else here_ref[0] ^ (start + block)

    @pl.when(step == 0)
    def enter():
        for block in range(blocks):
            gather_rows(
                block,
                place(block),
                x_refs[block][...],
                c_refs[block][...] if near else c_refs[block][0],
                rank_ref,
                mask_ref,
                router_ref,
                rows_x,
                rows_c,
                rows_w,
            )

    e = step
    x = rows_x[e]
    c = rows_c[e]
    weight = rows_w[e]
    out_x[0] = x
    out_c[0] = c
    both = mm(x, wide_ref[0])
    gate, up = both[:, :size], both[:, size:]
    back = mm(c, down_ref[0], NT)
    sigmoid = 1.0 / (1.0 + jnp.exp(-gate))
    activated = gate * sigmoid
    hidden = activated * up
    scored = jnp.sum(hidden * back, axis=1, keepdims=True)
    for block in range(blocks):
        part = scored[block * CAP : (block + 1) * CAP]
        chosen_ref[e, block : block + 1, :] = jnp.sum(
            jnp.where(one_hot_rows(rank_ref[place(block), pl.ds(e, 1), :], CAP), part, 0.0),
            axis=0,
            keepdims=True,
        )
    out_hidden[0] = (hidden * weight).astype(BF16)
    back = back * weight
    gate_back = (back * up * sigmoid * (1.0 + gate * (1.0 - sigmoid))).astype(BF16)
    up_back = (back * activated).astype(BF16)
    backs = jnp.concatenate([gate_back, up_back], axis=1)
    out_back[0] = backs
    rows_x[e] = mm(backs, wide_ref[0], NT).astype(BF16)

    @pl.when(step == owned - 1)
    def leave():
        for block in range(blocks):
            select = places(rank_ref, place(block), owned)
            dx_refs[block][:tokens, :] = scatter_rows(block, select, rows_x)
            experts = mask_ref.shape[1]
            lines = lax.broadcasted_iota(jnp.int32, (experts, tokens), 0) - here_ref[0] * owned
            high, low = 0.0, 0.0
            for expert in range(owned):
                value = chosen_ref[expert, block : block + 1, :]
                rounded = value.astype(BF16).astype(F32)
                high = high + jnp.where(lines == expert, rounded, 0.0)
                low = low + jnp.where(lines == expert, value - rounded, 0.0)
            dx_refs[block][tokens:, :tokens] = high.astype(BF16)
            dx_refs[block][tokens:, tokens : 2 * tokens] = low.astype(BF16)


def rear_kernel(blocks, start, owned, near, first, here_ref, *refs):
    x_ref, c_ref, back_ref, hidden_ref, rank_ref, down_ref = refs[:6]
    old_ref = None if first else refs[6]
    refs = refs[6:] if first else refs[7:]
    y_refs, refs = refs[:blocks], refs[blocks:]
    grad_ref, rows_y = refs
    step = pl.program_id(0)
    width = x_ref.shape[2]

    def place(block):
        return block if near else here_ref[0] ^ (start + block)

    hidden = hidden_ref[0]
    for lines, left, right in (
        (slice(0, width), x_ref[0], back_ref[0]),
        (slice(width, grad_ref.shape[1]), hidden, c_ref[0]),
    ):
        grad = mm(left, right, TN)
        if old_ref is not None:
            grad = grad + old_ref[0, lines, :].astype(F32)
        grad_ref[0, lines, :] = grad.astype(BF16)
    rows_y[step] = mm(hidden, down_ref[0]).astype(BF16)

    @pl.when(step == owned - 1)
    def leave():
        for block in range(blocks):
            y_refs[block][...] = scatter_rows(
                block, places(rank_ref, place(block), owned), rows_y
            )


def run_front(here, start, x, c, rank, mask, router, w_wide, w_down):
    blocks = len(x)
    tokens, width = x[0].shape
    owned, hidden, _ = w_down.shape
    near = isinstance(c, list)
    once = pl.Buffered(1)
    rows = blocks * CAP
    long = tokens + mask.shape[1]

    def fixed(*shape):
        return pl.BlockSpec(shape, lambda s, h: (0,) * len(shape), pipeline_mode=once)

    def block_of(m):
        return pl.BlockSpec(
            (1, tokens, width), lambda s, h: (h[0] ^ m, 0, 0), pipeline_mode=once
        )

    def expert(*shape):
        return pl.BlockSpec((1, *shape), lambda s, h: (s, 0, 0))

    def shape(*dims):
        return jax.ShapeDtypeStruct(dims, BF16)

    params = pltpu.CompilerParams(vmem_limit_bytes=60 * 1024 * 1024)
    one = fixed(tokens, width)
    result = pl.pallas_call(
        functools.partial(front_kernel, blocks, start, owned, near),
        grid_spec=pltpu.PrefetchScalarGridSpec(
            num_scalar_prefetch=1,
            grid=(owned,),
            in_specs=[
                *([one] * blocks),
                *([one] * blocks if near else [block_of(start + i) for i in range(blocks)]),
                fixed(*rank.shape),
                fixed(*mask.shape),
                fixed(*router.shape),
                expert(width, 2 * hidden),
                expert(hidden, width),
            ],
            out_specs=[
                *([fixed(long, width)] * blocks),
                expert(rows, width),
                expert(rows, width),
                expert(rows, 2 * hidden),
                expert(rows, hidden),
            ],
            scratch_shapes=[
                pltpu.VMEM((owned, rows, width), BF16),
                pltpu.VMEM((owned, rows, width), BF16),
                pltpu.VMEM((owned, rows, 1), F32),
                pltpu.VMEM((owned, blocks, tokens), F32),
            ],
        ),
        out_shape=[
            *([shape(long, width)] * blocks),
            shape(owned, rows, width),
            shape(owned, rows, width),
            shape(owned, rows, 2 * hidden),
            shape(owned, rows, hidden),
        ],
        compiler_params=params,
        cost_estimate=pl.CostEstimate(
            flops=2 * owned * rows * width * (5 * hidden + 3 * tokens),
            bytes_accessed=8 * owned * rows * width,
            transcendentals=owned * rows * hidden,
        ),
        name="experts_front",
    )(here, *x, *(c if near else [c] * blocks), rank, mask, router, w_wide, w_down)
    return result[:blocks], result[blocks:]


def run_rear(here, start, blocks, near, kept, rank, w_down, old):
    owned, hidden, width = w_down.shape
    tokens = rank.shape[2]
    rows = blocks * CAP
    first = old is None

    def fixed(*shape):
        return pl.BlockSpec(
            shape, lambda s, h: (0,) * len(shape), pipeline_mode=pl.Buffered(1)
        )

    def expert(*shape):
        return pl.BlockSpec((1, *shape), lambda s, h: (s, 0, 0))

    def shape(*dims):
        return jax.ShapeDtypeStruct(dims, BF16)

    grad_shape = (owned, width + hidden, width)
    *y, grad = pl.pallas_call(
        functools.partial(rear_kernel, blocks, start, owned, near, first),
        grid_spec=pltpu.PrefetchScalarGridSpec(
            num_scalar_prefetch=1,
            grid=(owned,),
            in_specs=[
                expert(rows, width),
                expert(rows, width),
                expert(rows, 2 * hidden),
                expert(rows, hidden),
                fixed(*rank.shape),
                expert(hidden, width),
                *([] if first else [expert(*grad_shape[1:])]),
            ],
            out_specs=[*([fixed(tokens, width)] * blocks), expert(*grad_shape[1:])],
            scratch_shapes=[pltpu.VMEM((owned, rows, width), BF16)],
        ),
        out_shape=[*([shape(tokens, width)] * blocks), shape(*grad_shape)],
        compiler_params=pltpu.CompilerParams(vmem_limit_bytes=60 * 1024 * 1024),
        cost_estimate=pl.CostEstimate(
            flops=2 * owned * rows * width * (4 * hidden + tokens),
            bytes_accessed=8 * owned * rows * width,
            transcendentals=0,
        ),
        name="experts_rear",
    )(here, *kept, rank, w_down, *([] if first else [old]))
    return y, grad


def swap(value, axis, bit):
    peers = lax.axis_size(axis)
    return lax.ppermute(value, axis, [(i, i ^ bit) for i in range(peers)])


def add_low(left, right):
    return (left.astype(F32) + right.astype(F32)).astype(BF16)


def gather_blocks(value, axis, bits):
    held = {0: value}
    for bit in bits:
        for m in list(held):
            held[m | bit] = swap(held[m], axis, bit)
    return [held[m] for m in range(len(held))]


def reduce_step(held, axis, bit):
    if not isinstance(held, dict):
        held = dict(enumerate(held))
    else:
        held = dict(held)
    for m in sorted(held, reverse=True):
        if m & bit:
            arrived = swap(held.pop(m), axis, bit)
            held[m ^ bit] = add_low(held[m ^ bit], arrived)
    return held


def reduce_blocks(held, axis, bits):
    for bit in bits:
        held = reduce_step(held, axis, bit)
    return held[0]


def bits_of(axis):
    peers = lax.axis_size(axis)
    return [1 << i for i in range(peers.bit_length() - 1)]


def side_of(axis, bit):
    return (lax.axis_index(axis) // bit) % 2


def begin_sum(grad):
    rows = grad.shape[1]
    half = rows // 4
    rails = []
    for rail, (first, second) in enumerate(((1, 2), (2, 1))):
        base = rail * (rows // 2)
        one = side_of("ctx", first)
        other = lax.dynamic_slice_in_dim(grad, base + (1 - one) * half, half, 1)
        mine = lax.dynamic_slice_in_dim(grad, base + one * half, half, 1)
        rails.append(add_low(mine, swap(other, "ctx", first)))
    return rails


def middle_sum(rails):
    held = []
    for mine, (first, second) in zip(rails, ((1, 2), (2, 1))):
        two = side_of("ctx", second)
        quarter = mine.shape[1] // 2
        other = lax.dynamic_slice_in_dim(mine, (1 - two) * quarter, quarter, 1)
        mine = lax.dynamic_slice_in_dim(mine, two * quarter, quarter, 1)
        held.append(add_low(mine, swap(other, "ctx", second)))
    return held


def end_sum(grad, held):
    rows = grad.shape[1]
    half, quarter = rows // 4, rows // 8
    result = grad
    for rail, (mine, (first, second)) in enumerate(zip(held, ((1, 2), (2, 1)))):
        base = rail * (rows // 2)
        one, two = side_of("ctx", first), side_of("ctx", second)
        across = swap(mine, "ctx", second)
        pieces = (
            (mine, one, two),
            (across, one, 1 - two),
            (swap(mine, "ctx", first), 1 - one, two),
            (swap(across, "ctx", first), 1 - one, 1 - two),
        )
        for piece, row, column in pieces:
            result = lax.dynamic_update_slice_in_dim(
                result, piece, base + row * half + column * quarter, 1
            )
    return result


def after(values, *others):
    return lax.optimization_barrier((values, others))[0]


def per_device(
    tokens,
    attn_gain,
    query_weight,
    key_weight,
    value_weight,
    output_weight,
    moe_gain,
    w_router,
    routes,
    w_gate,
    w_up,
    w_down,
    cotangent,
):
    tok_rows, model_width = tokens.shape[1:]
    experts = w_router.shape[1]
    owned = w_gate.shape[0]
    peers = lax.axis_size("exp")
    here = lax.axis_index("exp")
    own = lax.axis_index("ctx")
    exp_bits = bits_of("exp")
    ctx_bits = bits_of("ctx")
    positions = own * tok_rows + jnp.arange(tok_rows, dtype=jnp.int32)
    half = HEAD_DIM // 2
    inverse = THETA ** (-jnp.arange(half, dtype=F32) * 2.0 / HEAD_DIM)
    angles = inverse[:, None] * positions.astype(F32)[None, :]
    cosine, sine = jnp.cos(angles), jnp.sin(angles)

    layer_inputs = tokens[0].astype(F32)
    scaled_one, factor_one = normalize(layer_inputs)
    first_normalized = (scaled_one * attn_gain).astype(BF16)
    value_rows = mm(first_normalized, value_weight).astype(BF16)
    key_rows = (
        rotate_columns(
            jnp.einsum("de,td->et", key_weight, first_normalized, preferred_element_type=F32),
            cosine,
            sine,
            1.0,
        )
        .astype(BF16)
        .T
    )
    peer_at = jnp.arange(lax.axis_size("ctx"), dtype=jnp.int32) ^ own
    lane_angles = (
        (peer_at[:, None] * tok_rows + jnp.arange(tok_rows, dtype=jnp.int32)).astype(F32)[..., None]
        * inverse
    )
    lane_cosine = jnp.tile(jnp.cos(lane_angles), (1, 1, 4))
    lane_sine = jnp.tile(jnp.sin(lane_angles), (1, 1, 4))
    keys = gather_blocks(key_rows, "ctx", ctx_bits)
    values = gather_blocks(value_rows, "ctx", ctx_bits[::-1])
    routes_here = routes[0].T.astype(BF16)
    spare = jnp.zeros((16 - routes_here.shape[0], tok_rows), BF16)
    packed = jnp.concatenate([routes_here, spare])
    packed = jnp.concatenate([packed, jnp.zeros((16, model_width - tok_rows), BF16)], axis=1)
    all_cot = lax.all_gather(jnp.concatenate([cotangent[0], packed]), "exp", axis=0)
    all_routes = all_cot[:, tok_rows : tok_rows + routes_here.shape[0], :tok_rows]
    near_routes = jnp.stack([routes_here, swap(routes_here, "exp", 1)])
    near_cot = [cotangent[0], swap(cotangent[0], "exp", 1)]
    queries = (
        rotate_columns(
            jnp.einsum("de,td->et", query_weight, first_normalized, preferred_element_type=F32),
            cosine,
            sine,
            1.0,
        ).astype(BF16)
        * SCALE
    ).astype(BF16)
    own_index = jnp.full((1,), own, jnp.int32)
    queries, lane_cosine, lane_sine = lax.optimization_barrier((queries, lane_cosine, lane_sine))
    attended_wide, attended_low, logs = attend(own_index, queries, keys, values)
    normed_blocks = gather_blocks(after(first_normalized, keys[-1], values[-1]), "ctx", ctx_bits)
    residual_stream = layer_inputs + mm(attended_low, output_weight)
    scaled_two, factor_two = normalize(residual_stream)
    normed_two = (scaled_two * moe_gain).astype(BF16)

    order = jnp.arange(experts, dtype=jnp.int32)
    order = ((order // owned) ^ here) * owned + order % owned
    permutation = (jnp.arange(experts, dtype=jnp.int32)[:, None] == order[None, :]).astype(BF16)
    upto = jnp.triu(jnp.ones((tok_rows, tok_rows), BF16))

    def find(block_routes):
        named = jnp.any(
            block_routes.astype(jnp.int32)[:, :, None, :] == order[:, None], axis=1
        )
        mask = named.astype(BF16)
        rank = jnp.einsum("bes,st->bet", mask[:, :owned], upto, preferred_element_type=F32)
        return jnp.where(named[:, :owned], rank.astype(jnp.int32) - 1, -1), mask

    router = mm(w_router, permutation).astype(BF16)
    here_index = jnp.full((1,), here, jnp.int32)

    x_blocks = {0: normed_two}
    for bit in exp_bits[:0:-1]:
        x_blocks[bit] = swap(normed_two, "exp", bit)
    x_blocks[1] = swap(normed_two, "exp", 1)
    w_wide = jnp.concatenate([w_gate, w_up], axis=2)
    mixed, dx, pending, grads = [], [], [], [None]

    def finish_rear(behind):
        start, end, kept = pending.pop(0)
        y_part, grad = run_rear(
            here_index,
            start,
            end - start,
            start == 0,
            after(kept, behind),
            near_found[0] if start == 0 else found[0],
            w_down,
            grads[-1],
        )
        mixed.extend(y_part)
        grads.append(grad)

    near_found, found = find(near_routes), find(all_routes)
    ends = [2, 4] + list(range(8, peers + 1, 4))
    for start, end in zip([0] + ends, ends):
        if start == 2:
            for m in range(4, peers, 2):
                top = 1 << (m.bit_length() - 1)
                if m != top:
                    low = (m - top) & (top - m)
                    x_blocks[m] = swap(x_blocks[m - low], "exp", low)
            x_blocks[3] = swap(x_blocks[2], "exp", 1)
        elif start == 4:
            for m in range(5, peers, 2):
                x_blocks[m] = swap(x_blocks[m - 1], "exp", 1)
        near = start == 0
        dx_part, kept = run_front(
            here_index,
            start,
            [x_blocks[m] for m in range(start, end)],
            near_cot if near else all_cot,
            *(near_found if near else found),
            router,
            w_wide,
            w_down,
        )
        dx += dx_part
        pending.append((start, end, kept))
        if near:
            finish_rear(dx_part)
        if end in (2, 4):
            waiting = [m for m in x_blocks if m >= end]
            behind = mixed[0] if near else dx_part[0]
            x_blocks.update(zip(waiting, after([x_blocks[m] for m in waiting], behind)))
    held = reduce_step(dx, "exp", exp_bits[0])
    for index, bit in enumerate(exp_bits[1:]):
        moved = [m for m in sorted(held, reverse=True) if m & bit]
        arrived = [swap(held[m], "exp", bit) for m in moved]
        for _ in range(-(-len(pending) // (len(exp_bits) - 1 - index))):
            finish_rear(list(held.values()))
        arrived = after(arrived, grads[-1])
        for m, part in zip(moved, arrived):
            held[m ^ bit] = add_low(held[m ^ bit], part)
            del held[m]
    dx_sum = held[0].astype(F32)
    old = grads[-1]

    rails = begin_sum(old)
    gate_grad = dx_sum[tok_rows:, :tok_rows] + dx_sum[tok_rows:, tok_rows : 2 * tok_rows]
    named_here = jnp.any(routes[0].T[:, None, :] == jnp.arange(experts)[:, None], axis=0)
    logits = jnp.einsum("de,td->et", w_router, normed_two, preferred_element_type=F32)
    masked = jnp.where(named_here, logits, NEG)
    grown = jnp.where(named_here, jnp.exp(masked - jnp.max(masked, axis=0, keepdims=True)), 0.0)
    gate_weights = grown / jnp.sum(grown, axis=0, keepdims=True)
    chosen_grad = gate_weights * (
        gate_grad - jnp.sum(gate_weights * gate_grad, axis=0, keepdims=True)
    )
    logit_grad = chosen_grad.astype(BF16)
    router_grad = jnp.einsum("td,et->ed", normed_two, logit_grad, preferred_element_type=F32)

    upstream = cotangent[0].astype(F32)
    normed_two_grad = mm(logit_grad, w_router.T, TN) + dx_sum[:tok_rows]
    gain_two_grad = jnp.sum(normed_two_grad * scaled_two, axis=0)
    residual_grad = upstream + norm_back(normed_two_grad * moe_gain, scaled_two, factor_two)
    residual_low = residual_grad.astype(BF16)
    attended_grad = mm(output_weight, residual_low, NT).astype(BF16)
    attended_grad, normed_blocks = lax.optimization_barrier((attended_grad, normed_blocks))
    wout_grad = mm(attended_low, residual_low, TN)
    query_grad, key_parts, value_parts = attend_back(
        own_index,
        queries,
        keys,
        values,
        attended_grad,
        attended_wide,
        logs,
        lane_cosine,
        lane_sine,
    )
    wk_grad = sum(mm(rows, part, TN) for rows, part in zip(normed_blocks, key_parts))
    wv_grad = sum(mm(rows, part, TN) for rows, part in zip(normed_blocks, value_parts))
    key_back = reduce_blocks(key_parts, "ctx", ctx_bits)
    value_back = reduce_blocks(value_parts, "ctx", ctx_bits[::-1])
    query_back = rotate_columns(query_grad, cosine, sine, -1.0).astype(BF16)
    wq_grad = jnp.einsum("td,et->de", first_normalized, query_back, preferred_element_type=F32)
    normed_one_grad = (
        jnp.einsum("et,de->td", query_back, query_weight, preferred_element_type=F32)
        + mm(key_back, key_weight, NT)
        + mm(value_back, value_weight, NT)
    )
    input_grad = residual_grad + norm_back(normed_one_grad * attn_gain, scaled_one, factor_one)
    spare = jnp.zeros((63 - experts, model_width), F32)
    small = jnp.concatenate([router_grad, gain_two_grad[None], spare])
    sums = tuple(part.astype(BF16) for part in (wout_grad, wq_grad, wk_grad, wv_grad, small))
    rails, sums = lax.optimization_barrier((rails, sums))
    sums = lax.psum(sums, ("ctx", "exp"))
    rails = middle_sum(rails)
    expert_grads = end_sum(old, after(rails, key_back, value_back))
    wide, hidden = w_gate.shape[1:]
    wgate_grad = expert_grads[:, :wide, :hidden].astype(F32)
    wup_grad = expert_grads[:, :wide, hidden:].astype(F32)
    down_grad = expert_grads[:, wide:].astype(F32)
    mixed = reduce_blocks(after(mixed, residual_low), "exp", exp_bits)
    output = (residual_stream + mixed.astype(F32)).astype(BF16)
    input_grad, output, wgate_grad, wup_grad, down_grad, sums = lax.optimization_barrier(
        (input_grad, output, wgate_grad, wup_grad, down_grad, sums)
    )
    wout_grad, wq_grad, wk_grad, wv_grad, small = (part.astype(F32) for part in sums)
    router_grad, gain_two_grad = small[:experts].T, small[experts]
    gain_one_grad = (
        jnp.sum(wq_grad * query_weight.astype(F32), axis=1)
        + jnp.sum(wk_grad * key_weight.astype(F32), axis=1)
        + jnp.sum(wv_grad * value_weight.astype(F32), axis=1)
    ) / attn_gain
    return (
        output[None],
        input_grad[None],
        gain_one_grad,
        wq_grad,
        wk_grad,
        wv_grad,
        wout_grad,
        gain_two_grad,
        router_grad,
        wgate_grad,
        wup_grad,
        down_grad,
    )


def solution(mesh):
    return jax.shard_map(
        per_device,
        mesh=mesh,
        in_specs=(
            P("exp", "ctx", None),
            P(),
            P(),
            P(),
            P(),
            P(),
            P(),
            P(),
            P("exp", "ctx", None),
            P("exp", None, None),
            P("exp", None, None),
            P("exp", None, None),
            P("exp", "ctx", None),
        ),
        out_specs=(
            P("exp", "ctx", None),
            P("exp", "ctx", None),
            P(),
            P(),
            P(),
            P(),
            P(),
            P(),
            P(),
            P("exp", None, None),
            P("exp", None, None),
            P("exp", None, None),
        ),
        check_vma=False,
    )
```

time: 1050 us -> 748 us (0.71)
  waiting for transfers between devices: 673 us -> 289 us
  blocking collectives: 41 us -> 0 us
  starting transfers between devices: 36.4 us -> 74.9 us
  Pallas kernels: 141 us -> 178 us
  other arithmetic: 76.4 us -> 97.2 us
  local copies, waits for them, and re-layouts: 31.3 us -> 47.9 us
    psum x2 -> x1, waiting for transfers between devices: 345 us -> 54.7 us  [per_device(): sums = lax.psum(sums, ('ctx', 'exp'))]
    reduce_scatter x2 -> x0, waiting for transfers between devices: 110 us -> none  [per_device(): lax.psum_scatter(part, 'ctx', scatter_dimension=0, tiled=True).astype(F32)]
    convert_element_type x18 -> x30, other arithmetic: 37.7 us -> 79 us  [the longest x16 43.1 us: add_low(): return (left.astype(F32) + right.astype(F32)).astype(BF16)]
    psum x1 -> x0, blocking collectives: 41 us -> none  [per_device(): lax.psum(tuple((g.astype(BF16) for g in (wq_grad, wk_grad, wv_grad, gain_...]
    ppermute x42 -> x48, starting transfers between devices: 35.8 us -> 74.9 us  [swap(): return lax.ppermute(value, axis, [(i, i ^ bit) for i in range(peers)])]
    pallas_call x4 -> x8, Pallas kernels: 141 us -> 178 us  [the longest x3 89.6 us: run_front(): pl.pallas_call(functools.partial(front_kernel, blocks, start, owned, near...]
    ppermute x42 -> x48, waiting for transfers between devices: 198 us -> 235 us  [swap(): return lax.ppermute(value, axis, [(i, i ^ bit) for i in range(peers)])]
    dynamic_update_slice x0 -> x8, local copies, waits for them, and re-layouts: none -> 18.9 us  [end_sum(): lax.dynamic_update_slice_in_dim(result, piece, base + row * half + column...]
  transfers between devices with their start and end apart: 48 -> 50, of which waited for: 17 -> 17; matrix products, arithmetic and copies ran while one was open for 9% -> 22% of each run, Pallas kernels for 6% -> 24%
where the time goes in v2:
time: 748 us; the launch traced here: 743 us
  waiting for transfers between devices  289 us (39%)
  Pallas kernels  178 us (24%)
  other arithmetic  97.2 us (13%)
  starting transfers between devices  74.9 us (10%)
  local copies, waits for them, and re-layouts  47.9 us (6%)
  matrix products  40.3 us (5%)
  between operations  15.3 us (2%)
    ppermute x48, waiting for transfers between devices, swap(): return lax.ppermute(value, axis, [(i, i ^ bit) for i in range(peers)])  235 us
    pallas_call x3, Pallas kernels, run_front(): pl.pallas_call(functools.partial(front_kernel, blocks, start, owned, near...  89.6 us
    ppermute x48, starting transfers between devices, swap(): return lax.ppermute(value, axis, [(i, i ^ bit) for i in range(peers)])  74.9 us
    pallas_call x3, Pallas kernels, run_rear(): pl.pallas_call(functools.partial(rear_kernel, blocks, start, owned, near,...  64.6 us
    psum x1, waiting for transfers between devices, per_device(): sums = lax.psum(sums, ('ctx', 'exp'))  54.7 us
    convert_element_type x16, other arithmetic, add_low(): return (left.astype(F32) + right.astype(F32)).astype(BF16)  43.1 us
    dot_general x16, matrix products, mm(): return lax.dot_general(left, right, dims, preferred_element_type=F32)  29.1 us
    dynamic_update_slice x8, local copies, waits for them, and re-layouts, end_sum(): lax.dynamic_update_slice_in_dim(result, piece, base + row * half + column...  18.9 us
  transfers between devices with their start and end apart: 50, of which 17 were waited for; matrix products, arithmetic and copies ran while one was open for 22% of the time, Pallas kernels for 24%

profile of v2, /device:TPU:0, one launch (start us, length us, event | category | flops | bytes accessed | tf_op | source)
XLA Modules:
  0.0 743.2 jit_solution(1318255138421279524)
XLA Ops:
  32.3 10.3 %collective-permute-done.4.refs_6_ = bf16[512,512]{1,0:T(8,128)(2,1)} collective-permute-done((bf16[512,512]{1,0:T(8,128)(2,1)}, bf16[512,512]{1,0:T(8,128)(2,1)}, u32[]{:S(2)}, u32[]{:S(2)}) %collective-permute-start.4) | collective-permute-done | bytes 524320 | tf_op jit(solution)/shard_map/ppermute | solution.py:520
  54.0 8.3 %attend.1 = (f32[1024,512]{1,0:T(8,128)}, bf16[512,1024]{1,0:T(8,128)(2,1)S(1)}, f32[4,4,512]{2,1,0:T(4,128)S(1)}) custom-call(s32[1]{0:T(128)} %bitcast.2.own_ref, bf16[1024,512]{1,0:T(8,128)(2,1)} %bitcast.127, bf16[512,512]{1,0:T(8,128)(2,1)S(1)} %bitcast.118, bf16[512,512]{1,0:T(8,128)(2,1)S(1)} %collective-permute-done.refs_1_, ...), custom_call_target="tpu_custom_call" | custom-call | flops 17179869184 | bytes 6291456 | tf_op jit(solution)/shard_map/attend/pallas_call | solution.py:181
  72.9 23.8 %experts_front.3 = (bf16[544,1024]{1,0:T(8,128)(2,1)}, bf16[544,1024]{1,0:T(8,128)(2,1)}, bf16[4,384,1024]{2,1,0:T(8,128)(2,1)}, bf16[4,384,1024]{2,1,0:T(8,128)...) custom-call(s32[1]{0:T(128)} %bitcast.16.here_ref, bf16[512,1024]{1,0:T(8,128)(2,1)} %copy-done.23, ...), custom_call_target="tpu_custom_call" | custom-call | flops 12884901888 | bytes 12582912 | tf_op jit(solution)/shard_map/experts_front/pallas_call | solution.py:425
  96.8 17.0 %experts_rear.3 = (bf16[512,1024]{1,0:T(8,128)(2,1)}, bf16[512,1024]{1,0:T(8,128)(2,1)}, bf16[4,1536,1024]{2,1,0:T(8,128)(2,1)}) custom-call(s32[1]{0:T(128)} %bitcast.16.here_ref, bf16[4,384,1024]{2,1,0:T(8,128)(2,1)} %get-tuple-element.118.refs_0_, bf16[4,384,1024]{2,1,0:T(8,128)(2,1)} %get-tuple-element.119.refs_1_, ...), custom_call_target="tpu_custom_call" | custom-call | flops 8053063680 | bytes 12582912 | tf_op jit(solution)/shard_map/experts_rear/pallas_call | solution.py:489
  113.8 27.0 %collective-permute-done.10.refs_0_ = bf16[512,1024]{1,0:T(8,128)(2,1)} collective-permute-done((bf16[512,1024]{1,0:T(8,128)(2,1)S(1)}, bf16[512,1024]{1,0:T(8,128)(2,1)}, u32[]{:S(2)}, u32[]{:S(2)}) %collective-permute-start.10) | collective-permute-done | bytes 1048608 | tf_op jit(solution)/shard_map/ppermute | solution.py:520
  144.1 23.5 %experts_front.4 = (bf16[544,1024]{1,0:T(8,128)(2,1)}, bf16[544,1024]{1,0:T(8,128)(2,1)}, bf16[4,384,1024]{2,1,0:T(8,128)(2,1)}, bf16[4,384,1024]{2,1,0:T(8,128)...) custom-call(s32[1]{0:T(128)} %bitcast.16.here_ref, ...), custom_call_target="tpu_custom_call" | custom-call | flops 12884901888 | bytes 12582912 | tf_op jit(solution)/shard_map/experts_front/pallas_call | solution.py:425
  172.2 42.3 %experts_front.5 = (bf16[544,1024]{1,0:T(8,128)(2,1)}, bf16[544,1024]{1,0:T(8,128)(2,1)}, bf16[544,1024]{1,0:T(8,128)(2,1)}, bf16[544,1024]{1,0:T(8,128)(2,1)}, ...) custom-call(s32[1]{0:T(128)} %bitcast.16.here_ref, ...), custom_call_target="tpu_custom_call" | custom-call | flops 25769803776 | bytes 25165824 | tf_op jit(solution)/shard_map/experts_front/pallas_call | solution.py:425
  236.7 19.8 %experts_rear.4 = (bf16[512,1024]{1,0:T(8,128)(2,1)}, bf16[512,1024]{1,0:T(8,128)(2,1)}, bf16[4,1536,1024]{2,1,0:T(8,128)(2,1)}) custom-call(s32[1]{0:T(128)} %bitcast.16.here_ref, bf16[4,384,1024]{2,1,0:T(8,128)(2,1)} %get-tuple-element.137.refs_0_, bf16[4,384,1024]{2,1,0:T(8,128)(2,1)} %get-tuple-element.138.refs_1_, ...), custom_call_target="tpu_custom_call" | custom-call | flops 8053063680 | bytes 12582912 | tf_op jit(solution)/shard_map/experts_rear/pallas_call | solution.py:489
  256.4 21.7 %collective-permute-done.17 = bf16[544,1024]{1,0:T(8,128)(2,1)} collective-permute-done((bf16[544,1024]{1,0:T(8,128)(2,1)}, bf16[544,1024]{1,0:T(8,128)(2,1)}, u32[]{:S(2)}, u32[]{:S(2)}) %collective-permute-start.17) | collective-permute-done | bytes 1114144 | tf_op jit(solution)/shard_map/ppermute | solution.py:520
  285.9 27.9 %experts_rear.5 = (bf16[512,1024]{1,0:T(8,128)(2,1)}, bf16[512,1024]{1,0:T(8,128)(2,1)}, bf16[512,1024]{1,0:T(8,128)(2,1)}, bf16[512,1024]{1,0:T(8,128)(2,1)}, bf16[4,1536,1024]{2,1,0:T(8,128)(2,1)}) custom-call(s32[1]{0:T(128)} %bitcast.16.here_ref, bf16[4,768,1024]{2,1,0:T(8,128)(2,1)} %get-tuple-element.149.refs_0_, ...), custom_call_target="tpu_custom_call" | custom-call | flops 16106127360 | bytes 25165824 | tf_op jit(solution)/shard_map/experts_rear/pallas_call | solution.py:489
  313.8 6.3 constant_dynamic-slice_fusion.2
  321.8 3.8 collective-permute-start.38
  325.6 8.7 %collective-permute-done.21 = bf16[544,1024]{1,0:T(8,128)(2,1)} collective-permute-done((bf16[544,1024]{1,0:T(8,128)(2,1)}, bf16[544,1024]{1,0:T(8,128)(2,1)}, u32[]{:S(2)}, u32[]{:S(2)}) %collective-permute-start.21) | collective-permute-done | bytes 1114144 | tf_op jit(solution)/shard_map/ppermute | solution.py:520
  342.1 15.7 %attend_back.1 = (f32[1024,512]{1,0:T(8,128)}, bf16[512,512]{1,0:T(8,128)(2,1)S(1)}, bf16[512,512]{1,0:T(8,128)(2,1)S(1)}, bf16[512,512]{1,0:T(8,128)(2,1)S(1)},...) custom-call(s32[1]{0:T(128)} %bitcast.2.own_ref, ...), custom_call_target="tpu_custom_call" | custom-call | flops 42949672960 | bytes 6291456 | tf_op jit(solution)/shard_map/attend_back/pallas_call | solution.py:224
  357.9 22.3 %collective-permute-start.29 = (bf16[512,512]{1,0:T(8,128)(2,1)}, bf16[512,512]{1,0:T(8,128)(2,1)}, u32[]{:S(2)}, u32[]{:S(2)}) collective-permute-start(bf16[512,512]{1,0:T(8,128)(2,1)} %get-tuple-element.169), channel_id=1, source_target_pairs={{0,16},{8,24},{16,0},{24,8},{1,17},{9,25},{17,1},{25,9},{2,18},{10... | collective-permute-start | bytes 1572872 | tf_op jit(solution)/shard_map/ppermute | solution.py:520
  380.2 14.0 %collective-permute-start.26 = (bf16[512,512]{1,0:T(8,128)(2,1)}, bf16[512,512]{1,0:T(8,128)(2,1)}, u32[]{:S(2)}, u32[]{:S(2)}) collective-permute-start(bf16[512,512]{1,0:T(8,128)(2,1)} %get-tuple-element.165), channel_id=1, source_target_pairs={{0,8},{8,0},{16,24},{24,16},{1,9},{9,1},{17,25},{25,17},{2,10},{10... | collective-permute-start | bytes 1572872 | tf_op jit(solution)/shard_map/ppermute | solution.py:520
  416.8 8.2 %add_convert_fusion = (bf16[4,384,1024]{2,1,0:T(8,128)(2,1)S(1)}, bf16[4,384,1024]{2,1,0:T(8,128)(2,1)S(1)}) fusion(bf16[4,384,1024]{2,1,0:T(8,128)(2,1)} %collective-permute-done.39, bf16[4,1536,1024]{2,1,0:T(8,128)(2,1)} %get-tuple-element.153, s32[]{:T(128)S(6)} %select_n.142, bf16[4,384,1024]{2,1,0:T(8,128)(2,1)} %collective-permute-done.38, s32[]{:T(128)S(6)} %select_n.138), kind=kLoop, calls=%fused_computation | loop fusion | flops 12582912 | bytes 18874376 | tf_op jit(solution)/shard_map/convert_element_type | solution.py:524
  435.3 10.0 %collective-permute-done.30 = bf16[512,512]{1,0:T(8,128)(2,1)S(1)} collective-permute-done((bf16[512,512]{1,0:T(8,128)(2,1)}, bf16[512,512]{1,0:T(8,128)(2,1)S(1)}, u32[]{:S(2)}, u32[]{:S(2)}) %collective-permute-start.30) | collective-permute-done | bytes 524320 | tf_op jit(solution)/shard_map/ppermute | solution.py:520
  449.6 40.0 %collective-permute-done.25 = bf16[512,512]{1,0:T(8,128)(2,1)S(1)} collective-permute-done((bf16[512,512]{1,0:T(8,128)(2,1)S(1)}, bf16[512,512]{1,0:T(8,128)(2,1)S(1)}, u32[]{:S(2)}, u32[]{:S(2)}) %collective-permute-start.25) | collective-permute-done | bytes 524320 | tf_op jit(solution)/shard_map/ppermute | solution.py:520
  490.6 3.4 add_convert_fusion.3
  494.0 3.3 add_convert_fusion.2
  501.7 13.9 %collective-permute-done.36 = bf16[512,1024]{1,0:T(8,128)(2,1)} collective-permute-done((bf16[512,1024]{1,0:T(8,128)(2,1)S(1)}, bf16[512,1024]{1,0:T(8,128)(2,1)}, u32[]{:S(2)}, u32[]{:S(2)}) %collective-permute-start.36) | collective-permute-done | bytes 1048608 | tf_op jit(solution)/shard_map/ppermute | solution.py:520
  522.2 12.2 %collective-permute-done.42 = bf16[4,192,1024]{2,1,0:T(8,128)(2,1)} collective-permute-done((bf16[4,192,1024]{2,1,0:T(8,128)(2,1)}, bf16[4,192,1024]{2,1,0:T(8,128)(2,1)}, u32[]{:S(2)}, u32[]{:S(2)}) %collective-permute-start.42) | collective-permute-done | bytes 1572896 | tf_op jit(solution)/shard_map/ppermute | solution.py:520
  537.0 29.6 %collective-permute-done.33 = bf16[512,1024]{1,0:T(8,128)(2,1)} collective-permute-done((bf16[512,1024]{1,0:T(8,128)(2,1)}, bf16[512,1024]{1,0:T(8,128)(2,1)}, u32[]{:S(2)}, u32[]{:S(2)}) %collective-permute-start.33) | collective-permute-done | bytes 1048608 | tf_op jit(solution)/shard_map/ppermute | solution.py:520
  568.7 5.8 collective-permute-done.37
  574.5 5.9 add_convert_fusion.13
  588.6 34.5 %collective-permute-done.44 = bf16[4,192,1024]{2,1,0:T(8,128)(2,1)} collective-permute-done((bf16[4,192,1024]{2,1,0:T(8,128)(2,1)}, bf16[4,192,1024]{2,1,0:T(8,128)(2,1)}, u32[]{:S(2)}, u32[]{:S(2)}) %collective-permute-start.44) | collective-permute-done | bytes 1572896 | tf_op jit(solution)/shard_map/ppermute | solution.py:520
  632.6 14.9 %collective-permute-done.47 = bf16[4,192,1024]{2,1,0:T(8,128)(2,1)S(1)} collective-permute-done((bf16[4,192,1024]{2,1,0:T(8,128)(2,1)}, bf16[4,192,1024]{2,1,0:T(8,128)(2,1)S(1)}, u32[]{:S(2)}, u32[]{:S(2)}) %collective-permute-start.47) | collective-permute-done | bytes 1572896 | tf_op jit(solution)/shard_map/ppermute | solution.py:520
  648.8 6.6 slice_convert_fusion
  655.4 12.0 %slice_convert_fusion.1 = (f32[4,1024,512]{2,1,0:T(8,128)}, f32[4,1024,512]{2,1,0:T(8,128)}) fusion(bf16[4,1536,1024]{2,1,0:T(8,128)(2,1)} %constant_dynamic-update-slice_fusion.2), kind=kLoop, calls=%fused_computation.3 | loop fusion | flops 4194304 | bytes 25165824 | tf_op jit(solution)/shard_map/convert_element_type | solution.py:824
  667.5 54.7 %all-reduce.5.cloned.1.call-done = (bf16[1024,1024]{1,0:T(8,128)(2,1)}, bf16[1024,1024]{1,0:T(8,128)(2,1)}, bf16[1024,512]{1,0:T(8,128)(2,1)}, bf16[1024,512]{1,0:T(8,128)(2,1)}, bf16[64,1024]{1,0:T(8,128)(2,1)}) async-done(((bf16[1024,1024]{1,0:T(8,128)(2,1)}, bf16[1024,1024]{1,0:T(8,128)(2,1)}, bf16[1024,512]{1,0:T(8,128)(2,1)}, bf16[1024,512]{1,0:T(8,128)(2,1)}, bf16[64,1024]{1,0:T(8,128)(2,1)}), ...) | async-done | bytes 6422544 | tf_op jit(solution)/shard_map/psum | solution.py:819
  724.4 4.9 multiply_reduce_fusion
  (311 shorter events, 175.2 us)
Async XLA Ops:
  7.2 133.7 %all-gather.3.cloned.1.call-start = ((), (), s32[]{:S(2)}) async-start(), calls=%async_computation | async-start | bytes 9732096 | tf_op jit(solution)/shard_map/all_gather | solution.py:667
  10.5 711.6 %all-reduce.5.cloned.1.call-start = ((), (), s32[]{:S(2)}) async-start(), calls=%async_computation.1 | async-start | bytes 12845056 | tf_op jit(solution)/shard_map/psum | solution.py:819
  16.4 34.0 %collective-permute-start.1 = (bf16[512,512]{1,0:T(8,128)(2,1)S(1)}, bf16[512,512]{1,0:T(8,128)(2,1)}, u32[]{:S(2)}, u32[]{:S(2)}) collective-permute-start(bf16[512,512]{1,0:T(8,128)(2,1)S(1)} %bitcast.117), channel_id=1, source_target_pairs={{0,16},{8,24},{16,0},{24,8},{1,17},{9,25},{17,1},{25,9},{2,18},{10... | collective-permute-start | bytes 1572872 | tf_op jit(solution)/shard_map/ppermute | solution.py:520
  21.0 29.6 %collective-permute-start.3 = (bf16[512,512]{1,0:T(8,128)(2,1)}, bf16[512,512]{1,0:T(8,128)(2,1)}, u32[]{:S(2)}, u32[]{:S(2)}) collective-permute-start(bf16[512,512]{1,0:T(8,128)(2,1)} %convolution_convert_fusion.3.refs_4_), channel_id=1, source_target_pairs={{0,8},{8,0},{16,24},{24,16},{1,9},{9,1},{17,25},{25,17},{2,10},{10... | collective-permute-start | bytes 1572872 | tf_op jit(solution)/shard_map/ppermute | solution.py:520
  22.0 50.9 %collective-permute-start.7 = (bf16[512,1024]{1,0:T(8,128)(2,1)}, bf16[512,1024]{1,0:T(8,128)(2,1)}, u32[]{:S(2)}, u32[]{:S(2)}) collective-permute-start(bf16[512,1024]{1,0:T(8,128)(2,1)} %bitcast.refs_2_), channel_id=1, source_target_pairs={{0,1},{1,0},{2,3},{3,2},{4,5},{5,4},{6,7},{7,6},{8,9},{9,8},{10,11... | collective-permute-start | bytes 3145736 | tf_op jit(solution)/shard_map/ppermute | solution.py:520
  68.2 72.6 %collective-permute-start.10 = (bf16[512,1024]{1,0:T(8,128)(2,1)S(1)}, bf16[512,1024]{1,0:T(8,128)(2,1)}, u32[]{:S(2)}, u32[]{:S(2)}) collective-permute-start(bf16[512,1024]{1,0:T(8,128)(2,1)S(1)} %multiply_convert_fusion.refs_0_), channel_id=1, source_target_pairs={{0,4},{1,5},{2,6},{3,7},{4,0},{5,1},{6,2},{7,3},{8,12},{9,13},{10,... | collective-permute-start | bytes 3145736 | tf_op jit(solution)/shard_map/ppermute | solution.py:520
  71.3 69.6 %collective-permute-start.11 = (bf16[512,1024]{1,0:T(8,128)(2,1)S(1)}, bf16[512,1024]{1,0:T(8,128)(2,1)}, u32[]{:S(2)}, u32[]{:S(2)}) collective-permute-start(bf16[512,1024]{1,0:T(8,128)(2,1)S(1)} %multiply_convert_fusion.refs_0_), channel_id=1, source_target_pairs={{0,2},{1,3},{2,0},{3,1},{4,6},{5,7},{6,4},{7,5},{8,10},{9,11},{10,... | collective-permute-start | bytes 3145736 | tf_op jit(solution)/shard_map/ppermute | solution.py:520
  168.1 54.4 %collective-permute-start.22 = (bf16[512,1024]{1,0:T(8,128)(2,1)S(1)}, bf16[512,1024]{1,0:T(8,128)(2,1)}, u32[]{:S(2)}, u32[]{:S(2)}) collective-permute-start(bf16[512,1024]{1,0:T(8,128)(2,1)S(1)} %copy-done.21), channel_id=1, source_target_pairs={{0,8},{8,0},{16,24},{24,16},{1,9},{9,1},{17,25},{25,17},{2,10},{10... | collective-permute-start | bytes 3145736 | tf_op jit(solution)/shard_map/ppermute | solution.py:520
  169.7 54.5 %collective-permute-start.18 = (bf16[544,1024]{1,0:T(8,128)(2,1)}, bf16[544,1024]{1,0:T(8,128)(2,1)}, u32[]{:S(2)}, u32[]{:S(2)}) collective-permute-start(bf16[544,1024]{1,0:T(8,128)(2,1)} %get-tuple-element.130), channel_id=1, source_target_pairs={{0,1},{1,0},{2,3},{3,2},{4,5},{5,4},{6,7},{7,6},{8,9},{9,8},{10,11... | collective-permute-start | bytes 3342344 | tf_op jit(solution)/shard_map/ppermute | solution.py:520
  222.5 119.6 %collective-permute-start.23 = (bf16[512,1024]{1,0:T(8,128)(2,1)S(1)}, bf16[512,1024]{1,0:T(8,128)(2,1)}, u32[]{:S(2)}, u32[]{:S(2)}) collective-permute-start(bf16[512,1024]{1,0:T(8,128)(2,1)S(1)} %copy-done.21), channel_id=1, source_target_pairs={{0,16},{8,24},{16,0},{24,8},{1,17},{9,25},{17,1},{25,9},{2,18},{10... | collective-permute-start | bytes 3145736 | tf_op jit(solution)/shard_map/ppermute | solution.py:520
  224.2 117.9 %collective-permute-start.24 = (bf16[512,1024]{1,0:T(8,128)(2,1)}, bf16[512,1024]{1,0:T(8,128)(2,1)}, u32[]{:S(2)}, u32[]{:S(2)}) collective-permute-start(bf16[512,1024]{1,0:T(8,128)(2,1)} %collective-permute-done.22), channel_id=1, source_target_pairs={{0,16},{8,24},{16,0},{24,8},{1,17},{9,25},{17,1},{25,9},{2,18},{10... | collective-permute-start | bytes 3145736 | tf_op jit(solution)/shard_map/ppermute | solution.py:520
  232.2 45.9 %collective-permute-start.17 = (bf16[544,1024]{1,0:T(8,128)(2,1)}, bf16[544,1024]{1,0:T(8,128)(2,1)}, u32[]{:S(2)}, u32[]{:S(2)}) collective-permute-start(bf16[544,1024]{1,0:T(8,128)(2,1)} %add_convert_fusion.9), channel_id=1, source_target_pairs={{0,2},{1,3},{2,0},{3,1},{4,6},{5,7},{6,4},{7,5},{8,10},{9,11},{10,... | collective-permute-start | bytes 3342344 | tf_op jit(solution)/shard_map/ppermute | solution.py:520
  283.8 50.5 %collective-permute-start.21 = (bf16[544,1024]{1,0:T(8,128)(2,1)}, bf16[544,1024]{1,0:T(8,128)(2,1)}, u32[]{:S(2)}, u32[]{:S(2)}) collective-permute-start(bf16[544,1024]{1,0:T(8,128)(2,1)} %add_convert_fusion.5), channel_id=1, source_target_pairs={{0,4},{1,5},{2,6},{3,7},{4,0},{5,1},{6,2},{7,3},{8,12},{9,13},{10,... | collective-permute-start | bytes 3342344 | tf_op jit(solution)/shard_map/ppermute | solution.py:520
  320.1 96.6 %collective-permute-start.39 = (bf16[4,384,1024]{2,1,0:T(8,128)(2,1)}, bf16[4,384,1024]{2,1,0:T(8,128)(2,1)}, u32[]{:S(2)}, u32[]{:S(2)}) collective-permute-start(bf16[4,384,1024]{2,1,0:T(8,128)(2,1)} %get-tuple-element.225), channel_id=1, source_target_pairs={{0,16},{8,24},{16,0},{24,8},{1,17},{9,25},{17,1},{25,9},{2,18},{10... | collective-permute-start | bytes 9437192 | tf_op jit(solution)/shard_map/ppermute | solution.py:520
  321.8 95.0 %collective-permute-start.38 = (bf16[4,384,1024]{2,1,0:T(8,128)(2,1)}, bf16[4,384,1024]{2,1,0:T(8,128)(2,1)}, u32[]{:S(2)}, u32[]{:S(2)}) collective-permute-start(bf16[4,384,1024]{2,1,0:T(8,128)(2,1)} %get-tuple-element.226), channel_id=1, source_target_pairs={{0,8},{8,0},{16,24},{24,16},{1,9},{9,1},{17,25},{25,17},{2,10},{10... | collective-permute-start | bytes 9437192 | tf_op jit(solution)/shard_map/ppermute | solution.py:520
  357.9 70.5 %collective-permute-start.29 = (bf16[512,512]{1,0:T(8,128)(2,1)}, bf16[512,512]{1,0:T(8,128)(2,1)}, u32[]{:S(2)}, u32[]{:S(2)}) collective-permute-start(bf16[512,512]{1,0:T(8,128)(2,1)} %get-tuple-element.169), channel_id=1, source_target_pairs={{0,16},{8,24},{16,0},{24,8},{1,17},{9,25},{17,1},{25,9},{2,18},{10... | collective-permute-start | bytes 1572872 | tf_op jit(solution)/shard_map/ppermute | solution.py:520
  380.2 55.0 %collective-permute-start.28 = (bf16[512,512]{1,0:T(8,128)(2,1)S(1)}, bf16[512,512]{1,0:T(8,128)(2,1)}, u32[]{:S(2)}, u32[]{:S(2)}) collective-permute-start(bf16[512,512]{1,0:T(8,128)(2,1)S(1)} %get-tuple-element.167), channel_id=1, source_target_pairs={{0,16},{8,24},{16,0},{24,8},{1,17},{9,25},{17,1},{25,9},{2,18},{10... | collective-permute-start | bytes 1572872 | tf_op jit(solution)/shard_map/ppermute | solution.py:520
  380.2 51.4 %collective-permute-start.26 = (bf16[512,512]{1,0:T(8,128)(2,1)}, bf16[512,512]{1,0:T(8,128)(2,1)}, u32[]{:S(2)}, u32[]{:S(2)}) collective-permute-start(bf16[512,512]{1,0:T(8,128)(2,1)} %get-tuple-element.165), channel_id=1, source_target_pairs={{0,8},{8,0},{16,24},{24,16},{1,9},{9,1},{17,25},{25,17},{2,10},{10... | collective-permute-start | bytes 1572872 | tf_op jit(solution)/shard_map/ppermute | solution.py:520
  416.8 31.0 %collective-permute-start.35 = (bf16[512,1024]{1,0:T(8,128)(2,1)}, bf16[512,1024]{1,0:T(8,128)(2,1)}, u32[]{:S(2)}, u32[]{:S(2)}) collective-permute-start(bf16[512,1024]{1,0:T(8,128)(2,1)} %get-tuple-element.184), channel_id=1, source_target_pairs={{0,1},{1,0},{2,3},{3,2},{4,5},{5,4},{6,7},{7,6},{8,9},{9,8},{10,11... | collective-permute-start | bytes 3145736 | tf_op jit(solution)/shard_map/ppermute | solution.py:520
  426.4 64.2 %collective-permute-start.40 = (bf16[4,192,1024]{2,1,0:T(8,128)(2,1)}, bf16[4,192,1024]{2,1,0:T(8,128)(2,1)}, u32[]{:S(2)}, u32[]{:S(2)}) collective-permute-start(bf16[4,192,1024]{2,1,0:T(8,128)(2,1)} %constant_dynamic-slice_fusion.1), channel_id=1, source_target_pairs={{0,16},{8,24},{16,0},{24,8},{1,17},{9,25},{17,1},{25,9},{2,18},{10... | collective-permute-start | bytes 4718600 | tf_op jit(solution)/shard_map/ppermute | solution.py:520
  431.6 62.3 %collective-permute-start.41 = (bf16[4,192,1024]{2,1,0:T(8,128)(2,1)}, bf16[4,192,1024]{2,1,0:T(8,128)(2,1)}, u32[]{:S(2)}, u32[]{:S(2)}) collective-permute-start(bf16[4,192,1024]{2,1,0:T(8,128)(2,1)} %constant_dynamic-slice_fusion), channel_id=1, source_target_pairs={{0,8},{8,0},{16,24},{24,16},{1,9},{9,1},{17,25},{25,17},{2,10},{10... | collective-permute-start | bytes 4718600 | tf_op jit(solution)/shard_map/ppermute | solution.py:520
  435.1 54.4 %collective-permute-start.25 = (bf16[512,512]{1,0:T(8,128)(2,1)S(1)}, bf16[512,512]{1,0:T(8,128)(2,1)S(1)}, u32[]{:S(2)}, u32[]{:S(2)}) collective-permute-start(bf16[512,512]{1,0:T(8,128)(2,1)S(1)} %get-tuple-element.163), channel_id=1, source_target_pairs={{0,8},{8,0},{16,24},{24,16},{1,9},{9,1},{17,25},{25,17},{2,10},{10... | collective-permute-start | bytes 1572872 | tf_op jit(solution)/shard_map/ppermute | solution.py:520
  445.3 44.2 %collective-permute-start.27 = (bf16[512,512]{1,0:T(8,128)(2,1)S(1)}, bf16[512,512]{1,0:T(8,128)(2,1)S(1)}, u32[]{:S(2)}, u32[]{:S(2)}) collective-permute-start(bf16[512,512]{1,0:T(8,128)(2,1)S(1)} %add_convert_fusion.25), channel_id=1, source_target_pairs={{0,16},{8,24},{16,0},{24,8},{1,17},{9,25},{17,1},{25,9},{2,18},{10... | collective-permute-start | bytes 1572872 | tf_op jit(solution)/shard_map/ppermute | solution.py:520
  447.8 53.6 %collective-permute-start.34 = (bf16[512,1024]{1,0:T(8,128)(2,1)}, bf16[512,1024]{1,0:T(8,128)(2,1)}, u32[]{:S(2)}, u32[]{:S(2)}) collective-permute-start(bf16[512,1024]{1,0:T(8,128)(2,1)} %get-tuple-element.182), channel_id=1, source_target_pairs={{0,1},{1,0},{2,3},{3,2},{4,5},{5,4},{6,7},{7,6},{8,9},{9,8},{10,11... | collective-permute-start | bytes 3145736 | tf_op jit(solution)/shard_map/ppermute | solution.py:520
  497.3 37.1 %collective-permute-start.42 = (bf16[4,192,1024]{2,1,0:T(8,128)(2,1)}, bf16[4,192,1024]{2,1,0:T(8,128)(2,1)}, u32[]{:S(2)}, u32[]{:S(2)}) collective-permute-start(bf16[4,192,1024]{2,1,0:T(8,128)(2,1)} %add_convert_fusion.3), channel_id=1, source_target_pairs={{0,16},{8,24},{16,0},{24,8},{1,17},{9,25},{17,1},{25,9},{2,18},{10... | collective-permute-start | bytes 4718600 | tf_op jit(solution)/shard_map/ppermute | solution.py:520
  499.6 67.0 %collective-permute-start.33 = (bf16[512,1024]{1,0:T(8,128)(2,1)}, bf16[512,1024]{1,0:T(8,128)(2,1)}, u32[]{:S(2)}, u32[]{:S(2)}) collective-permute-start(bf16[512,1024]{1,0:T(8,128)(2,1)} %add_convert_fusion.19), channel_id=1, source_target_pairs={{0,2},{1,3},{2,0},{3,1},{4,6},{5,7},{6,4},{7,5},{8,10},{9,11},{10,... | collective-permute-start | bytes 3145736 | tf_op jit(solution)/shard_map/ppermute | solution.py:520
  501.4 65.8 %collective-permute-start.45 = (bf16[4,192,1024]{2,1,0:T(8,128)(2,1)}, bf16[4,192,1024]{2,1,0:T(8,128)(2,1)}, u32[]{:S(2)}, u32[]{:S(2)}) collective-permute-start(bf16[4,192,1024]{2,1,0:T(8,128)(2,1)} %add_convert_fusion.2), channel_id=1, source_target_pairs={{0,8},{8,0},{16,24},{24,16},{1,9},{9,1},{17,25},{25,17},{2,10},{10... | collective-permute-start | bytes 4718600 | tf_op jit(solution)/shard_map/ppermute | solution.py:520
  518.8 55.7 %collective-permute-start.37 = (bf16[512,1024]{1,0:T(8,128)(2,1)}, bf16[512,1024]{1,0:T(8,128)(2,1)}, u32[]{:S(2)}, u32[]{:S(2)}) collective-permute-start(bf16[512,1024]{1,0:T(8,128)(2,1)} %add_convert_fusion.15), channel_id=1, source_target_pairs={{0,4},{1,5},{2,6},{3,7},{4,0},{5,1},{6,2},{7,3},{8,12},{9,13},{10,... | collective-permute-start | bytes 3145736 | tf_op jit(solution)/shard_map/ppermute | solution.py:520
  521.8 64.1 %collective-permute-start.43 = (bf16[4,192,1024]{2,1,0:T(8,128)(2,1)}, bf16[4,192,1024]{2,1,0:T(8,128)(2,1)}, u32[]{:S(2)}, u32[]{:S(2)}) collective-permute-start(bf16[4,192,1024]{2,1,0:T(8,128)(2,1)} %add_convert_fusion.3), channel_id=1, source_target_pairs={{0,8},{8,0},{16,24},{24,16},{1,9},{9,1},{17,25},{25,17},{2,10},{10... | collective-permute-start | bytes 4718600 | tf_op jit(solution)/shard_map/ppermute | solution.py:520
  534.4 88.7 %collective-permute-start.44 = (bf16[4,192,1024]{2,1,0:T(8,128)(2,1)}, bf16[4,192,1024]{2,1,0:T(8,128)(2,1)}, u32[]{:S(2)}, u32[]{:S(2)}) collective-permute-start(bf16[4,192,1024]{2,1,0:T(8,128)(2,1)} %collective-permute-done.42), channel_id=1, source_target_pairs={{0,8},{8,0},{16,24},{24,16},{1,9},{9,1},{17,25},{25,17},{2,10},{10... | collective-permute-start | bytes 4718600 | tf_op jit(solution)/shard_map/ppermute | solution.py:520
  566.6 64.6 %collective-permute-start.46 = (bf16[4,192,1024]{2,1,0:T(8,128)(2,1)}, bf16[4,192,1024]{2,1,0:T(8,128)(2,1)S(1)}, u32[]{:S(2)}, u32[]{:S(2)}) collective-permute-start(bf16[4,192,1024]{2,1,0:T(8,128)(2,1)} %add_convert_fusion.2), channel_id=1, source_target_pairs={{0,16},{8,24},{16,0},{24,8},{1,17},{9,25},{17,1},{25,9},{2,18},{10... | collective-permute-start | bytes 4718600 | tf_op jit(solution)/shard_map/ppermute | solution.py:520
  567.2 80.3 %collective-permute-start.47 = (bf16[4,192,1024]{2,1,0:T(8,128)(2,1)}, bf16[4,192,1024]{2,1,0:T(8,128)(2,1)S(1)}, u32[]{:S(2)}, u32[]{:S(2)}) collective-permute-start(bf16[4,192,1024]{2,1,0:T(8,128)(2,1)} %collective-permute-done.45), channel_id=1, source_target_pairs={{0,16},{8,24},{16,0},{24,8},{1,17},{9,25},{17,1},{25,9},{2,18},{10... | collective-permute-start | bytes 4718600 | tf_op jit(solution)/shard_map/ppermute | solution.py:520
  (80 other events, 979.6 us)
Sparse Core Ops, SparseCore 0:
  10.6 121.0 all-gather.2
  537.1 184.9 all-reduce.4

commit v3 on v2

--- a/solution.py
+++ b/solution.py
@@ -559,49 +559,83 @@
     return (lax.axis_index(axis) // bit) % 2
 
 
+RAILS = ((1, 2), (2, 1))
+
+
 def begin_sum(grad):
-    rows = grad.shape[1]
-    half = rows // 4
+    columns = grad.shape[2]
+    half = columns // 4
     rails = []
-    for rail, (first, second) in enumerate(((1, 2), (2, 1))):
-        base = rail * (rows // 2)
+    for rail, (first, _) in enumerate(RAILS):
+        base = rail * (columns // 2)
         one = side_of("ctx", first)
-        other = lax.dynamic_slice_in_dim(grad, base + (1 - one) * half, half, 1)
-        mine = lax.dynamic_slice_in_dim(grad, base + one * half, half, 1)
+        other = lax.dynamic_slice_in_dim(grad, base + (1 - one) * half, half, 2)
+        mine = lax.dynamic_slice_in_dim(grad, base + one * half, half, 2)
         rails.append(add_low(mine, swap(other, "ctx", first)))
     return rails
 
 
 def middle_sum(rails):
     held = []
-    for mine, (first, second) in zip(rails, ((1, 2), (2, 1))):
+    for mine, (_, second) in zip(rails, RAILS):
         two = side_of("ctx", second)
-        quarter = mine.shape[1] // 2
-        other = lax.dynamic_slice_in_dim(mine, (1 - two) * quarter, quarter, 1)
-        mine = lax.dynamic_slice_in_dim(mine, two * quarter, quarter, 1)
+        quarter = mine.shape[2] // 2
+        other = lax.dynamic_slice_in_dim(mine, (1 - two) * quarter, quarter, 2)
+        mine = lax.dynamic_slice_in_dim(mine, two * quarter, quarter, 2)
         held.append(add_low(mine, swap(other, "ctx", second)))
     return held
 
 
-def end_sum(grad, held):
-    rows = grad.shape[1]
-    half, quarter = rows // 4, rows // 8
-    result = grad
-    for rail, (mine, (first, second)) in enumerate(zip(held, ((1, 2), (2, 1)))):
-        base = rail * (rows // 2)
+def end_sum(held, others):
+    across = [swap(mine, "ctx", second) for mine, (_, second) in zip(held, RAILS)]
+    along = [swap(mine, "ctx", first) for mine, (first, _) in zip(held, RAILS)]
+    across, others = lax.optimization_barrier((across, others))
+    pieces, spots = [], []
+    for index, (first, second) in enumerate(RAILS):
         one, two = side_of("ctx", first), side_of("ctx", second)
-        across = swap(mine, "ctx", second)
-        pieces = (
-            (mine, one, two),
-            (across, one, 1 - two),
-            (swap(mine, "ctx", first), 1 - one, two),
-            (swap(across, "ctx", first), 1 - one, 1 - two),
-        )
-        for piece, row, column in pieces:
-            result = lax.dynamic_update_slice_in_dim(
-                result, piece, base + row * half + column * quarter, 1
-            )
-    return result
+        pieces += [held[index], across[index], along[index], swap(across[index], "ctx", first)]
+        spots += [2 * one + two, 2 * one + 1 - two, 2 * (1 - one) + two, 2 * (1 - one) + 1 - two]
+    return pieces, jnp.stack(spots).astype(jnp.int32), others
+
+
+def assemble_kernel(width, spots_ref, *refs):
+    pieces, (gate_ref, up_ref, down_ref) = refs[:8], refs[8:]
+    part = pieces[0].shape[2]
+    for index in range(8):
+        out_ref = gate_ref if index < 4 else up_ref
+        spot = spots_ref[index]
+        out_ref[0, :, pl.ds(pl.multiple_of(spot * part, part), part)] = pieces[index][
+            0, :width
+        ].astype(F32)
+        spot = spot + index // 4 * 4
+        down_ref[0, :, pl.ds(pl.multiple_of(spot * part, part), part)] = pieces[index][
+            0, width:
+        ].astype(F32)
+
+
+def assemble(pieces, spots, width):
+    owned, rows, part = pieces[0].shape
+    hidden = rows - width
+
+    def block(*shape):
+        return pl.BlockSpec((1, *shape), lambda e, at: (e, 0, 0))
+
+    return pl.pallas_call(
+        functools.partial(assemble_kernel, width),
+        grid_spec=pltpu.PrefetchScalarGridSpec(
+            num_scalar_prefetch=1,
+            grid=(owned,),
+            in_specs=[block(rows, part)] * 8,
+            out_specs=[block(width, 4 * part), block(width, 4 * part), block(hidden, 8 * part)],
+        ),
+        out_shape=[
+            jax.ShapeDtypeStruct((owned, width, 4 * part), F32),
+            jax.ShapeDtypeStruct((owned, width, 4 * part), F32),
+            jax.ShapeDtypeStruct((owned, hidden, 8 * part), F32),
+        ],
+        compiler_params=pltpu.CompilerParams(vmem_limit_bytes=48 * 1024 * 1024),
+        name="assemble",
+    )(spots, *pieces)
 
 
 def after(values, *others):
@@ -818,16 +852,16 @@
     rails, sums = lax.optimization_barrier((rails, sums))
     sums = lax.psum(sums, ("ctx", "exp"))
     rails = middle_sum(rails)
-    expert_grads = end_sum(old, after(rails, key_back, value_back))
-    wide, hidden = w_gate.shape[1:]
-    wgate_grad = expert_grads[:, :wide, :hidden].astype(F32)
-    wup_grad = expert_grads[:, :wide, hidden:].astype(F32)
-    down_grad = expert_grads[:, wide:].astype(F32)
-    mixed = reduce_blocks(after(mixed, residual_low), "exp", exp_bits)
+    mixed = after(mixed, residual_low)
+    for bit in exp_bits[:-1]:
+        mixed = reduce_step(mixed, "exp", bit)
+    arrived = swap(mixed[exp_bits[-1]], "exp", exp_bits[-1])
+    pieces, spots, (sums, arrived) = end_sum(
+        after(rails, key_back, value_back), (sums, arrived)
+    )
+    wgate_grad, wup_grad, down_grad = assemble(pieces, spots, w_gate.shape[1])
+    mixed = add_low(mixed[0], arrived)
     output = (residual_stream + mixed.astype(F32)).astype(BF16)
-    input_grad, output, wgate_grad, wup_grad, down_grad, sums = lax.optimization_barrier(
-        (input_grad, output, wgate_grad, wup_grad, down_grad, sums)
-    )
     wout_grad, wq_grad, wk_grad, wv_grad, small = (part.astype(F32) for part in sums)
     router_grad, gain_two_grad = small[:experts].T, small[experts]
     gain_one_grad = (

time: 748 us -> 720 us (0.963)
  other arithmetic: 97.2 us -> 70.1 us
  local copies, waits for them, and re-layouts: 47.9 us -> 29.5 us
  Pallas kernels: 178 us -> 191 us
    convert_element_type x3 -> x0, other arithmetic: 24.6 us -> none  [the longest x1 12 us: per_device(): wup_grad = expert_grads[:, :wide, hidden:].astype(F32)]
    dynamic_update_slice x8 -> x0, local copies, waits for them, and re-layouts: 18.9 us -> none  [end_sum(): lax.dynamic_update_slice_in_dim(result, piece, base + row * half + column...]
    ppermute x48, waiting for transfers between devices: 235 us -> 216 us  [swap(): return lax.ppermute(value, axis, [(i, i ^ bit) for i in range(peers)])]
    psum x1, waiting for transfers between devices: 54.7 us -> 70 us  [per_device(): sums = lax.psum(sums, ('ctx', 'exp'))]
    pallas_call x0 -> x1, Pallas kernels: none -> 12.5 us  [assemble(): pl.pallas_call(functools.partial(assemble_kernel, width), grid_spec=pltpu...]
  transfers between devices with their start and end apart: 50 -> 50, of which waited for: 17 -> 15; matrix products, arithmetic and copies ran while one was open for 22% -> 19% of each run, Pallas kernels for 24% -> 25%
where the time goes in v3:
time: 720 us; the launch traced here: 715 us
  waiting for transfers between devices  287 us (40%)
  Pallas kernels  191 us (27%)
  starting transfers between devices  81.4 us (11%)
  other arithmetic  70.1 us (10%)
  matrix products  42 us (6%)
  local copies, waits for them, and re-layouts  29.5 us (4%)
  between operations  15.4 us (2%)
    ppermute x48, waiting for transfers between devices, swap(): return lax.ppermute(value, axis, [(i, i ^ bit) for i in range(peers)])  216 us
    pallas_call x3, Pallas kernels, run_front(): pl.pallas_call(functools.partial(front_kernel, blocks, start, owned, near...  89.5 us
    ppermute x48, starting transfers between devices, swap(): return lax.ppermute(value, axis, [(i, i ^ bit) for i in range(peers)])  81.3 us
    psum x1, waiting for transfers between devices, per_device(): sums = lax.psum(sums, ('ctx', 'exp'))  70 us
    pallas_call x3, Pallas kernels, run_rear(): pl.pallas_call(functools.partial(rear_kernel, blocks, start, owned, near,...  64.8 us
    convert_element_type x16, other arithmetic, add_low(): return (left.astype(F32) + right.astype(F32)).astype(BF16)  37.6 us
    dot_general x16, matrix products, mm(): return lax.dot_general(left, right, dims, preferred_element_type=F32)  29.2 us
    pallas_call x1, Pallas kernels, attend_back(): pl.pallas_call(functools.partial(attend_back_kernel, peers), grid=(pairs,...  15.5 us
  transfers between devices with their start and end apart: 50, of which 15 were waited for; matrix products, arithmetic and copies ran while one was open for 19% of the time, Pallas kernels for 25%

profile of v3, /device:TPU:0, one launch (start us, length us, event | category | flops | bytes accessed | tf_op | source)
XLA Modules:
  0.0 715.5 jit_solution(3365482339058068474)
XLA Ops:
  18.0 3.0 convolution_convert_fusion.3.refs_4_
  24.7 3.0 copy.52
  32.2 10.4 %collective-permute-done.4.refs_6_ = bf16[512,512]{1,0:T(8,128)(2,1)} collective-permute-done((bf16[512,512]{1,0:T(8,128)(2,1)}, bf16[512,512]{1,0:T(8,128)(2,1)}, u32[]{:S(2)}, u32[]{:S(2)}) %collective-permute-start.4) | collective-permute-done | bytes 524320 | tf_op jit(solution)/shard_map/ppermute | solution.py:520
  54.0 8.3 %attend.1 = (f32[1024,512]{1,0:T(8,128)}, bf16[512,1024]{1,0:T(8,128)(2,1)S(1)}, f32[4,4,512]{2,1,0:T(4,128)S(1)}) custom-call(s32[1]{0:T(128)} %bitcast.1.own_ref, bf16[1024,512]{1,0:T(8,128)(2,1)} %bitcast.137, bf16[512,512]{1,0:T(8,128)(2,1)S(1)} %bitcast.130, bf16[512,512]{1,0:T(8,128)(2,1)S(1)} %collective-permute-done.refs_1_, ...), custom_call_target="tpu_custom_call" | custom-call | flops 17179869184 | bytes 6291456 | tf_op jit(solution)/shard_map/attend/pallas_call | solution.py:181
  72.9 23.6 %experts_front.3 = (bf16[544,1024]{1,0:T(8,128)(2,1)}, bf16[544,1024]{1,0:T(8,128)(2,1)}, bf16[4,384,1024]{2,1,0:T(8,128)(2,1)}, bf16[4,384,1024]{2,1,0:T(8,128)...) custom-call(s32[1]{0:T(128)} %bitcast.12.here_ref, bf16[512,1024]{1,0:T(8,128)(2,1)} %copy-done.28, ...), custom_call_target="tpu_custom_call" | custom-call | flops 12884901888 | bytes 12582912 | tf_op jit(solution)/shard_map/experts_front/pallas_call | solution.py:425
  96.5 17.2 %experts_rear.3 = (bf16[512,1024]{1,0:T(8,128)(2,1)}, bf16[512,1024]{1,0:T(8,128)(2,1)}, bf16[4,1536,1024]{2,1,0:T(8,128)(2,1)}) custom-call(s32[1]{0:T(128)} %bitcast.12.here_ref, bf16[4,384,1024]{2,1,0:T(8,128)(2,1)} %get-tuple-element.119.refs_0_, bf16[4,384,1024]{2,1,0:T(8,128)(2,1)} %get-tuple-element.120.refs_1_, ...), custom_call_target="tpu_custom_call" | custom-call | flops 8053063680 | bytes 12582912 | tf_op jit(solution)/shard_map/experts_rear/pallas_call | solution.py:489
  113.7 25.2 %collective-permute-done.10.refs_0_ = bf16[512,1024]{1,0:T(8,128)(2,1)} collective-permute-done((bf16[512,1024]{1,0:T(8,128)(2,1)S(1)}, bf16[512,1024]{1,0:T(8,128)(2,1)}, u32[]{:S(2)}, u32[]{:S(2)}) %collective-permute-start.10) | collective-permute-done | bytes 1048608 | tf_op jit(solution)/shard_map/ppermute | solution.py:520
  144.9 23.5 %experts_front.4 = (bf16[544,1024]{1,0:T(8,128)(2,1)}, bf16[544,1024]{1,0:T(8,128)(2,1)}, bf16[4,384,1024]{2,1,0:T(8,128)(2,1)}, bf16[4,384,1024]{2,1,0:T(8,128)...) custom-call(s32[1]{0:T(128)} %bitcast.12.here_ref, ...), custom_call_target="tpu_custom_call" | custom-call | flops 12884901888 | bytes 12582912 | tf_op jit(solution)/shard_map/experts_front/pallas_call | solution.py:425
  172.9 42.4 %experts_front.5 = (bf16[544,1024]{1,0:T(8,128)(2,1)}, bf16[544,1024]{1,0:T(8,128)(2,1)}, bf16[544,1024]{1,0:T(8,128)(2,1)}, bf16[544,1024]{1,0:T(8,128)(2,1)}, ...) custom-call(s32[1]{0:T(128)} %bitcast.12.here_ref, ...), custom_call_target="tpu_custom_call" | custom-call | flops 25769803776 | bytes 25165824 | tf_op jit(solution)/shard_map/experts_front/pallas_call | solution.py:425
  225.4 3.0 add_convert_fusion.9
  237.3 19.7 %experts_rear.4 = (bf16[512,1024]{1,0:T(8,128)(2,1)}, bf16[512,1024]{1,0:T(8,128)(2,1)}, bf16[4,1536,1024]{2,1,0:T(8,128)(2,1)}) custom-call(s32[1]{0:T(128)} %bitcast.12.here_ref, bf16[4,384,1024]{2,1,0:T(8,128)(2,1)} %get-tuple-element.139.refs_0_, bf16[4,384,1024]{2,1,0:T(8,128)(2,1)} %get-tuple-element.140.refs_1_, ...), custom_call_target="tpu_custom_call" | custom-call | flops 8053063680 | bytes 12582912 | tf_op jit(solution)/shard_map/experts_rear/pallas_call | solution.py:489
  257.0 21.8 %collective-permute-done.19 = bf16[544,1024]{1,0:T(8,128)(2,1)} collective-permute-done((bf16[544,1024]{1,0:T(8,128)(2,1)}, bf16[544,1024]{1,0:T(8,128)(2,1)}, u32[]{:S(2)}, u32[]{:S(2)}) %collective-permute-start.19) | collective-permute-done | bytes 1114144 | tf_op jit(solution)/shard_map/ppermute | solution.py:520
  286.1 27.8 %experts_rear.5 = (bf16[512,1024]{1,0:T(8,128)(2,1)}, bf16[512,1024]{1,0:T(8,128)(2,1)}, bf16[512,1024]{1,0:T(8,128)(2,1)}, bf16[512,1024]{1,0:T(8,128)(2,1)}, bf16[4,1536,1024]{2,1,0:T(8,128)(2,1)}) custom-call(s32[1]{0:T(128)} %bitcast.12.here_ref, bf16[4,768,1024]{2,1,0:T(8,128)(2,1)} %get-tuple-element.153.refs_0_, ...), custom_call_target="tpu_custom_call" | custom-call | flops 16106127360 | bytes 25165824 | tf_op jit(solution)/shard_map/experts_rear/pallas_call | solution.py:489
  313.9 6.1 constant_dynamic-slice_fusion.2
  320.0 3.8 collective-permute-start.25
  325.4 9.5 %collective-permute-done.21 = bf16[544,1024]{1,0:T(8,128)(2,1)} collective-permute-done((bf16[544,1024]{1,0:T(8,128)(2,1)}, bf16[544,1024]{1,0:T(8,128)(2,1)}, u32[]{:S(2)}, u32[]{:S(2)}) %collective-permute-start.21) | collective-permute-done | bytes 1114144 | tf_op jit(solution)/shard_map/ppermute | solution.py:520
  342.4 15.5 %attend_back.1 = (f32[1024,512]{1,0:T(8,128)}, bf16[512,512]{1,0:T(8,128)(2,1)S(1)}, bf16[512,512]{1,0:T(8,128)(2,1)S(1)}, bf16[512,512]{1,0:T(8,128)(2,1)S(1)},...) custom-call(s32[1]{0:T(128)} %bitcast.1.own_ref, ...), custom_call_target="tpu_custom_call" | custom-call | flops 42949672960 | bytes 6291456 | tf_op jit(solution)/shard_map/attend_back/pallas_call | solution.py:224
  357.9 13.7 %collective-permute-start.32 = (bf16[512,512]{1,0:T(8,128)(2,1)S(1)}, bf16[512,512]{1,0:T(8,128)(2,1)}, u32[]{:S(2)}, u32[]{:S(2)}) collective-permute-start(bf16[512,512]{1,0:T(8,128)(2,1)S(1)} %get-tuple-element.177), channel_id=1, source_target_pairs={{0,8},{8,0},{16,24},{24,16},{1,9},{9,1},{17,25},{25,17},{2,10},{10... | collective-permute-start | bytes 1572872 | tf_op jit(solution)/shard_map/ppermute | solution.py:520
  375.7 22.3 %collective-permute-start.36 = (bf16[512,512]{1,0:T(8,128)(2,1)}, bf16[512,512]{1,0:T(8,128)(2,1)}, u32[]{:S(2)}, u32[]{:S(2)}) collective-permute-start(bf16[512,512]{1,0:T(8,128)(2,1)} %get-tuple-element.185), channel_id=1, source_target_pairs={{0,16},{8,24},{16,0},{24,8},{1,17},{9,25},{17,1},{25,9},{2,18},{10... | collective-permute-start | bytes 1572872 | tf_op jit(solution)/shard_map/ppermute | solution.py:520
  409.6 3.1 add_convert_fusion.16
  413.4 3.1 add_convert_fusion.17
  420.6 6.2 add_convert_fusion
  433.9 6.1 collective-permute-done.34
  446.1 43.6 %collective-permute-done.37 = bf16[512,512]{1,0:T(8,128)(2,1)S(1)} collective-permute-done((bf16[512,512]{1,0:T(8,128)(2,1)S(1)}, bf16[512,512]{1,0:T(8,128)(2,1)S(1)}, u32[]{:S(2)}, u32[]{:S(2)}) %collective-permute-start.37) | collective-permute-done | bytes 524320 | tf_op jit(solution)/shard_map/ppermute | solution.py:520
  493.6 3.4 add_convert_fusion.2.refs_4_
  500.9 27.3 %collective-permute-done.42 = bf16[512,1024]{1,0:T(8,128)(2,1)S(1)} collective-permute-done((bf16[512,1024]{1,0:T(8,128)(2,1)S(1)}, bf16[512,1024]{1,0:T(8,128)(2,1)S(1)}, u32[]{:S(2)}, u32[]{:S(2)}) %collective-permute-start.42) | collective-permute-done | bytes 1048608 | tf_op jit(solution)/shard_map/ppermute | solution.py:520
  536.4 42.5 %collective-permute-done.43 = bf16[512,1024]{1,0:T(8,128)(2,1)S(1)} collective-permute-done((bf16[512,1024]{1,0:T(8,128)(2,1)S(1)}, bf16[512,1024]{1,0:T(8,128)(2,1)S(1)}, u32[]{:S(2)}, u32[]{:S(2)}) %collective-permute-start.43) | collective-permute-done | bytes 1048608 | tf_op jit(solution)/shard_map/ppermute | solution.py:520
  581.4 70.0 %all-reduce.5.cloned.1.call-done = (bf16[1024,1024]{1,0:T(8,128)(2,1)}, bf16[1024,1024]{1,0:T(8,128)(2,1)}, bf16[1024,512]{1,0:T(8,128)(2,1)}, bf16[1024,512]{1,0:T(8,128)(2,1)}, bf16[64,1024]{1,0:T(8,128)(2,1)}) async-done(((bf16[1024,1024]{1,0:T(8,128)(2,1)}, bf16[1024,1024]{1,0:T(8,128)(2,1)}, bf16[1024,512]{1,0:T(8,128)(2,1)}, bf16[1024,512]{1,0:T(8,128)(2,1)}, bf16[64,1024]{1,0:T(8,128)(2,1)}), ...) | async-done | bytes 6422544 | tf_op jit(solution)/shard_map/psum | solution.py:853
  651.5 4.9 multiply_reduce_fusion
  666.0 4.5 fusion.12
  670.4 21.6 %collective-permute-done.45.refs_3_ = bf16[4,1536,128]{2,1,0:T(8,128)(2,1)S(1)} collective-permute-done((bf16[4,1536,128]{2,1,0:T(8,128)(2,1)S(1)}, bf16[4,1536,128]{2,1,0:T(8,128)(2,1)S(1)}, u32[]{:S(2)}, u32[]{:S(2)}) %collective-permute-start.45) | collective-permute-done | bytes 1572896 | tf_op jit(solution)/shard_map/ppermute | solution.py:520
  695.9 12.5 %assemble.1 = (f32[4,1024,512]{2,1,0:T(8,128)}, f32[4,1024,512]{2,1,0:T(8,128)}, f32[4,512,1024]{2,1,0:T(8,128)}) custom-call(s32[8]{0:T(128)S(1)} %stack.67.spots_ref, bf16[4,1536,128]{2,1,0:T(8,128)(2,1)S(1)} %copy-done.3, bf16[4,1536,128]{2,1,0:T(8,128)(2,1)S(1)} %copy-done.5, bf16[4,1536,128]{2,1,0:T(8,128)(2,1)} %collective-permute-done.44.refs_2_, ...), custom_call_target="tpu_custom_call" | custom-call | tf_op jit(solution)/shard_map/assemble/pallas_call | solution.py:623
  (325 shorter events, 151.6 us)
Async XLA Ops:
  7.2 134.5 %all-gather.3.cloned.1.call-start = ((), (), s32[]{:S(2)}) async-start(), calls=%async_computation | async-start | bytes 9732096 | tf_op jit(solution)/shard_map/all_gather | solution.py:701
  10.5 641.0 %all-reduce.5.cloned.1.call-start = ((), (), s32[]{:S(2)}) async-start(), calls=%async_computation.1 | async-start | bytes 12845056 | tf_op jit(solution)/shard_map/psum | solution.py:853
  22.0 44.4 %collective-permute-start.8 = (bf16[8,512]{1,0:T(8,128)(2,1)S(1)}, bf16[8,512]{1,0:T(8,128)(2,1)S(1)}, u32[]{:S(2)}, u32[]{:S(2)}) collective-permute-start(bf16[8,512]{1,0:T(8,128)(2,1)S(1)} %bitcast_convert_fusion), channel_id=1, source_target_pairs={{0,1},{1,0},{2,3},{3,2},{4,5},{5,4},{6,7},{7,6},{8,9},{9,8},{10,11... | collective-permute-start | bytes 24584 | tf_op jit(solution)/shard_map/ppermute | solution.py:520
  68.2 70.7 %collective-permute-start.10 = (bf16[512,1024]{1,0:T(8,128)(2,1)S(1)}, bf16[512,1024]{1,0:T(8,128)(2,1)}, u32[]{:S(2)}, u32[]{:S(2)}) collective-permute-start(bf16[512,1024]{1,0:T(8,128)(2,1)S(1)} %multiply_convert_fusion.refs_0_), channel_id=1, source_target_pairs={{0,2},{1,3},{2,0},{3,1},{4,6},{5,7},{6,4},{7,5},{8,10},{9,11},{10,... | collective-permute-start | bytes 3145736 | tf_op jit(solution)/shard_map/ppermute | solution.py:520
  70.2 68.7 %collective-permute-start.9 = (bf16[512,1024]{1,0:T(8,128)(2,1)S(1)}, bf16[512,1024]{1,0:T(8,128)(2,1)}, u32[]{:S(2)}, u32[]{:S(2)}) collective-permute-start(bf16[512,1024]{1,0:T(8,128)(2,1)S(1)} %multiply_convert_fusion.refs_0_), channel_id=1, source_target_pairs={{0,4},{1,5},{2,6},{3,7},{4,0},{5,1},{6,2},{7,3},{8,12},{9,13},{10,... | collective-permute-start | bytes 3145736 | tf_op jit(solution)/shard_map/ppermute | solution.py:520
  168.9 54.4 %collective-permute-start.27 = (bf16[512,1024]{1,0:T(8,128)(2,1)S(1)}, bf16[512,1024]{1,0:T(8,128)(2,1)}, u32[]{:S(2)}, u32[]{:S(2)}) collective-permute-start(bf16[512,1024]{1,0:T(8,128)(2,1)S(1)} %copy-done.26), channel_id=1, source_target_pairs={{0,8},{8,0},{16,24},{24,16},{1,9},{9,1},{17,25},{25,17},{2,10},{10... | collective-permute-start | bytes 3145736 | tf_op jit(solution)/shard_map/ppermute | solution.py:520
  170.5 54.5 %collective-permute-start.13 = (bf16[544,1024]{1,0:T(8,128)(2,1)}, bf16[544,1024]{1,0:T(8,128)(2,1)}, u32[]{:S(2)}, u32[]{:S(2)}) collective-permute-start(bf16[544,1024]{1,0:T(8,128)(2,1)} %get-tuple-element.131), channel_id=1, source_target_pairs={{0,1},{1,0},{2,3},{3,2},{4,5},{5,4},{6,7},{7,6},{8,9},{9,8},{10,11... | collective-permute-start | bytes 3342344 | tf_op jit(solution)/shard_map/ppermute | solution.py:520
  223.3 119.1 %collective-permute-start.28 = (bf16[512,1024]{1,0:T(8,128)(2,1)S(1)}, bf16[512,1024]{1,0:T(8,128)(2,1)}, u32[]{:S(2)}, u32[]{:S(2)}) collective-permute-start(bf16[512,1024]{1,0:T(8,128)(2,1)S(1)} %copy-done.26), channel_id=1, source_target_pairs={{0,16},{8,24},{16,0},{24,8},{1,17},{9,25},{17,1},{25,9},{2,18},{10... | collective-permute-start | bytes 3145736 | tf_op jit(solution)/shard_map/ppermute | solution.py:520
  225.0 117.4 %collective-permute-start.29 = (bf16[512,1024]{1,0:T(8,128)(2,1)}, bf16[512,1024]{1,0:T(8,128)(2,1)}, u32[]{:S(2)}, u32[]{:S(2)}) collective-permute-start(bf16[512,1024]{1,0:T(8,128)(2,1)} %collective-permute-done.27), channel_id=1, source_target_pairs={{0,16},{8,24},{16,0},{24,8},{1,17},{9,25},{17,1},{25,9},{2,18},{10... | collective-permute-start | bytes 3145736 | tf_op jit(solution)/shard_map/ppermute | solution.py:520
  231.7 47.1 %collective-permute-start.19 = (bf16[544,1024]{1,0:T(8,128)(2,1)}, bf16[544,1024]{1,0:T(8,128)(2,1)}, u32[]{:S(2)}, u32[]{:S(2)}) collective-permute-start(bf16[544,1024]{1,0:T(8,128)(2,1)} %add_convert_fusion.7), channel_id=1, source_target_pairs={{0,2},{1,3},{2,0},{3,1},{4,6},{5,7},{6,4},{7,5},{8,10},{9,11},{10,... | collective-permute-start | bytes 3342344 | tf_op jit(solution)/shard_map/ppermute | solution.py:520
  284.5 50.4 %collective-permute-start.21 = (bf16[544,1024]{1,0:T(8,128)(2,1)}, bf16[544,1024]{1,0:T(8,128)(2,1)}, u32[]{:S(2)}, u32[]{:S(2)}) collective-permute-start(bf16[544,1024]{1,0:T(8,128)(2,1)} %add_convert_fusion.5), channel_id=1, source_target_pairs={{0,4},{1,5},{2,6},{3,7},{4,0},{5,1},{6,2},{7,3},{8,12},{9,13},{10,... | collective-permute-start | bytes 3342344 | tf_op jit(solution)/shard_map/ppermute | solution.py:520
  320.0 99.2 %collective-permute-start.25 = (bf16[4,1536,256]{2,1,0:T(8,128)(2,1)}, bf16[4,1536,256]{2,1,0:T(8,128)(2,1)}, u32[]{:S(2)}, u32[]{:S(2)}) collective-permute-start(bf16[4,1536,256]{2,1,0:T(8,128)(2,1)} %get-tuple-element.226), channel_id=1, source_target_pairs={{0,8},{8,0},{16,24},{24,16},{1,9},{9,1},{17,25},{25,17},{2,10},{10... | collective-permute-start | bytes 9437192 | tf_op jit(solution)/shard_map/ppermute | solution.py:520
  323.8 95.4 %collective-permute-start.26 = (bf16[4,1536,256]{2,1,0:T(8,128)(2,1)}, bf16[4,1536,256]{2,1,0:T(8,128)(2,1)}, u32[]{:S(2)}, u32[]{:S(2)}) collective-permute-start(bf16[4,1536,256]{2,1,0:T(8,128)(2,1)} %get-tuple-element.225), channel_id=1, source_target_pairs={{0,16},{8,24},{16,0},{24,8},{1,17},{9,25},{17,1},{25,9},{2,18},{10... | collective-permute-start | bytes 9437192 | tf_op jit(solution)/shard_map/ppermute | solution.py:520
  357.9 75.2 %collective-permute-start.32 = (bf16[512,512]{1,0:T(8,128)(2,1)S(1)}, bf16[512,512]{1,0:T(8,128)(2,1)}, u32[]{:S(2)}, u32[]{:S(2)}) collective-permute-start(bf16[512,512]{1,0:T(8,128)(2,1)S(1)} %get-tuple-element.177), channel_id=1, source_target_pairs={{0,8},{8,0},{16,24},{24,16},{1,9},{9,1},{17,25},{25,17},{2,10},{10... | collective-permute-start | bytes 1572872 | tf_op jit(solution)/shard_map/ppermute | solution.py:520
  375.7 40.9 %collective-permute-start.33 = (bf16[512,512]{1,0:T(8,128)(2,1)}, bf16[512,512]{1,0:T(8,128)(2,1)}, u32[]{:S(2)}, u32[]{:S(2)}) collective-permute-start(bf16[512,512]{1,0:T(8,128)(2,1)} %get-tuple-element.181), channel_id=1, source_target_pairs={{0,8},{8,0},{16,24},{24,16},{1,9},{9,1},{17,25},{25,17},{2,10},{10... | collective-permute-start | bytes 1572872 | tf_op jit(solution)/shard_map/ppermute | solution.py:520
  375.7 52.8 %collective-permute-start.36 = (bf16[512,512]{1,0:T(8,128)(2,1)}, bf16[512,512]{1,0:T(8,128)(2,1)}, u32[]{:S(2)}, u32[]{:S(2)}) collective-permute-start(bf16[512,512]{1,0:T(8,128)(2,1)} %get-tuple-element.185), channel_id=1, source_target_pairs={{0,16},{8,24},{16,0},{24,8},{1,17},{9,25},{17,1},{25,9},{2,18},{10... | collective-permute-start | bytes 1572872 | tf_op jit(solution)/shard_map/ppermute | solution.py:520
  419.1 71.9 %collective-permute-start.41 = (bf16[512,1024]{1,0:T(8,128)(2,1)}, bf16[512,1024]{1,0:T(8,128)(2,1)}, u32[]{:S(2)}, u32[]{:S(2)}) collective-permute-start(bf16[512,1024]{1,0:T(8,128)(2,1)} %get-tuple-element.198), channel_id=1, source_target_pairs={{0,1},{1,0},{2,3},{3,2},{4,5},{5,4},{6,7},{7,6},{8,9},{9,8},{10,11... | collective-permute-start | bytes 3145736 | tf_op jit(solution)/shard_map/ppermute | solution.py:520
  428.5 65.0 %collective-permute-start.31 = (bf16[4,1536,128]{2,1,0:T(8,128)(2,1)}, bf16[4,1536,128]{2,1,0:T(8,128)(2,1)}, u32[]{:S(2)}, u32[]{:S(2)}) collective-permute-start(bf16[4,1536,128]{2,1,0:T(8,128)(2,1)} %constant_dynamic-slice_fusion), channel_id=1, source_target_pairs={{0,8},{8,0},{16,24},{24,16},{1,9},{9,1},{17,25},{25,17},{2,10},{10... | collective-permute-start | bytes 4718600 | tf_op jit(solution)/shard_map/ppermute | solution.py:520
  433.1 56.6 %collective-permute-start.37 = (bf16[512,512]{1,0:T(8,128)(2,1)S(1)}, bf16[512,512]{1,0:T(8,128)(2,1)S(1)}, u32[]{:S(2)}, u32[]{:S(2)}) collective-permute-start(bf16[512,512]{1,0:T(8,128)(2,1)S(1)} %add_convert_fusion.22), channel_id=1, source_target_pairs={{0,8},{8,0},{16,24},{24,16},{1,9},{9,1},{17,25},{25,17},{2,10},{10... | collective-permute-start | bytes 1572872 | tf_op jit(solution)/shard_map/ppermute | solution.py:520
  440.0 57.0 %collective-permute-start.30 = (bf16[4,1536,128]{2,1,0:T(8,128)(2,1)}, bf16[4,1536,128]{2,1,0:T(8,128)(2,1)}, u32[]{:S(2)}, u32[]{:S(2)}) collective-permute-start(bf16[4,1536,128]{2,1,0:T(8,128)(2,1)} %constant_dynamic-slice_fusion.1), channel_id=1, source_target_pairs={{0,16},{8,24},{16,0},{24,8},{1,17},{9,25},{17,1},{25,9},{2,18},{10... | collective-permute-start | bytes 4718600 | tf_op jit(solution)/shard_map/ppermute | solution.py:520
  446.1 53.2 %collective-permute-start.40 = (bf16[512,1024]{1,0:T(8,128)(2,1)}, bf16[512,1024]{1,0:T(8,128)(2,1)S(1)}, u32[]{:S(2)}, u32[]{:S(2)}) collective-permute-start(bf16[512,1024]{1,0:T(8,128)(2,1)} %get-tuple-element.196), channel_id=1, source_target_pairs={{0,1},{1,0},{2,3},{3,2},{4,5},{5,4},{6,7},{7,6},{8,9},{9,8},{10,11... | collective-permute-start | bytes 3145736 | tf_op jit(solution)/shard_map/ppermute | solution.py:520
  489.7 39.6 %collective-permute-start.23 = (bf16[512,1024]{1,0:T(8,128)(2,1)}, bf16[512,1024]{1,0:T(8,128)(2,1)S(1)}, u32[]{:S(2)}, u32[]{:S(2)}) collective-permute-start(bf16[512,1024]{1,0:T(8,128)(2,1)} %get-tuple-element.166), channel_id=1, source_target_pairs={{0,1},{1,0},{2,3},{3,2},{4,5},{5,4},{6,7},{7,6},{8,9},{9,8},{10,11... | collective-permute-start | bytes 3145736 | tf_op jit(solution)/shard_map/ppermute | solution.py:520
  491.0 170.1 %collective-permute-start.22 = (bf16[512,1024]{1,0:T(8,128)(2,1)}, bf16[512,1024]{1,0:T(8,128)(2,1)}, u32[]{:S(2)}, u32[]{:S(2)}) collective-permute-start(bf16[512,1024]{1,0:T(8,128)(2,1)} %get-tuple-element.164), channel_id=1, source_target_pairs={{0,1},{1,0},{2,3},{3,2},{4,5},{5,4},{6,7},{7,6},{8,9},{9,8},{10,11... | collective-permute-start | bytes 3145736 | tf_op jit(solution)/shard_map/ppermute | solution.py:520
  493.5 34.6 %collective-permute-start.42 = (bf16[512,1024]{1,0:T(8,128)(2,1)S(1)}, bf16[512,1024]{1,0:T(8,128)(2,1)S(1)}, u32[]{:S(2)}, u32[]{:S(2)}) collective-permute-start(bf16[512,1024]{1,0:T(8,128)(2,1)S(1)} %add_convert_fusion.14), channel_id=1, source_target_pairs={{0,2},{1,3},{2,0},{3,1},{4,6},{5,7},{6,4},{7,5},{8,10},{9,11},{10,... | collective-permute-start | bytes 3145736 | tf_op jit(solution)/shard_map/ppermute | solution.py:520
  499.0 82.4 %collective-permute-start.38 = (bf16[4,1536,128]{2,1,0:T(8,128)(2,1)S(1)}, bf16[4,1536,128]{2,1,0:T(8,128)(2,1)S(1)}, u32[]{:S(2)}, u32[]{:S(2)}) collective-permute-start(bf16[4,1536,128]{2,1,0:T(8,128)(2,1)S(1)} %add_convert_fusion.3.refs_0_), channel_id=1, source_target_pairs={{0,16},{8,24},{16,0},{24,8},{1,17},{9,25},{17,1},{25,9},{2,18},{10... | collective-permute-start | bytes 4718600 | tf_op jit(solution)/shard_map/ppermute | solution.py:520
  499.3 82.2 %collective-permute-start.39 = (bf16[4,1536,128]{2,1,0:T(8,128)(2,1)}, bf16[4,1536,128]{2,1,0:T(8,128)(2,1)}, u32[]{:S(2)}, u32[]{:S(2)}) collective-permute-start(bf16[4,1536,128]{2,1,0:T(8,128)(2,1)} %add_convert_fusion.2.refs_4_), channel_id=1, source_target_pairs={{0,8},{8,0},{16,24},{24,16},{1,9},{9,1},{17,25},{25,17},{2,10},{10... | collective-permute-start | bytes 4718600 | tf_op jit(solution)/shard_map/ppermute | solution.py:520
  528.8 50.1 %collective-permute-start.43 = (bf16[512,1024]{1,0:T(8,128)(2,1)S(1)}, bf16[512,1024]{1,0:T(8,128)(2,1)S(1)}, u32[]{:S(2)}, u32[]{:S(2)}) collective-permute-start(bf16[512,1024]{1,0:T(8,128)(2,1)S(1)} %add_convert_fusion.13), channel_id=1, source_target_pairs={{0,4},{1,5},{2,6},{3,7},{4,0},{5,1},{6,2},{7,3},{8,12},{9,13},{10,... | collective-permute-start | bytes 3145736 | tf_op jit(solution)/shard_map/ppermute | solution.py:520
  530.7 135.0 %collective-permute-start.24 = (bf16[512,1024]{1,0:T(8,128)(2,1)}, bf16[512,1024]{1,0:T(8,128)(2,1)}, u32[]{:S(2)}, u32[]{:S(2)}) collective-permute-start(bf16[512,1024]{1,0:T(8,128)(2,1)} %add_convert_fusion.19), channel_id=1, source_target_pairs={{0,2},{1,3},{2,0},{3,1},{4,6},{5,7},{6,4},{7,5},{8,10},{9,11},{10,... | collective-permute-start | bytes 3145736 | tf_op jit(solution)/shard_map/ppermute | solution.py:520
  578.9 91.6 %collective-permute-start.44 = (bf16[4,1536,128]{2,1,0:T(8,128)(2,1)S(1)}, bf16[4,1536,128]{2,1,0:T(8,128)(2,1)}, u32[]{:S(2)}, u32[]{:S(2)}) collective-permute-start(bf16[4,1536,128]{2,1,0:T(8,128)(2,1)S(1)} %add_convert_fusion.3.refs_0_), channel_id=1, source_target_pairs={{0,8},{8,0},{16,24},{24,16},{1,9},{9,1},{17,25},{25,17},{2,10},{10... | collective-permute-start | bytes 4718600 | tf_op jit(solution)/shard_map/ppermute | solution.py:520
  581.3 89.1 %collective-permute-start.46 = (bf16[4,1536,128]{2,1,0:T(8,128)(2,1)}, bf16[4,1536,128]{2,1,0:T(8,128)(2,1)}, u32[]{:S(2)}, u32[]{:S(2)}) collective-permute-start(bf16[4,1536,128]{2,1,0:T(8,128)(2,1)} %add_convert_fusion.2.refs_4_), channel_id=1, source_target_pairs={{0,16},{8,24},{16,0},{24,8},{1,17},{9,25},{17,1},{25,9},{2,18},{10... | collective-permute-start | bytes 4718600 | tf_op jit(solution)/shard_map/ppermute | solution.py:520
  657.0 35.0 %collective-permute-start.45 = (bf16[4,1536,128]{2,1,0:T(8,128)(2,1)S(1)}, bf16[4,1536,128]{2,1,0:T(8,128)(2,1)S(1)}, u32[]{:S(2)}, u32[]{:S(2)}) collective-permute-start(bf16[4,1536,128]{2,1,0:T(8,128)(2,1)S(1)} %collective-permute-done.38.refs_1_), channel_id=1, source_target_pairs={{0,8},{8,0},{16,24},{24,16},{1,9},{9,1},{17,25},{25,17},{2,10},{10... | collective-permute-start | bytes 4718600 | tf_op jit(solution)/shard_map/ppermute | solution.py:520
  661.1 34.8 %collective-permute-start.47 = (bf16[4,1536,128]{2,1,0:T(8,128)(2,1)}, bf16[4,1536,128]{2,1,0:T(8,128)(2,1)}, u32[]{:S(2)}, u32[]{:S(2)}) collective-permute-start(bf16[4,1536,128]{2,1,0:T(8,128)(2,1)} %collective-permute-done.39.refs_5_), channel_id=1, source_target_pairs={{0,16},{8,24},{16,0},{24,8},{1,17},{9,25},{17,1},{25,9},{2,18},{10... | collective-permute-start | bytes 4718600 | tf_op jit(solution)/shard_map/ppermute | solution.py:520
  (91 other events, 1219.1 us)
Sparse Core Ops, SparseCore 0:
  10.6 117.3 all-gather.2
  446.2 205.2 all-reduce.4
